TPU v7x, 32 devices: a whole 2x2x4 slice. The times are simulated.
32 devices in a mesh: tile: 16 (over z, x, core), spec: 2 (over y).
Axes of the slice: x: 2, y: 2, z: 4, core: 2. Of those that a mesh axis runs over, the one named last changes fastest.
Arguments:
- mixing: float32 [72, 1, 6, 128, 128], P('spec', None, None, 'tile'), may hold values from -6 to 6
- layer_mass: float32 [1, 6, 128, 128], P(None, None, 'tile', 'spec'), may hold values from 0.6 to 1.4
- mass_east: float32 [1, 6, 128, 128], P(None, None, 'tile', 'spec'), may hold values from -0.12 to 0.12
- mass_north: float32 [1, 6, 128, 128], P(None, None, 'tile', 'spec'), may hold values from -0.12 to 0.12
- face_slot: int32 [6], replicated, may hold values from 0 to 5, each once
Outputs:
- advected: float32 [72, 1, 6, 128, 128], P('spec', None, None, 'tile')
Inputs may be any that keep to these rules, and one draw needn't show every extreme that they name: face_slot[s] names the cube face kept in storage slot s; each of the six faces appears once.
All inputs are finite; a program needn't handle non-finite values.
Results may differ from a plain program's by a relative error of at most 0.00002.
Values sent between devices are 32-bit elements; how exact they have to be, the bound alone decides.
No kernel may reach another device: no remote copies, remote signals or barrier semaphores. Data moves between devices by JAX's collectives and lax.ppermute only.
A program may use at most 128 MiB of HBM per device.

v0:
```python
import jax
import jax.numpy as jnp
from jax import lax
from jax.sharding import PartitionSpec as P


def with_halo(cells, sides, width):
    for axis, dim in sides:
        count = lax.axis_size(axis)
        ends = count - 1
        head = lax.slice_in_dim(cells, 0, width, axis=dim)
        tail = lax.slice_in_dim(cells, cells.shape[dim] - width, cells.shape[dim], axis=dim)
        cells = jnp.concatenate(
            [
                lax.ppermute(tail, axis, [(i, (i + 1) % count) for i in range(ends)]),
                cells,
                lax.ppermute(head, axis, [((i + 1) % count, i) for i in range(ends)]),
            ],
            axis=dim,
        )
    return cells


def from_root(shard, axis, root):
    mine = lax.axis_index(axis) == root
    return lax.psum(jnp.where(mine, shard, jnp.zeros_like(shard)), axis)


def advect(tracer, layer, wide, tall, mass_wide, mass_tall, east_flow, north_flow):
    cols = tracer.shape[-1]
    rows = tracer.shape[-2]
    edge_x = (
        7.0 * (wide[..., 1 : cols + 2] + wide[..., 2 : cols + 3])
        - (wide[..., 0 : cols + 1] + wide[..., 3 : cols + 4])
    ) / 12.0
    courant_x = east_flow / (0.5 * (mass_wide[..., 1 : cols + 2] + mass_wide[..., 2 : cols + 3]))
    flux_x = east_flow * edge_x + 0.5 * jnp.abs(east_flow) * (1.0 - jnp.abs(courant_x)) * (
        wide[..., 1 : cols + 2] - wide[..., 2 : cols + 3]
    )
    edge_y = (
        7.0 * (tall[..., 1 : rows + 2, :] + tall[..., 2 : rows + 3, :])
        - (tall[..., 0 : rows + 1, :] + tall[..., 3 : rows + 4, :])
    ) / 12.0
    courant_y = north_flow / (
        0.5 * (mass_tall[..., 1 : rows + 2, :] + mass_tall[..., 2 : rows + 3, :])
    )
    flux_y = north_flow * edge_y + 0.5 * jnp.abs(north_flow) * (1.0 - jnp.abs(courant_y)) * (
        tall[..., 1 : rows + 2, :] - tall[..., 2 : rows + 3, :]
    )
    layer_new = (
        layer
        - (east_flow[..., 1:] - east_flow[..., :-1])
        - (north_flow[..., 1:, :] - north_flow[..., :-1, :])
    )
    change = flux_x[..., 1:] - flux_x[..., :-1] + (flux_y[..., 1:, :] - flux_y[..., :-1, :])
    return (tracer * layer - change) / layer_new


def local(mixing, layer_mass, mass_east, mass_north, face_slot):
    count = lax.axis_size("tile")
    place = lax.axis_index("tile")
    groups, levels, faces, rows, width = mixing.shape
    faces_iota = jnp.arange(6, dtype=jnp.int32)
    match = (face_slot[None, :] == faces_iota[:, None]).astype(jnp.int32)
    inverse = jnp.sum(faces_iota[None, :] * match, axis=1)
    shared = (
        lax.all_gather(layer_mass, "spec", axis=3, tiled=True),
        lax.all_gather(mass_east, "spec", axis=3, tiled=True),
        lax.all_gather(mass_north, "spec", axis=3, tiled=True),
    )
    fluxes = jnp.take(jnp.concatenate(shared, axis=0), inverse, axis=1)
    tracer = jnp.take(mixing.reshape(groups * levels, faces, rows, width), inverse, axis=1)
    planes = jnp.concatenate([tracer, fluxes], axis=0)
    tracer_ch = groups * levels

    def turn(values):
        return jnp.concatenate(
            [
                values[: tracer_ch + levels],
                values[tracer_ch + 2 * levels :],
                values[tracer_ch + levels : tracer_ch + 2 * levels],
            ],
            axis=0,
        )

    padded = with_halo(planes, (("tile", 2),), 2)
    low_full = from_root(planes[:, :, 0:2], "tile", 0)
    high_full = from_root(planes[:, :, rows - 2 :], "tile", count - 1)
    offset = (count - 1 - place) * rows
    low_piece = jnp.flip(lax.dynamic_slice_in_dim(low_full, offset, rows, 3), axis=-1)
    high_piece = jnp.flip(lax.dynamic_slice_in_dim(high_full, offset, rows, 3), axis=-1)
    border = jnp.concatenate([planes[..., 0:2], planes[..., width - 2 :]], axis=-1)
    columns = lax.all_gather(jnp.swapaxes(border, -1, -2), "tile", axis=3, tiled=True)
    low_turn = turn(low_piece)
    high_turn = turn(high_piece)
    col_turn = turn(columns)
    first = place == 0
    final = place == count - 1
    wide_list = []
    tall_list = []
    for face in range(6):
        own = planes[:, face]
        if face % 2 == 0:
            east_part = planes[:, (face + 1) % 6, :, 0:2]
            west_part = jnp.swapaxes(high_turn[:, (face - 2) % 6], -1, -2)
            south_end = high_full[:, (face - 1) % 6]
            north_end = jnp.flip(col_turn[:, (face + 2) % 6, 0:2], axis=-1)
        else:
            east_part = jnp.swapaxes(low_turn[:, (face + 2) % 6], -1, -2)
            west_part = planes[:, (face - 1) % 6, :, width - 2 :]
            south_end = jnp.flip(col_turn[:, (face - 2) % 6, 2:4], axis=-1)
            north_end = low_full[:, (face + 1) % 6]
        south_part = jnp.where(first, south_end, padded[:, face, 0:2])
        north_part = jnp.where(final, north_end, padded[:, face, rows + 2 :])
        wide_list.append(jnp.concatenate([west_part, own, east_part], axis=-1))
        tall_list.append(jnp.concatenate([south_part, own, north_part], axis=-2))
    wide = jnp.stack(wide_list, axis=1)
    tall = jnp.stack(tall_list, axis=1)
    tracer_wide = wide[:tracer_ch].reshape(groups, levels, faces, rows, width + 4)
    tracer_tall = tall[:tracer_ch].reshape(groups, levels, faces, rows + 4, width)
    mass_wide = wide[tracer_ch : tracer_ch + levels]
    mass_tall = tall[tracer_ch : tracer_ch + levels]
    east_flow = wide[tracer_ch + levels : tracer_ch + 2 * levels][..., 2 : width + 3]
    north_flow = tall[tracer_ch + 2 * levels :][..., 2 : rows + 3, :]
    tracer_own = tracer.reshape(groups, levels, faces, rows, width)
    layer_own = fluxes[0:levels]
    result = advect(
        tracer_own, layer_own, tracer_wide, tracer_tall, mass_wide, mass_tall, east_flow, north_flow
    )
    return jnp.take(result, face_slot, axis=2)


def solution(mesh):
    placed = (
        P("spec", None, None, "tile", None),
        P(None, None, "tile", "spec"),
        P(None, None, "tile", "spec"),
        P(None, None, "tile", "spec"),
        P(),
    )
    return jax.shard_map(
        local,
        mesh=mesh,
        in_specs=placed,
        out_specs=P("spec", None, None, "tile", None),
        check_vma=False,
    )
```

profile of v0, /device:TPU:0, one launch (start us, length us, event | category | flops | bytes accessed | tf_op | source)
XLA Modules:
  0.0 165.6 jit_solution(583746398492781314)
XLA Ops:
  6.5 0.9 select_reduce_fusion
  7.4 0.7 compare_and_fusion
  8.1 0.7 compare_select_fusion.2
  8.7 0.9 copy.178
  9.6 8.5 %all_gather.12 = f32[1,6,8,128]{2,0,1,3:T(1,128)S(1)} all-gather(f32[1,6,8,64]{2,0,1,3:T(1,128)S(1)} %copy.178), channel_id=1, replica_groups=mesh['tile'=16,'spec'=2] {'spec'}, dimensions={3}, use_global_device_ids=true | all-gather | bytes 36864 | tf_op jit(solution)/shard_map/all_gather | solution.py:67
  18.1 0.3 copy.181
  18.4 0.9 copy.179
  19.3 6.8 %all_gather.13 = f32[1,6,8,128]{2,0,1,3:T(1,128)S(1)} all-gather(f32[1,6,8,64]{2,0,1,3:T(1,128)S(1)} %copy.179), channel_id=1, replica_groups=mesh['tile'=16,'spec'=2] {'spec'}, dimensions={3}, use_global_device_ids=true | all-gather | bytes 36864 | tf_op jit(solution)/shard_map/all_gather | solution.py:68
  26.1 0.3 copy.182
  26.5 6.3 %all_gather.14 = f32[1,6,8,128]{2,0,1,3:T(1,128)S(1)} all-gather(f32[1,6,8,64]{2,0,1,3:T(1,128)S(1)} %copy.180), channel_id=1, replica_groups=mesh['tile'=16,'spec'=2] {'spec'}, dimensions={3}, use_global_device_ids=true | all-gather | bytes 36864 | tf_op jit(solution)/shard_map/all_gather | solution.py:69
  32.9 0.3 copy.183
  33.2 0.6 gather_fusion.1
  33.8 0.6 gather_fusion
  34.6 1.1 broadcast_select_fusion.1
  35.7 0.8 copy.193
  36.5 2.0 %collective-permute-start = (f32[39,6,2,128]{3,2,1,0:T(2,128)}, f32[39,6,2,128]{3,2,1,0:T(2,128)}, u32[]{:S(2)}, u32[]{:S(2)}) collective-permute-start(f32[39,6,2,128]{3,2,1,0:T(2,128)} %copy.193), channel_id=1, source_target_pairs={{0,2},{2,4},{4,6},{6,8},{8,10},{10,12},{12,14},{14,16},{16,18},{18... | collective-permute-start | bytes 718856 | tf_op jit(solution)/shard_map/ppermute | solution.py:15
  38.5 0.8 copy.199
  39.2 1.3 collective-permute-start.1
  40.6 1.0 fusion.6
  41.6 1.5 fusion.8
  43.1 0.5 copy.195
  43.6 30.0 %all_gather.15 = f32[39,6,4,128]{0,2,1,3:T(4,128)S(1)} all-gather(f32[39,6,4,8]{0,2,1,3:T(4,128)S(1)} %copy.195), channel_id=1, replica_groups=mesh['tile'=16,'spec'=2] {'tile'}, dimensions={3}, use_global_device_ids=true | all-gather | bytes 509184 | tf_op jit(solution)/shard_map/all_gather | solution.py:93
  73.6 3.3 %fusion.91 = (f32[1,6,4,128]{0,2,1,3:T(4,128)}, f32[1,6,4,128]{0,2,1,3:T(4,128)}) fusion(f32[39,6,4,128]{0,2,1,3:T(4,128)S(1)} %all_gather.15), kind=kLoop, calls=%fused_computation.197 | loop fusion | bytes 49152 | tf_op jit(solution)/shard_map/slice | solution.py:80
  76.9 1.7 %copy.214 = f32[1,6,4,128]{3,2,0,1:T(4,128)S(1)} copy(f32[1,6,4,128]{0,2,1,3:T(4,128)} %get-tuple-element.15) | data formatting | bytes 24576
  78.6 1.7 %copy.215 = f32[1,6,4,128]{3,2,0,1:T(4,128)S(1)} copy(f32[1,6,4,128]{0,2,1,3:T(4,128)} %get-tuple-element.16) | data formatting | bytes 24576
  80.3 1.4 copy.213
  81.7 1.2 fusion.67
  83.0 0.1 rev.25
  83.2 0.8 rev.27
  84.0 0.8 rev.22
  84.7 0.8 rev.24
  85.5 0.8 rev.26
  86.3 0.9 fusion.49
  87.2 49.3 %all-reduce.3.cloned.1.call-done = (f32[39,6,2,128]{3,2,0,1:T(2,128)}, f32[39,6,2,128]{3,2,0,1:T(2,128)}) async-done(((f32[39,6,2,128]{3,2,0,1:T(2,128)}, f32[39,6,2,128]{3,2,0,1:T(2,128)}), (f32[39,6,2,128]{3,2,0,1:T(2,128)}, f32[39,6,2,128]{3,2,0,1:T(2,128)})) %all-reduce.3.cloned.1.call-update) | async-done | bytes 479248 | tf_op jit(solution)/shard_map/psum | solution.py:26
  136.5 1.2 constant_dynamic-slice_fusion.2
  137.7 0.8 constant_dynamic-slice_fusion.1
  138.5 0.8 constant_dynamic-slice_fusion.5
  139.3 1.2 constant_dynamic-slice_fusion
  140.6 0.1 copy.185
  141.0 0.9 slice.281
  142.2 0.2 copy.187
  142.6 0.9 slice.293
  143.6 0.3 copy.188
  143.9 0.2 copy.189
  144.1 0.3 copy.190
  144.4 0.2 copy.191
  144.5 0.3 copy.192
  144.8 1.1 fusion.14
  145.9 1.1 fusion.15
  147.0 1.1 fusion.16
  148.2 0.2 fusion.17
  148.4 0.2 fusion.18
  148.5 0.2 fusion.19
  149.1 0.6 copy-done.4
  149.7 0.9 fusion.70
  150.6 0.9 fusion.68
  151.6 0.9 fusion.65
  152.5 0.9 fusion.66
  154.0 1.4 fusion.5
  155.5 0.8 fusion.2
  156.3 0.3 copy-done.2
  156.6 0.4 fusion.12
  157.0 0.6 gather_fusion.2
  157.7 1.0 copy.211
  (50 shorter events, 2.5 us)
Async XLA Ops:
  6.5 27.2 %copy-start = (f32[36,1,6,8,128]{4,3,2,1,0:T(8,128)S(1)}, f32[36,1,6,8,128]{4,3,2,1,0:T(8,128)}, u32[]{:S(2)}) copy-start(f32[36,1,6,8,128]{4,3,2,1,0:T(8,128)} %param.5) | copy-start | bytes 2654212
  6.5 19.8 %copy-start.9 = (f32[1,6,8,64]{3,2,1,0:T(8,128)S(1)}, f32[1,6,8,64]{3,2,1,0:T(8,128)}, u32[]{:S(2)}) copy-start(f32[1,6,8,64]{3,2,1,0:T(8,128)} %param.8) | copy-start | bytes 36868
  6.5 129.9 %all-reduce.3.cloned.1.call-start = ((), (), s32[]{:S(2)}) async-start(), calls=%async_computation | async-start | bytes 958464 | tf_op jit(solution)/shard_map/psum | solution.py:26
  34.4 1.3 copy-start.1
  36.5 112.6 %collective-permute-start = (f32[39,6,2,128]{3,2,1,0:T(2,128)}, f32[39,6,2,128]{3,2,1,0:T(2,128)}, u32[]{:S(2)}, u32[]{:S(2)}) collective-permute-start(f32[39,6,2,128]{3,2,1,0:T(2,128)} %copy.193), channel_id=1, source_target_pairs={{0,2},{2,4},{4,6},{6,8},{8,10},{10,12},{12,14},{14,16},{16,18},{18... | collective-permute-start | bytes 718856 | tf_op jit(solution)/shard_map/ppermute | solution.py:15
  39.2 111.3 %collective-permute-start.1 = (f32[39,6,2,128]{3,2,1,0:T(2,128)}, f32[39,6,2,128]{3,2,1,0:T(2,128)}, u32[]{:S(2)}, u32[]{:S(2)}) collective-permute-start(f32[39,6,2,128]{3,2,1,0:T(2,128)} %copy.199), channel_id=1, source_target_pairs={{2,0},{4,2},{6,4},{8,6},{10,8},{12,10},{14,12},{16,14},{18,16},{20... | collective-permute-start | bytes 718856 | tf_op jit(solution)/shard_map/ppermute | solution.py:17
  148.7 0.9 copy-start.4
  148.8 1.8 %copy-start.6 = (f32[39,2,128]{2,1,0:T(2,128)S(1)}, f32[39,2,128]{2,1,0:T(2,128)}, u32[]{:S(2)}) copy-start(f32[39,2,128]{2,1,0:T(2,128)} %rev.22) | copy-start | bytes 119812
  148.8 1.8 %copy-start.7 = (f32[39,2,128]{2,1,0:T(2,128)S(1)}, f32[39,2,128]{2,1,0:T(2,128)}, u32[]{:S(2)}) copy-start(f32[39,2,128]{2,1,0:T(2,128)} %rev.24) | copy-start | bytes 119812
  148.8 1.8 %copy-start.8 = (f32[39,2,128]{2,1,0:T(2,128)S(1)}, f32[39,2,128]{2,1,0:T(2,128)}, u32[]{:S(2)}) copy-start(f32[39,2,128]{2,1,0:T(2,128)} %rev.26) | copy-start | bytes 119812
  148.8 2.8 %copy-start.3 = (f32[39,6,2,128]{3,2,0,1:T(2,128)S(1)}, f32[39,6,2,128]{3,2,0,1:T(2,128)}, u32[]{:S(2)}) copy-start(f32[39,6,2,128]{3,2,0,1:T(2,128)} %get-tuple-element.6) | copy-start | bytes 718852
  148.9 3.5 %copy-start.5 = (f32[39,2,128]{2,1,0:T(2,128)S(1)}, f32[39,2,128]{2,1,0:T(2,128)}, u32[]{:S(2)}) copy-start(f32[39,2,128]{2,1,0:T(2,128)} %rev.27) | copy-start | bytes 119812
  155.4 1.2 copy-start.2
Sparse Core Ops, SparseCore 0:
  40.7 95.7 all-reduce.2
where the time goes:
time: 167 us; the launch traced here: 166 us
  blocking collectives  51.7 us (31%)
  waiting for transfers between devices  49.3 us (30%)
  local copies, waits for them, and re-layouts  28.4 us (17%)
  other arithmetic  19.2 us (11%)
  between operations  13.8 us (8%)
  starting transfers between devices  3.27 us (2%)
    psum x1, waiting for transfers between devices, from_root(): return lax.psum(jnp.where(mine, shard, jnp.zeros_like(shard)), axis)  49.3 us
    all_gather x1, blocking collectives, local(): lax.all_gather(jnp.swapaxes(border, -1, -2), 'tile', axis=3, tiled=True)  30 us
    all_gather x1, blocking collectives, local(): lax.all_gather(layer_mass, 'spec', axis=3, tiled=True)  8.53 us
    unnamed x26, local copies, waits for them, and re-layouts  7.64 us
    all_gather x1, blocking collectives, local(): lax.all_gather(mass_east, 'spec', axis=3, tiled=True)  6.76 us
    all_gather x1, blocking collectives, local(): lax.all_gather(mass_north, 'spec', axis=3, tiled=True)  6.35 us
    slice x6, local copies, waits for them, and re-layouts, turn(): values[tracer_ch + 2 * levels:]  5.24 us
    slice x5, local copies, waits for them, and re-layouts, turn(): values[:tracer_ch + levels]  4.51 us
  transfers between devices with their start and end apart: 3, of which 1 were waited for; matrix products, arithmetic and copies ran while one was open for 19% of the time, Pallas kernels for 0%

commit v1 on v0

v1 whole, which is shorter than its diff:
```python
import jax
import jax.numpy as jnp
from jax import lax
from jax.experimental import pallas as pl
from jax.experimental.pallas import tpu as pltpu
from jax.sharding import PartitionSpec as P

F32 = jnp.float32


def up(value, unit):
    return -(-value // unit) * unit


class Sizes:
    def __init__(self, mixing, halves, tiles):
        self.species, _, _, self.rows, self.width = mixing.shape
        self.tiles, self.halves = tiles, halves
        self.group = up(2 * self.species, 8)
        self.flux = 3 * self.group
        self.block = up(self.flux + 6, 8)
        self.lanes = up(self.block, 128)
        self.extra = 2 * self.block
        self.sent = self.extra + 8 * (self.lanes // 128)


def slots(face_slot):
    return [sum(jnp.where(face_slot[s] == f, s, 0) for s in range(6)) for f in range(6)]


def reversal(width):
    i = lax.broadcasted_iota(jnp.int32, (width, width), 0)
    j = lax.broadcasted_iota(jnp.int32, (width, width), 1)
    return jnp.where(i + j == width - 1, 1.0, 0.0).astype(F32)


def pack_kernel(z, face_slot, mixing, own, other, to_a, to_b, slots_out, kept, full):
    place = lax.axis_index("tile")
    half = lax.axis_index("spec")
    slot = slots(face_slot)
    even = lax.rem(place, 2) == 0
    first = place == 0
    width, species = z.width, z.species
    for c in range(3):
        for f in range(6):
            if z.halves == 2:
                a, b = own[c, slot[f]], other[c, slot[f]]
                parts = [jnp.where(half == 0, a, b), jnp.where(half == 0, b, a)]
            else:
                parts = [other[n, c, slot[f]] for n in range(z.halves)]
            full[c * 6 + f] = jnp.concatenate(parts, axis=-1)

    def both(low, high, at):
        to_a[pl.ds(at, low.shape[0])] = jnp.where(even, high, low)
        to_b[pl.ds(at, low.shape[0])] = jnp.where(even, low, high)

    lane = lax.broadcasted_iota(jnp.int32, (8, 128), 1)
    gathers = []
    for parity in range(2):
        base = parity * z.block
        lanes = [jnp.zeros((8, 128), F32) for _ in range(z.lanes // 128)]
        for a in range(3):
            f = 2 * a + parity
            for s in range(0, species):
                tile = mixing[s, 0, slot[f]]
                at = a * z.group + 2 * s
                both(tile[0:2], tile[6:8], base + at)
                edge = tile[:, :128] if parity == 0 else tile[:, width - 128 :]
                shift = (at - (0 if parity == 0 else 126)) % 128
                moved = pltpu.roll(edge, shift, 1) if shift else edge
                k = at // 128
                lanes[k] = jnp.where((lane >> 1) == (at % 128) // 2, moved, lanes[k])
            for at, low_from, col_from in ((z.flux + a, 0, 0), (z.flux + 3 + a, 2, 1)):
                rows = full[low_from * 6 + f]
                both(rows[0:1], rows[7:8], base + at)
                cols = full[col_from * 6 + f]
                edge = cols[:, :128] if parity == 0 else cols[:, width - 128 :]
                shift = (at - (0 if parity == 0 else 127)) % 128
                moved = pltpu.roll(edge, shift, 1) if shift else edge
                k = at // 128
                lanes[k] = jnp.where(lane == at % 128, moved, lanes[k])
        if z.block > z.flux + 6:
            pad = z.block - z.flux - 6
            both(jnp.zeros((pad, width), F32), jnp.zeros((pad, width), F32), base + z.flux + 6)
        if z.group > 2 * species:
            pad = z.group - 2 * species
            for a in range(3):
                both(
                    jnp.zeros((pad, width), F32),
                    jnp.zeros((pad, width), F32),
                    base + a * z.group + 2 * species,
                )
        gathers.append(lanes)
    for k in range(z.lanes // 128):
        even_cols, odd_cols = gathers[0][k], gathers[1][k]
        kept[:, k * 128 : (k + 1) * 128] = jnp.where(first, odd_cols, even_cols)
        spare = jnp.where(first, even_cols, odd_cols)
        at = z.extra + 8 * k
        if width > 128:
            spare = jnp.concatenate([spare] * (width // 128), axis=-1)
        to_a[pl.ds(at, 8)] = spare
        to_b[pl.ds(at, 8)] = spare
        slots_out[0:8, k * 128 : (k + 1) * 128] = odd_cols
        slots_out[8 * (z.tiles - 1) :, k * 128 : (k + 1) * 128] = even_cols

    @pl.when(first | (place == z.tiles - 1))
    def _():
        start = pl.multiple_of(jnp.where(first, z.block, 0), 8)
        rows = to_b[pl.ds(start, z.block)]
        if z.lanes > z.block:
            rows = jnp.concatenate([rows, jnp.zeros((z.lanes - z.block, width), F32)], axis=0)
        slots_out[...] = lax.dot_general(
            reversal(width),
            rows,
            (((1,), (1,)), ((), ())),
            precision=lax.Precision.HIGHEST,
            preferred_element_type=F32,
        )


def step_kernel(
    z, face_slot, mixing, from_a, from_b, arrived, kept, full, out,
    south, north, side, coef, result, copy_sem, out_sem,
):
    place = lax.axis_index("tile")
    slot = slots(face_slot)
    even = lax.rem(place, 2) == 0
    first = place == 0
    last = place == z.tiles - 1
    width, species, block = z.width, z.species, z.block
    blocks = pl.ds(0, 2 * block)

    def halo(source_s, source_n):
        return (
            pltpu.make_async_copy(source_s.at[blocks], south.at[blocks], copy_sem.at[0]),
            pltpu.make_async_copy(source_n.at[blocks], north.at[blocks], copy_sem.at[1]),
        )

    @pl.when(even)
    def _():
        for copy in halo(from_b, from_a):
            copy.start()
        for copy in halo(from_b, from_a):
            copy.wait()

    @pl.when(jnp.logical_not(even))
    def _():
        for copy in halo(from_a, from_b):
            copy.start()
        for copy in halo(from_a, from_b):
            copy.wait()

    lane = lax.broadcasted_iota(jnp.int32, (8, width), 1)
    row = lax.broadcasted_iota(jnp.int32, (8, width), 0)
    lane1 = lax.broadcasted_iota(jnp.int32, (8, 128), 1)

    @pl.when(first | last)
    def _():
        fetch = pltpu.make_async_copy(
            from_b.at[pl.ds(z.extra, z.sent - z.extra)], side.at[pl.ds(0, z.sent - z.extra)], copy_sem.at[2]
        )
        fetch.start()
        fetch.wait()
        pieces = []
        for k in range(z.lanes // 128):
            part = slice(k * 128, (k + 1) * 128)
            spare = side[8 * k : 8 * k + 8, 0:128]
            mine = kept[:, part]
            head = jnp.where(first, mine, spare)
            tail = jnp.where(first, spare, mine)
            pieces.append(jnp.concatenate([head, arrived[8 : 8 * (z.tiles - 1), part], tail], axis=0))
        cols = jnp.concatenate(pieces, axis=1) if len(pieces) > 1 else pieces[0]
        turned = lax.dot_general(
            cols,
            reversal(width),
            (((0,), (0,)), ((), ())),
            precision=lax.Precision.HIGHEST,
            preferred_element_type=F32,
        )[:block]

        @pl.when(first)
        def _():
            south[2 * block : 3 * block] = turned

        @pl.when(last)
        def _():
            north[2 * block : 3 * block] = turned

    south_at = [jnp.where(first, block, 0), jnp.where(first, 2 * block, block)]
    north_at = [jnp.where(last, 2 * block, 0), jnp.where(last, 0, block)]
    south_a = [jnp.where(first, (a + 2) % 3, a) for a in range(3)]
    north_a = [jnp.where(last, (a + 1) % 3, a) for a in range(3)]

    def one(ref, at):
        eight = pl.multiple_of(lax.div(at, 8) * 8, 8)
        rows = ref[pl.ds(eight, 8)]
        return jnp.sum(jnp.where(row == at - eight, rows, 0.0), axis=0, keepdims=True)

    def spread(k, lane_at):
        part = arrived[8 * k : 8 * k + 8, (lane_at // 128) * 128 : (lane_at // 128) * 128 + 128]
        return jnp.sum(jnp.where(lane1 == lane_at % 128, part, 0.0), axis=1, keepdims=True)

    def left(x, ghost, n):
        return pltpu.roll(jnp.where(lane >= width - n, ghost, x), n, 1)

    def right(x, ghost, n):
        return pltpu.roll(jnp.where(lane < n, ghost, x), width - n, 1)

    def below(x, ghost, n):
        return pltpu.roll(jnp.where(row >= 8 - n, ghost, x), n, 0)

    def above(x, ghost, n):
        return pltpu.roll(jnp.where(row < n, ghost, x), 8 - n, 0)

    def upwind(u, total):
        return 0.5 * jnp.abs(u) * (1.0 - jnp.abs(u / (0.5 * total)))

    for f in range(6):
        a, parity = f // 2, f % 2
        dp, fx, fy = full[f], full[6 + f], full[12 + f]
        if parity == 0:
            west = spread(z.tiles - 1, z.flux + (a + 2) % 3)
            east, east_u = full[f + 1], full[6 + f + 1]
        else:
            west = full[f - 1]
            east = spread(0, z.flux + (a + 1) % 3)
            east_u = spread(0, z.flux + 3 + (a + 1) % 3)
        dp_w, dp_e = left(dp, west, 1), right(dp, east, 1)
        u0, u1 = fx, right(fx, east_u, 1)
        dp_s = below(dp, one(south, south_at[parity] + z.flux + south_a[a]), 1)
        dp_n = above(dp, one(north, north_at[parity] + z.flux + north_a[a]), 1)
        v0, v1 = fy, above(fy, one(north, north_at[parity] + z.flux + 3 + north_a[a]), 1)
        inverse = 1.0 / (dp - (u1 - u0) - (v1 - v0))
        center = dp
        for n, (w0, w1, d0, d1) in enumerate(((u0, u1, dp_w, dp_e), (v0, v1, dp_s, dp_n))):
            b0, b1 = upwind(w0, d0 + dp), upwind(w1, dp + d1)
            p0, p1 = w0 * (1.0 / 12.0), w1 * (1.0 / 12.0)
            coef[f, 4 * n] = -p0 * inverse
            coef[f, 4 * n + 1] = (7.0 * p0 + b0 + p1) * inverse
            coef[f, 4 * n + 2] = (-p0 - 7.0 * p1 + b1) * inverse
            coef[f, 4 * n + 3] = p1 * inverse
            center = center + (7.0 * p0 - b0) - (7.0 * p1 + b1)
        coef[f, 8] = center * inverse

    def ghosts(a, s):
        east_at = ((a + 1) % 3) * z.group + 2 * s
        west_at = ((a + 2) % 3) * z.group + 2 * s
        east = arrived[0:8, (east_at // 128) * 128 : (east_at // 128) * 128 + 128]
        west = arrived[8 * (z.tiles - 1) :, (west_at // 128) * 128 : (west_at // 128) * 128 + 128]
        east = pltpu.roll(east, -east_at % 128, 1) if east_at % 128 else east
        west_shift = (126 - west_at) % 128
        west = pltpu.roll(west, west_shift, 1) if west_shift else west
        return jnp.where(lane1 < 2, east, west)

    for a in range(3):
        for s in range(species):
            side[pl.ds((a * species + s) * 8, 8), 0:128] = ghosts(a, s)

    def strip(a, first_s, count, south_rows, north_rows):
        fe, fo = 2 * a, 2 * a + 1
        ce = [coef[fe, n] for n in range(9)]
        co = [coef[fo, n] for n in range(9)]
        for u in range(count):
            s = first_s + u
            qe, qo = mixing[s, 0, slot[fe]], mixing[s, 0, slot[fo]]
            g = side[pl.ds(pl.multiple_of((a * species + s) * 8, 8), 8), 0:128]
            if width > 128:
                g = jnp.concatenate([g] * (width // 128), axis=-1)
            for q, west, east, c, parity, f in ((qe, g, qo, ce, 0, fe), (qo, qe, g, co, 1, fo)):
                sv, nv = south_rows[parity], north_rows[parity]
                sv = pltpu.roll(sv, (6 - 2 * u) % 8, 0) if (6 - 2 * u) % 8 else sv
                nv = pltpu.roll(nv, (-2 * u) % 8, 0) if u else nv
                value = c[8] * q
                value += c[0] * left(q, west, 2)
                value += c[1] * left(q, west, 1)
                value += c[2] * right(q, east, 1)
                value += c[3] * right(q, east, 2)
                value += c[4] * below(q, sv, 2)
                value += c[5] * below(q, sv, 1)
                value += c[6] * above(q, nv, 1)
                value += c[7] * above(q, nv, 2)
                result[s, slot[f]] = value

    def quad(it, count):
        for a in range(3):
            at = [south_at[p] + south_a[a] * z.group + 8 * it for p in range(2)]
            s_rows = [south[pl.ds(pl.multiple_of(x, 8), 8)] for x in at]
            at = [north_at[p] + north_a[a] * z.group + 8 * it for p in range(2)]
            n_rows = [north[pl.ds(pl.multiple_of(x, 8), 8)] for x in at]
            strip(a, 4 * it, count, s_rows, n_rows)
        part = pl.ds(4 * it, count)
        pltpu.make_async_copy(result.at[part], out.at[part, 0], out_sem).start()

    @pl.loop(0, species // 4)
    def _(it):
        quad(it, 4)

    if species % 4:
        quad(species // 4, species % 4)
    pltpu.make_async_copy(result, out.at[:, 0], out_sem).wait()


def local(mixing, layer_mass, mass_east, mass_north, face_slot):
    tiles = lax.axis_size("tile")
    halves = lax.axis_size("spec")
    z = Sizes(mixing, halves, tiles)
    assert z.rows == 8 and mixing.shape[1] == 1
    own = jnp.concatenate([layer_mass, mass_east, mass_north], axis=0)
    if halves == 2:
        other = lax.ppermute(own, "spec", [(0, 1), (1, 0)])
    else:
        other = lax.all_gather(own, "spec", axis=0, tiled=False)
    smem = pl.BlockSpec(memory_space=pltpu.SMEM)
    vmem = pl.BlockSpec(memory_space=pltpu.VMEM)
    hbm = pl.BlockSpec(memory_space=pl.ANY)
    sent = jax.ShapeDtypeStruct((z.sent, z.width), F32)
    to_a, to_b, slots_out, kept, full = pl.pallas_call(
        lambda *refs: pack_kernel(z, *refs),
        out_shape=(
            sent,
            sent,
            jax.ShapeDtypeStruct((8 * tiles, z.lanes), F32),
            jax.ShapeDtypeStruct((8, z.lanes), F32),
            jax.ShapeDtypeStruct((18, 8, z.width), F32),
        ),
        in_specs=[smem, vmem, vmem, vmem],
        out_specs=[vmem] * 5,
        name="pack",
    )(face_slot, mixing, own, other)
    arrived = lax.all_to_all(slots_out, "tile", 0, 0, tiled=True)
    from_a = lax.ppermute(to_a, "tile", [(i, i ^ 1) for i in range(tiles)])
    pairs = [(i, (i + 1) % tiles) if i % 2 else (i, (i - 1) % tiles) for i in range(tiles)]
    from_b = lax.ppermute(to_b, "tile", pairs)
    return pl.pallas_call(
        lambda *refs: step_kernel(z, *refs),
        out_shape=jax.ShapeDtypeStruct(mixing.shape, F32),
        in_specs=[smem, vmem, hbm, hbm, vmem, vmem, vmem],
        out_specs=hbm,
        scratch_shapes=[
            pltpu.VMEM((3 * z.block, z.width), F32),
            pltpu.VMEM((3 * z.block, z.width), F32),
            pltpu.VMEM((z.species * 24, z.width), F32),
            pltpu.VMEM((6, 9, 8, z.width), F32),
            pltpu.VMEM((z.species, 6, 8, z.width), F32),
            pltpu.SemaphoreType.DMA((3,)),
            pltpu.SemaphoreType.DMA,
        ],
        name="step",
    )(face_slot, mixing, from_a, from_b, arrived, kept, full)


def solution(mesh):
    flux = P(None, None, "tile", "spec")
    cells = P("spec", None, None, "tile", None)
    return jax.shard_map(
        local,
        mesh=mesh,
        in_specs=(cells, flux, flux, flux, P()),
        out_specs=cells,
        check_vma=False,
    )
```

time: 167 us -> 34.4 us (0.21)
  blocking collectives: 51.7 us -> 0 us
  waiting for transfers between devices: 49.3 us -> 8.06 us
  local copies, waits for them, and re-layouts: 28.4 us -> 2.86 us
  other arithmetic: 19.2 us -> 0 us
  between operations: 13.8 us -> 0.03 us
  starting transfers between devices: 3.27 us -> 13.9 us
  Pallas kernels: 0 us -> 9.1 us
    all_gather x4 -> x0, blocking collectives: 51.7 us -> none  [the longest x1 30 us: local(): lax.all_gather(jnp.swapaxes(border, -1, -2), 'tile', axis=3, tiled=True)]
    psum x1 -> x0, waiting for transfers between devices: 49.3 us -> none  [from_root(): return lax.psum(jnp.where(mine, shard, jnp.zeros_like(shard)), axis)]
    slice x16 -> x0, local copies, waits for them, and re-layouts: 11.7 us -> none  [the longest x6 5.24 us: turn(): values[tracer_ch + 2 * levels:]]
    pallas_call x0 -> x2, Pallas kernels: none -> 9.1 us  [the longest x1 6.27 us: local(): pl.pallas_call(lambda *refs: step_kernel(z, *refs), out_shape=jax.ShapeDt...]
    ppermute x2 -> x3, waiting for transfers between devices: 0.01 us -> 8.06 us  [the longest x1 5.73 us: local(): from_b = lax.ppermute(to_b, 'tile', pairs)]
    all_to_all x0 -> x1, starting transfers between devices: none -> 6.17 us  [local(): arrived = lax.all_to_all(slots_out, 'tile', 0, 0, tiled=True)]
    select_n x10 -> x0, other arithmetic: 5.62 us -> none  [the longest x2 1.79 us: local(): north_part = jnp.where(final, north_end, padded[:, face, rows + 2:])]
    unnamed x26 -> x18, local copies, waits for them, and re-layouts: 7.64 us -> 2.86 us
  transfers between devices with their start and end apart: 3 -> 4, of which waited for: 1 -> 2; matrix products, arithmetic and copies ran while one was open for 19% -> 0% of each run, Pallas kernels for 0% -> 0%
where the time goes in v1:
time: 34.4 us; the launch traced here: 33.9 us
  starting transfers between devices  13.9 us (40%)
  Pallas kernels  9.1 us (26%)
  waiting for transfers between devices  8.06 us (23%)
  local copies, waits for them, and re-layouts  2.86 us (8%)
    pallas_call x1, Pallas kernels, local(): pl.pallas_call(lambda *refs: step_kernel(z, *refs), out_shape=jax.ShapeDt...  6.27 us
    all_to_all x1, starting transfers between devices, local(): arrived = lax.all_to_all(slots_out, 'tile', 0, 0, tiled=True)  6.17 us
    ppermute x1, waiting for transfers between devices, local(): from_b = lax.ppermute(to_b, 'tile', pairs)  5.73 us
    ppermute x1, starting transfers between devices, local(): from_b = lax.ppermute(to_b, 'tile', pairs)  4.33 us
    ppermute x1, starting transfers between devices, local(): other = lax.ppermute(own, 'spec', [(0, 1), (1, 0)])  2.97 us
    unnamed x18, local copies, waits for them, and re-layouts  2.86 us
    pallas_call x1, Pallas kernels, local(): pl.pallas_call(lambda *refs: pack_kernel(z, *refs), out_shape=(sent, sent...  2.83 us
    ppermute x1, waiting for transfers between devices, local(): other = lax.ppermute(own, 'spec', [(0, 1), (1, 0)])  2.33 us
  transfers between devices with their start and end apart: 4, of which 2 were waited for; matrix products, arithmetic and copies ran while one was open for 0% of the time, Pallas kernels for 0%

profile of v1, /device:TPU:0, one launch (start us, length us, event | category | flops | bytes accessed | tf_op | source)
XLA Modules:
  0.0 33.9 jit_solution(14475680047657799940)
XLA Ops:
  0.0 0.0 copy-start.5
  0.0 0.7 %constant_dynamic-update-slice_fusion.2 = f32[3,6,8,64]{3,2,1,0:T(8,128)S(1)} fusion(f32[1,6,8,64]{3,2,1,0:T(8,128)} %param.6), kind=kLoop, calls=%fused_computation.2 | loop fusion | bytes 36864
  0.7 0.0 copy-done.5
  0.8 0.0 copy-start.6
  0.8 0.7 %copy-done.6 = f32[1,6,8,64]{3,2,1,0:T(8,128)S(1)} copy-done((f32[1,6,8,64]{3,2,1,0:T(8,128)S(1)}, f32[1,6,8,64]{3,2,1,0:T(8,128)}, u32[]{:S(2)}) %copy-start.6) | copy-done | bytes 12312
  1.5 0.0 copy-start.3
  1.5 3.0 %collective-permute-start = (f32[3,6,8,64]{3,2,1,0:T(8,128)S(1)}, f32[3,6,8,64]{3,2,1,0:T(8,128)S(1)}, u32[]{:S(2)}, u32[]{:S(2)}) collective-permute-start(f32[3,6,8,64]{3,2,1,0:T(8,128)S(1)} %constant_dynamic-update-slice_fusion.refs_2_), channel_id=1, source_target_pairs={{0,1},{1,0},{2,3},{3,2},{4,5},{5,4},{6,7},{7,6},{8,9},{9,8},{10,11... | collective-permute-start | bytes 110600 | tf_op jit(solution)/shard_map/ppermute | solution.py:310
  4.5 2.3 %collective-permute-done.refs_3_ = f32[3,6,8,64]{3,2,1,0:T(8,128)S(1)} collective-permute-done((f32[3,6,8,64]{3,2,1,0:T(8,128)S(1)}, f32[3,6,8,64]{3,2,1,0:T(8,128)S(1)}, u32[]{:S(2)}, u32[]{:S(2)}) %collective-permute-start) | collective-permute-done | bytes 36896 | tf_op jit(solution)/shard_map/ppermute | solution.py:310
  6.8 0.0 copy-done.3
  6.8 0.0 copy-start.4
  6.8 0.6 %copy-done.4 = f32[3,6,8,64]{3,2,1,0:T(8,128)} copy-done((f32[3,6,8,64]{3,2,1,0:T(8,128)}, f32[3,6,8,64]{3,2,1,0:T(8,128)S(1)}, u32[]{:S(2)}) %copy-start.4) | copy-done | bytes 36888
  7.4 2.8 %pack.1 = (f32[464,128]{1,0:T(8,128)}, f32[464,128]{1,0:T(8,128)}, f32[128,256]{1,0:T(8,128)}, f32[8,256]{1,0:T(8,128)}, f32[18,8,128]{2,1,0:T(8,128)}) custom-call(s32[6]{0:T(128)} %refs_0_.3, f32[36,1,6,8,128]{4,3,2,1,0:T(8,128)} %refs_1_.3, f32[3,6,8,64]{3,2,1,0:T(8,128)} %copy-done.3, f32[3,6,8,64]{3,2,1,0:T(8,128)} %copy-done.4), custom_call_target="tpu_custom_call" | custom-call | tf_op jit(solution)/shard_map/pack/pallas_call | solution.py:317
  10.3 0.0 copy-start.7
  10.3 6.2 %all-to-all-start = ((f32[16,8,256]{2,1,0:T(8,128)}), f32[16,8,256]{2,1,0:T(8,128)S(1)}, u32[]{:S(2)}, u32[]{:S(2)}) async-start(f32[16,8,256]{2,1,0:T(8,128)} %bitcast.3), calls=%async_computation | async-start | bytes 262144 | tf_op jit(solution)/shard_map/all_to_all | solution.py:330
  16.4 0.4 %collective-permute-start.1 = (f32[464,128]{1,0:T(8,128)}, f32[464,128]{1,0:T(8,128)S(1)}, u32[]{:S(2)}, u32[]{:S(2)}) collective-permute-start(f32[464,128]{1,0:T(8,128)} %get-tuple-element.10), channel_id=1, source_target_pairs={{0,2},{2,0},{4,6},{6,4},{8,10},{10,8},{12,14},{14,12},{16,18},{18,... | collective-permute-start | bytes 712712 | tf_op jit(solution)/shard_map/ppermute | solution.py:331
  16.8 0.0 copy-done.7
  16.8 4.3 %collective-permute-start.2 = (f32[464,128]{1,0:T(8,128)S(1)}, f32[464,128]{1,0:T(8,128)S(1)}, u32[]{:S(2)}, u32[]{:S(2)}) collective-permute-start(f32[464,128]{1,0:T(8,128)S(1)} %copy-done.7), channel_id=1, source_target_pairs={{0,30},{2,4},{4,2},{6,8},{8,6},{10,12},{12,10},{14,16},{16,14},{18... | collective-permute-start | bytes 712712 | tf_op jit(solution)/shard_map/ppermute | solution.py:333
  21.2 0.0 collective-permute-done.1.refs_2_
  21.2 0.0 copy-start.1
  21.2 5.7 %collective-permute-done.2.refs_3_ = f32[464,128]{1,0:T(8,128)S(1)} collective-permute-done((f32[464,128]{1,0:T(8,128)S(1)}, f32[464,128]{1,0:T(8,128)S(1)}, u32[]{:S(2)}, u32[]{:S(2)}) %collective-permute-start.2) | collective-permute-done | bytes 237600 | tf_op jit(solution)/shard_map/ppermute | solution.py:333
  26.9 0.0 copy-start.2
  26.9 0.0 all-to-all-done
  26.9 0.0 copy-start
  26.9 0.0 copy-done.1
  26.9 0.7 %copy-done.2 = f32[464,128]{1,0:T(8,128)} copy-done((f32[464,128]{1,0:T(8,128)}, f32[464,128]{1,0:T(8,128)S(1)}, u32[]{:S(2)}) %copy-start.2) | copy-done | bytes 237592
  27.6 0.1 copy-done
  27.7 6.3 %step.1 = f32[36,1,6,8,128]{4,3,2,1,0:T(8,128)} custom-call(s32[6]{0:T(128)} %refs_0_.3, f32[36,1,6,8,128]{4,3,2,1,0:T(8,128)} %refs_1_.3, f32[464,128]{1,0:T(8,128)} %copy-done.1, f32[464,128]{1,0:T(8,128)} %copy-done.2, f32[128,256]{1,0:T(8,128)} %bitcast.2, f32[8,256]{1,0:T(8,128)} %get-tuple-element.13.refs_5_, f32[18,8,128]{2,1,0:T(8,128)} %get-tuple-element.14.refs_6_), custom_call_target="tpu_custom_call" | custom-call | tf_op jit(solution)/shard_map/step/pallas_call | solution.py:334
  (2 shorter events, 0.0 us)
Async XLA Ops:
  0.0 0.8 %copy-start.5 = (f32[1,6,8,64]{3,2,1,0:T(8,128)S(1)}, f32[1,6,8,64]{3,2,1,0:T(8,128)}, u32[]{:S(2)}) copy-start(f32[1,6,8,64]{3,2,1,0:T(8,128)} %param.7) | copy-start | bytes 36868
  0.8 0.7 %copy-start.6 = (f32[1,6,8,64]{3,2,1,0:T(8,128)S(1)}, f32[1,6,8,64]{3,2,1,0:T(8,128)}, u32[]{:S(2)}) copy-start(f32[1,6,8,64]{3,2,1,0:T(8,128)} %param.8) | copy-start | bytes 36868
  1.5 5.3 %copy-start.3 = (f32[3,6,8,64]{3,2,1,0:T(8,128)}, f32[3,6,8,64]{3,2,1,0:T(8,128)S(1)}, u32[]{:S(2)}) copy-start(f32[3,6,8,64]{3,2,1,0:T(8,128)S(1)} %constant_dynamic-update-slice_fusion.refs_2_) | copy-start | bytes 110596
  1.5 5.3 %collective-permute-start = (f32[3,6,8,64]{3,2,1,0:T(8,128)S(1)}, f32[3,6,8,64]{3,2,1,0:T(8,128)S(1)}, u32[]{:S(2)}, u32[]{:S(2)}) collective-permute-start(f32[3,6,8,64]{3,2,1,0:T(8,128)S(1)} %constant_dynamic-update-slice_fusion.refs_2_), channel_id=1, source_target_pairs={{0,1},{1,0},{2,3},{3,2},{4,5},{5,4},{6,7},{7,6},{8,9},{9,8},{10,11... | collective-permute-start | bytes 110600 | tf_op jit(solution)/shard_map/ppermute | solution.py:310
  6.8 0.6 %copy-start.4 = (f32[3,6,8,64]{3,2,1,0:T(8,128)}, f32[3,6,8,64]{3,2,1,0:T(8,128)S(1)}, u32[]{:S(2)}) copy-start(f32[3,6,8,64]{3,2,1,0:T(8,128)S(1)} %collective-permute-done.refs_3_) | copy-start | bytes 110596
  10.3 6.6 %copy-start.7 = (f32[464,128]{1,0:T(8,128)S(1)}, f32[464,128]{1,0:T(8,128)}, u32[]{:S(2)}) copy-start(f32[464,128]{1,0:T(8,128)} %get-tuple-element.11) | copy-start | bytes 712708
  10.3 16.7 %all-to-all-start = ((f32[16,8,256]{2,1,0:T(8,128)}), f32[16,8,256]{2,1,0:T(8,128)S(1)}, u32[]{:S(2)}, u32[]{:S(2)}) async-start(f32[16,8,256]{2,1,0:T(8,128)} %bitcast.3), calls=%async_computation | async-start | bytes 262144 | tf_op jit(solution)/shard_map/all_to_all | solution.py:330
  16.4 4.8 %collective-permute-start.1 = (f32[464,128]{1,0:T(8,128)}, f32[464,128]{1,0:T(8,128)S(1)}, u32[]{:S(2)}, u32[]{:S(2)}) collective-permute-start(f32[464,128]{1,0:T(8,128)} %get-tuple-element.10), channel_id=1, source_target_pairs={{0,2},{2,0},{4,6},{6,4},{8,10},{10,8},{12,14},{14,12},{16,18},{18,... | collective-permute-start | bytes 712712 | tf_op jit(solution)/shard_map/ppermute | solution.py:331
  16.8 10.1 %collective-permute-start.2 = (f32[464,128]{1,0:T(8,128)S(1)}, f32[464,128]{1,0:T(8,128)S(1)}, u32[]{:S(2)}, u32[]{:S(2)}) collective-permute-start(f32[464,128]{1,0:T(8,128)S(1)} %copy-done.7), channel_id=1, source_target_pairs={{0,30},{2,4},{4,2},{6,8},{8,6},{10,12},{12,10},{14,16},{16,14},{18... | collective-permute-start | bytes 712712 | tf_op jit(solution)/shard_map/ppermute | solution.py:333
  21.2 5.7 %copy-start.1 = (f32[464,128]{1,0:T(8,128)}, f32[464,128]{1,0:T(8,128)S(1)}, u32[]{:S(2)}) copy-start(f32[464,128]{1,0:T(8,128)S(1)} %collective-permute-done.1.refs_2_) | copy-start | bytes 712708
  26.9 0.7 %copy-start.2 = (f32[464,128]{1,0:T(8,128)}, f32[464,128]{1,0:T(8,128)S(1)}, u32[]{:S(2)}) copy-start(f32[464,128]{1,0:T(8,128)S(1)} %collective-permute-done.2.refs_3_) | copy-start | bytes 712708
  26.9 0.7 %copy-start = (f32[16,8,256]{2,1,0:T(8,128)}, f32[16,8,256]{2,1,0:T(8,128)S(1)}, u32[]{:S(2)}) copy-start(f32[16,8,256]{2,1,0:T(8,128)S(1)} %all-to-all-done) | copy-start | bytes 393220

commit v2 on v1

v2 whole, which is shorter than its diff:
```python
import jax
import jax.numpy as jnp
from jax import lax
from jax.experimental import pallas as pl
from jax.experimental.pallas import tpu as pltpu
from jax.sharding import PartitionSpec as P

F32 = jnp.float32
VMEM_LIMIT = 12 << 20


def up(value, unit):
    return -(-value // unit) * unit


class Sizes:
    def __init__(self, mixing, halves, tiles):
        self.species, _, _, self.rows, self.width = mixing.shape
        self.tiles, self.halves = tiles, halves
        self.part = self.width // halves
        self.group = up(2 * self.species, 8)
        self.flux = 3 * self.group
        self.flux2 = self.flux + 8
        self.lanes = up(self.flux2 + 8, 128)
        self.vregs = self.lanes // 128
        self.dp_at = 2 * self.flux
        self.fy_at = self.dp_at + 8
        self.extra = self.fy_at + 8
        self.sent = self.extra + 8 * self.vregs
        self.per = 128 // self.part
        self.own = up(18, self.per) // self.per
        self.chunks = 4


def slots(face_slot):
    return [sum(jnp.where(face_slot[s] == f, s, 0) for s in range(6)) for f in range(6)]


def roll(x, shift, axis):
    shift %= x.shape[axis]
    return pltpu.roll(x, shift, axis) if shift else x


def reverse8(x):
    row = lax.broadcasted_iota(jnp.int32, x.shape, 0)
    x = jnp.where((row & 1) == 0, roll(x, -1, 0), roll(x, 1, 0))
    x = jnp.where((row & 2) == 0, roll(x, -2, 0), roll(x, 2, 0))
    return roll(x, 4, 0)


def pack_kernel(
    z, face_slot, mixing_in, dp_in, fx_in, fy_in, to_a, to_b, out, kept, full, own, order, mixing, fluxes, sems
):
    cuts = [z.species * n // z.chunks for n in range(z.chunks + 1)]
    copies = [
        pltpu.make_async_copy(ref, fluxes.at[c], sems.at[c]) for c, ref in enumerate((dp_in, fx_in, fy_in))
    ]
    for n in range(z.chunks):
        some = pl.ds(cuts[n], cuts[n + 1] - cuts[n])
        copies.append(pltpu.make_async_copy(mixing_in.at[some], mixing.at[some], sems.at[3 + n]))
    for copy in copies:
        copy.start()
    place = lax.axis_index("tile")
    half = lax.axis_index("spec")
    slot = slots(face_slot)
    even = lax.rem(place, 2) == 0
    first, last = place == 0, place == z.tiles - 1
    width, part, species, n_half = z.width, z.part, z.species, z.halves
    places = lax.broadcasted_iota(jnp.int32, (8, 128), 1)
    order[...] = sum(jnp.where(places == f, slot[f], 0) for f in range(6))
    for copy in copies[:3]:
        copy.wait()
    raw = [[fluxes[c, 0, slot[f]] for f in range(6)] for c in range(3)]

    def placed(x):
        return jnp.concatenate([jnp.where(half == n, x, 0.0) for n in range(n_half)], axis=-1)

    for c in range(3):
        for f in range(6):
            full[c * 6 + f] = placed(raw[c][f])
    flat = [raw[c][f] for c in range(3) for f in range(6)]
    for n in range(z.own):
        tiles = flat[n * z.per : (n + 1) * z.per]
        tiles += [tiles[0]] * (z.per - len(tiles))
        own[n] = jnp.concatenate(tiles, axis=-1) if z.per > 1 else tiles[0]

    def both(low, high, at):
        to_a[pl.ds(at, low.shape[0])] = jnp.where(even, high, low)
        to_b[pl.ds(at, low.shape[0])] = jnp.where(even, low, high)

    pad = jnp.zeros((2, part), F32)
    low_dp = jnp.concatenate([x[0:1] for x in raw[0]] + [pad], axis=0)
    high_dp = jnp.concatenate([x[7:8] for x in raw[0]] + [pad], axis=0)
    low_fy = jnp.concatenate([x[0:1] for x in raw[2]] + [pad], axis=0)
    both(placed(low_dp), placed(high_dp), z.dp_at)
    both(placed(low_fy), placed(low_fy), z.fy_at)

    lane = lax.broadcasted_iota(jnp.int32, (8, 128), 1)
    gathers = [[jnp.zeros((8, 128), F32) for _ in range(z.vregs)] for _ in range(2)]
    for parity in range(2):
        for a in range(3):
            f = 2 * a + parity
            if z.group > 2 * species:
                zero = jnp.zeros((z.group - 2 * species, width), F32)
                both(zero, zero, parity * z.flux + a * z.group + 2 * species)
            for c in range(2):
                at = z.flux2 + 3 * c + a
                tile = full[c * 6 + f]
                edge = tile[:, :128] if parity == 0 else tile[:, width - 128 :]
                moved = roll(edge, at - (0 if parity == 0 else 127), 1)
                k = at // 128
                gathers[parity][k] = jnp.where(lane == at % 128, moved, gathers[parity][k])
    for n in range(z.chunks):
        copies[3 + n].wait()
        for s in range(cuts[n], cuts[n + 1]):
            for f in range(6):
                a, parity = f // 2, f % 2
                tile = mixing[s, 0, slot[f]]
                at = a * z.group + 2 * s
                both(tile[0:2], tile[6:8], parity * z.flux + at)
                edge = tile[:, :128] if parity == 0 else tile[:, width - 128 :]
                moved = roll(edge, at - (0 if parity == 0 else 126), 1)
                k = at // 128
                gathers[parity][k] = jnp.where((lane >> 1) == (at % 128) // 2, moved, gathers[parity][k])
    gathers = [[reverse8(x) for x in lanes] for lanes in gathers]
    for k in range(z.vregs):
        even_cols, odd_cols = gathers[0][k], gathers[1][k]
        kept[:, k * 128 : (k + 1) * 128] = jnp.where(first, odd_cols, even_cols)
        spare = jnp.where(first, even_cols, odd_cols)
        spare = jnp.concatenate([spare] * (width // 128), axis=-1) if width > 128 else spare
        to_a[pl.ds(z.extra + 8 * k, 8)] = spare
        to_b[pl.ds(z.extra + 8 * k, 8)] = spare

    ends = ((0, gathers[1]), (z.tiles - 1, gathers[0]))

    @pl.when(first | last)
    def _():
        start = pl.multiple_of(jnp.where(first, z.flux, 0), 8)
        edge_rows = [
            jnp.where(first, raw[c][2 * a + 1][0:1], raw[c][2 * a][7:8]) for c in (0, 2) for a in range(3)
        ]
        rows = [
            to_b[pl.ds(start, z.flux)],
            placed(jnp.concatenate(edge_rows + [pad], axis=0)),
            jnp.zeros((z.lanes - z.flux - 8, width), F32),
        ]
        turned = jnp.concatenate(rows, axis=0).T
        for t in range(z.tiles):
            at = 8 * (z.tiles - 1 - t)
            for n in range(n_half):
                out[t * n_half + n] = turned[at : at + 8]
        for t, cols in ends:
            at = 8 * (z.tiles - 1 - t)
            k = z.flux2 // 128
            here = (lane >= z.flux2 % 128) & (lane < z.flux2 % 128 + 8)
            mixed = jnp.where(here, cols[k], turned[at : at + 8, k * 128 : (k + 1) * 128])
            for n in range(n_half):
                out[t * n_half + n, :, k * 128 : (k + 1) * 128] = mixed

    @pl.when(jnp.logical_not(first | last))
    def _():
        for t, cols in ends:
            for n in range(n_half):
                for k in range(z.vregs):
                    out[t * n_half + n, :, k * 128 : (k + 1) * 128] = cols[k]

    north = lax.rem(place + 1, z.tiles) * n_half
    south = lax.rem(place + z.tiles - 1, z.tiles) * n_half
    for d in range(1, n_half):
        other = lax.rem(half + d, n_half)
        out[north + other, :, 0 : 2 * part] = jnp.concatenate([high_dp, high_dp], axis=-1)
        out[south + other, :, 0 : 2 * part] = jnp.concatenate([low_dp, low_fy], axis=-1)


def step_kernel(
    z, order_in, mixing, from_a, from_b, arrived, kept, full_in, others, out,
    order, south, north, turned, side, coef, result, order_sem, out_sem,
):
    place = lax.axis_index("tile")
    half = lax.axis_index("spec")
    fetch = pltpu.make_async_copy(order_in, order, order_sem)
    fetch.start()
    even = lax.rem(place, 2) == 0
    first = place == 0
    last = place == z.tiles - 1
    width, part, species, n_half = z.width, z.part, z.species, z.halves
    lane = lax.broadcasted_iota(jnp.int32, (8, width), 1)
    row = lax.broadcasted_iota(jnp.int32, (8, width), 0)
    lane1 = lax.broadcasted_iota(jnp.int32, (8, 128), 1)

    halo = z.dp_at
    a_rows, b_rows = from_a[0:halo], from_b[0:halo]
    south[0:halo] = jnp.where(even, b_rows, a_rows)
    north[0:halo] = jnp.where(even, a_rows, b_rows)

    @pl.when(first | last)
    def _():
        holder = jnp.where(first, n_half - 1, 0)
        pieces = []
        for k in range(z.vregs):
            lanes = slice(k * 128, (k + 1) * 128)
            spare = from_b[z.extra + 8 * k : z.extra + 8 * k + 8, 0:128]
            mine = kept[:, lanes]
            parts = []
            for t in reversed(range(z.tiles)):
                if t == 0:
                    x = jnp.where(first, mine, spare)
                elif t == z.tiles - 1:
                    x = jnp.where(first, spare, mine)
                else:
                    x = arrived[t * n_half + half, :, lanes]
                if (k + 1) * 128 > z.flux:
                    x = jnp.where(lane1 + k * 128 < z.flux, x, arrived[t * n_half + holder, :, lanes])
                parts.append(x)
            pieces.append(jnp.concatenate(parts, axis=0).T)
        ghost = jnp.concatenate(pieces, axis=0) if len(pieces) > 1 else pieces[0]

        @pl.when(first)
        def _():
            south[halo : halo + z.flux] = ghost[: z.flux]

        @pl.when(last)
        def _():
            north[halo : halo + z.flux] = ghost[: z.flux]

        turned[...] = ghost[z.flux2 : z.flux2 + 8]

    full = []
    for n in range(18):
        at = (n % z.per) * part
        if n_half == 2:
            x = others[n // z.per][:, at : at + part]
            rest = jnp.concatenate([jnp.where(half == h, 0.0, x) for h in range(2)], axis=-1)
            full.append(full_in[n] + rest)
        else:
            full.append(
                jnp.concatenate([others[h, n // z.per][:, at : at + part] for h in range(n_half)], axis=-1)
            )

    def edge_rows(neighbour, which, mine):
        total = mine
        for n in range(n_half):
            x = arrived[neighbour * n_half + n, :, 0:128]
            x = jnp.concatenate([x] * (width // 128), axis=-1) if width > 128 else x
            x = roll(x, (n - which) * part, 1)
            total = jnp.where((lane >= n * part) & (lane < (n + 1) * part) & (half != n), x, total)
        return total

    below_tile = lax.rem(place + z.tiles - 1, z.tiles)
    above_tile = lax.rem(place + 1, z.tiles)
    a_dp, b_dp = from_a[z.dp_at : z.dp_at + 8], from_b[z.dp_at : z.dp_at + 8]
    a_fy, b_fy = from_a[z.fy_at : z.fy_at + 8], from_b[z.fy_at : z.fy_at + 8]
    dp_south = edge_rows(below_tile, 0, jnp.where(even, b_dp, a_dp))
    dp_north = edge_rows(above_tile, 0, jnp.where(even, a_dp, b_dp))
    fy_north = edge_rows(above_tile, 1, jnp.where(even, a_fy, b_fy))
    gathered = turned[...]

    block = z.flux
    south_at = [jnp.where(first, block, 0), jnp.where(first, 2 * block, block)]
    north_at = [jnp.where(last, 2 * block, 0), jnp.where(last, 0, block)]
    south_a = [jnp.where(first, (a + 2) % 3, a) for a in range(3)]
    north_a = [jnp.where(last, (a + 1) % 3, a) for a in range(3)]

    def come(end, holder):
        tracer = [reverse8(arrived[end * n_half + half, :, k * 128 : (k + 1) * 128]) for k in range(z.vregs)]
        k = z.flux // 128
        return tracer, reverse8(arrived[end * n_half + holder, :, k * 128 : (k + 1) * 128])

    holder = lax.div(width - 8 - 8 * place, part)
    east_cols, east_flux = come(0, holder)
    west_cols, west_flux = come(z.tiles - 1, holder)

    def column(flux, n):
        at = (z.flux + n) % 128
        return flux[:, at : at + 1]

    def left(x, ghost, n):
        return pltpu.roll(jnp.where(lane >= width - n, ghost, x), n, 1)

    def right(x, ghost, n):
        return pltpu.roll(jnp.where(lane < n, ghost, x), width - n, 1)

    def below(x, ghost, n):
        return pltpu.roll(jnp.where(row >= 8 - n, ghost, x), n, 0)

    def above(x, ghost, n):
        return pltpu.roll(jnp.where(row < n, ghost, x), 8 - n, 0)

    def upwind(u, total):
        return 0.5 * jnp.abs(u) * (1.0 - jnp.abs(u / (0.5 * total)))

    for f in range(6):
        a, parity = f // 2, f % 2
        dp, fx, fy = full[f], full[6 + f], full[12 + f]
        if parity == 0:
            west = column(west_flux, (a + 2) % 3)
            east, east_u = full[f + 1], full[6 + f + 1]
            s_end = roll(dp_south, 7 - (f - 1) % 6, 0)
            n_end = [roll(gathered, -((a + 1) % 3) - 3 * c, 0) for c in range(2)]
        else:
            west = full[f - 1]
            east = column(east_flux, (a + 1) % 3)
            east_u = column(east_flux, 3 + (a + 1) % 3)
            s_end = roll(gathered, 7 - (a + 2) % 3, 0)
            n_end = [roll(x, -((f + 1) % 6), 0) for x in (dp_north, fy_north)]
        dp_w, dp_e = left(dp, west, 1), right(dp, east, 1)
        u0, u1 = fx, right(fx, east_u, 1)
        dp_s = below(dp, jnp.where(first, s_end, roll(dp_south, 7 - f, 0)), 1)
        dp_n = above(dp, jnp.where(last, n_end[0], roll(dp_north, -f, 0)), 1)
        v0, v1 = fy, above(fy, jnp.where(last, n_end[1], roll(fy_north, -f, 0)), 1)
        inverse = 1.0 / (dp - (u1 - u0) - (v1 - v0))
        center = dp
        for n, (w0, w1, d0, d1) in enumerate(((u0, u1, dp_w, dp_e), (v0, v1, dp_s, dp_n))):
            b0, b1 = upwind(w0, d0 + dp), upwind(w1, dp + d1)
            p0, p1 = w0 * (1.0 / 12.0), w1 * (1.0 / 12.0)
            coef[f, 4 * n] = -p0 * inverse
            coef[f, 4 * n + 1] = (7.0 * p0 + b0 + p1) * inverse
            coef[f, 4 * n + 2] = (-p0 - 7.0 * p1 + b1) * inverse
            coef[f, 4 * n + 3] = p1 * inverse
            center = center + (7.0 * p0 - b0) - (7.0 * p1 + b1)
        coef[f, 8] = center * inverse

    for a in range(3):
        for s in range(species):
            east_at = ((a + 1) % 3) * z.group + 2 * s
            west_at = ((a + 2) % 3) * z.group + 2 * s
            east = roll(east_cols[east_at // 128], -east_at, 1)
            west = roll(west_cols[west_at // 128], 126 - west_at, 1)
            side[a * species + s] = jnp.where(lane1 < 2, east, west)

    fetch.wait()
    slot = [order[0, f] for f in range(6)]

    def strip(a, first_s, count, south_rows, north_rows):
        fe, fo = 2 * a, 2 * a + 1
        ce = [coef[fe, n] for n in range(9)]
        co = [coef[fo, n] for n in range(9)]
        for u in range(count):
            s = first_s + u
            qe, qo = mixing[s, 0, slot[fe]], mixing[s, 0, slot[fo]]
            g = side[a * species + s]
            g = jnp.concatenate([g] * (width // 128), axis=-1) if width > 128 else g
            for q, west, east, c, parity, f in ((qe, g, qo, ce, 0, fe), (qo, qe, g, co, 1, fo)):
                sv = roll(south_rows[parity], 6 - 2 * u, 0)
                nv = roll(north_rows[parity], -2 * u, 0)
                value = c[8] * q
                value += c[0] * left(q, west, 2)
                value += c[1] * left(q, west, 1)
                value += c[2] * right(q, east, 1)
                value += c[3] * right(q, east, 2)
                value += c[4] * below(q, sv, 2)
                value += c[5] * below(q, sv, 1)
                value += c[6] * above(q, nv, 1)
                value += c[7] * above(q, nv, 2)
                result[s, slot[f]] = value

    def quad(it, count):
        for a in range(3):
            at = [south_at[p] + south_a[a] * z.group + 8 * it for p in range(2)]
            s_rows = [south[pl.ds(pl.multiple_of(x, 8), 8)] for x in at]
            at = [north_at[p] + north_a[a] * z.group + 8 * it for p in range(2)]
            n_rows = [north[pl.ds(pl.multiple_of(x, 8), 8)] for x in at]
            strip(a, 4 * it, count, s_rows, n_rows)
        part = pl.ds(4 * it, count)
        pltpu.make_async_copy(result.at[part], out.at[part, 0], out_sem).start()

    @pl.loop(0, species // 4)
    def _(it):
        quad(it, 4)

    if species % 4:
        quad(species // 4, species % 4)
    pltpu.make_async_copy(result, out.at[:, 0], out_sem).wait()


def local(mixing, layer_mass, mass_east, mass_north, face_slot):
    tiles = lax.axis_size("tile")
    halves = lax.axis_size("spec")
    z = Sizes(mixing, halves, tiles)
    assert z.rows == 8 and mixing.shape[1] == 1 and tiles > 2 and tiles % 2 == 0
    assert z.width == 8 * tiles and z.width % 128 == 0 and 128 % z.part == 0 and 2 * z.part <= z.flux
    smem = pl.BlockSpec(memory_space=pltpu.SMEM)
    vmem = pl.BlockSpec(memory_space=pltpu.VMEM)
    params = pltpu.CompilerParams(vmem_limit_bytes=VMEM_LIMIT)

    def f32(*shape):
        return jax.ShapeDtypeStruct(shape, F32)

    to_a, to_b, messages, kept, full, own, order = pl.pallas_call(
        lambda *refs: pack_kernel(z, *refs),
        out_shape=(
            f32(z.sent, z.width),
            f32(z.sent, z.width),
            f32(tiles * halves, 8, z.lanes),
            f32(8, z.lanes),
            f32(18, 8, z.width),
            f32(z.own, 8, 128),
            jax.ShapeDtypeStruct((8, 128), jnp.int32),
        ),
        in_specs=[smem] + [pl.BlockSpec(memory_space=pltpu.HBM)] * 4,
        out_specs=[vmem] * 7,
        scratch_shapes=[
            pltpu.VMEM(mixing.shape, F32),
            pltpu.VMEM((3,) + layer_mass.shape, F32),
            pltpu.SemaphoreType.DMA((3 + z.chunks,)),
        ],
        name="pack",
    )(face_slot, mixing, layer_mass, mass_east, mass_north)
    arrived = lax.all_to_all(messages, ("tile", "spec"), 0, 0, tiled=True)
    if halves == 2:
        others = lax.ppermute(own, "spec", [(0, 1), (1, 0)])
    else:
        others = lax.all_gather(own, "spec", axis=0, tiled=False)
    from_a = lax.ppermute(to_a, "tile", [(i, i ^ 1) for i in range(tiles)])
    pairs = [(i, (i + 1) % tiles) if i % 2 else (i, (i - 1) % tiles) for i in range(tiles)]
    from_b = lax.ppermute(to_b, "tile", pairs)
    return pl.pallas_call(
        lambda *refs: step_kernel(z, *refs),
        out_shape=f32(*mixing.shape),
        in_specs=[vmem] * 8,
        out_specs=pl.BlockSpec(memory_space=pl.ANY),
        scratch_shapes=[
            pltpu.SMEM((8, 128), jnp.int32),
            pltpu.VMEM((3 * z.flux, z.width), F32),
            pltpu.VMEM((3 * z.flux, z.width), F32),
            pltpu.VMEM((8, z.width), F32),
            pltpu.VMEM((3 * z.species, 8, 128), F32),
            pltpu.VMEM((6, 9, 8, z.width), F32),
            pltpu.VMEM((z.species, 6, 8, z.width), F32),
            pltpu.SemaphoreType.DMA,
            pltpu.SemaphoreType.DMA,
        ],
        compiler_params=params,
        name="step",
    )(order, mixing, from_a, from_b, arrived, kept, full, others)


def solution(mesh):
    flux = P(None, None, "tile", "spec")
    cells = P("spec", None, None, "tile", None)
    return jax.shard_map(
        local,
        mesh=mesh,
        in_specs=(cells, flux, flux, flux, P()),
        out_specs=cells,
        check_vma=False,
    )
```

time: 34.4 us -> 26.6 us (0.77)
  the two profiles are of different devices: /device:TPU:0 before, /device:TPU:1 now
where the time goes in v2:
time: 26.6 us; the launch traced here: 26.4 us
  starting transfers between devices  10.1 us (38%)
  waiting for transfers between devices  10 us (38%)
  Pallas kernels  6.15 us (23%)
    all_to_all x1, starting transfers between devices, local(): arrived = lax.all_to_all(messages, ('tile', 'spec'), 0, 0, tiled=True)  7.1 us
    all_to_all x1, waiting for transfers between devices, local(): arrived = lax.all_to_all(messages, ('tile', 'spec'), 0, 0, tiled=True)  3.85 us
    ppermute x1, waiting for transfers between devices, local(): from_b = lax.ppermute(to_b, 'tile', pairs)  3.81 us
    pallas_call x1, Pallas kernels, local(): pl.pallas_call(lambda *refs: pack_kernel(z, *refs), out_shape=(f32(z.sent...  3.28 us
    pallas_call x1, Pallas kernels, local(): pl.pallas_call(lambda *refs: step_kernel(z, *refs), out_shape=f32(*mixing...  2.88 us
    ppermute x1, waiting for transfers between devices, local(): others = lax.ppermute(own, 'spec', [(0, 1), (1, 0)])  2.36 us
    ppermute x1, starting transfers between devices, local(): from_b = lax.ppermute(to_b, 'tile', pairs)  1.52 us
    ppermute x1, starting transfers between devices, local(): others = lax.ppermute(own, 'spec', [(0, 1), (1, 0)])  1.18 us
  transfers between devices with their start and end apart: 4, of which 3 were waited for; matrix products, arithmetic and copies ran while one was open for 0% of the time, Pallas kernels for 0%

profile of v2, /device:TPU:1, one launch (start us, length us, event | category | flops | bytes accessed | tf_op | source)
XLA Modules:
  0.0 26.4 jit_solution(2071214380639783065)
XLA Ops:
  0.0 0.0 copy-start
  0.0 3.3 %pack.1 = (f32[464,128]{1,0:T(8,128)}, f32[464,128]{1,0:T(8,128)}, f32[32,8,256]{2,1,0:T(8,128)}, f32[8,256]{1,0:T(8,128)}, f32[18,8,128]{2,1,0:T(8,128)}, /*index=5*/f32[9,8,128]{2,1,0:T(8,128)}, s32[8,128]{1,0:T(8,128)}) custom-call(s32[6]{0:T(128)} %refs_0_.1, f32[36,1,6,8,128]{4,3,2,1,0:T(8,128)} %refs_1_.3, f32[1,6,8,64]{3,2,1,0:T(8,128)} %refs_2_.1, ...), custom_call_target="tpu_custom_call" | custom-call | tf_op jit(solution)/shard_map/pack/pallas_call | solution.py:389
  3.3 0.0 copy-start.4
  3.3 0.0 copy-start.5
  3.3 0.0 copy-start.1
  3.3 0.0 copy-start.3
  3.3 7.1 %all-to-all-start = ((f32[32,8,256]{2,1,0:T(8,128)}), f32[32,8,256]{2,1,0:T(8,128)S(1)}, u32[]{:S(2)}, u32[]{:S(2)}) async-start(f32[32,8,256]{2,1,0:T(8,128)} %get-tuple-element.15), calls=%async_computation | async-start | bytes 524288 | tf_op jit(solution)/shard_map/all_to_all | solution.py:409
  10.4 0.0 copy-start.2
  10.4 0.3 %collective-permute-start = (f32[464,128]{1,0:T(8,128)}, f32[464,128]{1,0:T(8,128)S(1)}, u32[]{:S(2)}, u32[]{:S(2)}) collective-permute-start(f32[464,128]{1,0:T(8,128)} %get-tuple-element.13), channel_id=1, source_target_pairs={{0,2},{2,0},{4,6},{6,4},{8,10},{10,8},{12,14},{14,12},{16,18},{18,... | collective-permute-start | bytes 712712 | tf_op jit(solution)/shard_map/ppermute | solution.py:414
  10.8 0.0 copy-done.4
  10.8 1.5 %collective-permute-start.1 = (f32[464,128]{1,0:T(8,128)S(1)}, f32[464,128]{1,0:T(8,128)S(1)}, u32[]{:S(2)}, u32[]{:S(2)}) collective-permute-start(f32[464,128]{1,0:T(8,128)S(1)} %copy-done.4), channel_id=1, source_target_pairs={{0,30},{2,4},{4,2},{6,8},{8,6},{10,12},{12,10},{14,16},{16,14},{18... | collective-permute-start | bytes 712712 | tf_op jit(solution)/shard_map/ppermute | solution.py:416
  12.3 0.0 copy-done.5
  12.3 1.2 %collective-permute-start.2 = (f32[9,8,128]{2,1,0:T(8,128)S(1)}, f32[9,8,128]{2,1,0:T(8,128)S(1)}, u32[]{:S(2)}, u32[]{:S(2)}) collective-permute-start(f32[9,8,128]{2,1,0:T(8,128)S(1)} %copy-done.5), channel_id=1, source_target_pairs={{0,1},{1,0},{2,3},{3,2},{4,5},{5,4},{6,7},{7,6},{8,9},{9,8},{10,11... | collective-permute-start | bytes 110600 | tf_op jit(solution)/shard_map/ppermute | solution.py:411
  13.5 2.4 %collective-permute-done.2.refs_7_ = f32[9,8,128]{2,1,0:T(8,128)S(1)} collective-permute-done((f32[9,8,128]{2,1,0:T(8,128)S(1)}, f32[9,8,128]{2,1,0:T(8,128)S(1)}, u32[]{:S(2)}, u32[]{:S(2)}) %collective-permute-start.2) | collective-permute-done | bytes 36896 | tf_op jit(solution)/shard_map/ppermute | solution.py:411
  15.8 0.0 collective-permute-done.refs_2_
  15.8 3.8 %collective-permute-done.1.refs_3_ = f32[464,128]{1,0:T(8,128)S(1)} collective-permute-done((f32[464,128]{1,0:T(8,128)S(1)}, f32[464,128]{1,0:T(8,128)S(1)}, u32[]{:S(2)}, u32[]{:S(2)}) %collective-permute-start.1) | collective-permute-done | bytes 237600 | tf_op jit(solution)/shard_map/ppermute | solution.py:416
  19.6 3.8 %all-to-all-done.refs_4_ = f32[32,8,256]{2,1,0:T(8,128)S(1)} async-done(((f32[32,8,256]{2,1,0:T(8,128)}), f32[32,8,256]{2,1,0:T(8,128)S(1)}, u32[]{:S(2)}, u32[]{:S(2)}) %all-to-all-start) | async-done | bytes 262176 | tf_op jit(solution)/shard_map/all_to_all | solution.py:409
  23.5 0.0 copy-done
  23.5 0.0 copy-done.1
  23.5 0.0 copy-done.3
  23.5 0.0 copy-done.2
  23.5 2.9 %step.1 = f32[36,1,6,8,128]{4,3,2,1,0:T(8,128)} custom-call(s32[8,128]{1,0:T(8,128)S(1)} %copy-done.3, f32[36,1,6,8,128]{4,3,2,1,0:T(8,128)S(1)} %copy-done, f32[464,128]{1,0:T(8,128)S(1)} %collective-permute-done.refs_2_, f32[464,128]{1,0:T(8,128)S(1)} %collective-permute-done.1.refs_3_, f32[32,8,256]{2,1,0:T(8,128)S(1)} %all-to-all-done.refs_4_, ...), custom_call_target="tpu_custom_call" | custom-call | tf_op jit(solution)/shard_map/step/pallas_call | solution.py:417
Async XLA Ops:
  0.0 23.5 %copy-start = (f32[36,1,6,8,128]{4,3,2,1,0:T(8,128)S(1)}, f32[36,1,6,8,128]{4,3,2,1,0:T(8,128)}, u32[]{:S(2)}) copy-start(f32[36,1,6,8,128]{4,3,2,1,0:T(8,128)} %refs_1_.3) | copy-start | bytes 2654212
  3.3 7.5 %copy-start.4 = (f32[464,128]{1,0:T(8,128)S(1)}, f32[464,128]{1,0:T(8,128)}, u32[]{:S(2)}) copy-start(f32[464,128]{1,0:T(8,128)} %get-tuple-element.14) | copy-start | bytes 712708
  3.3 9.0 %copy-start.5 = (f32[9,8,128]{2,1,0:T(8,128)S(1)}, f32[9,8,128]{2,1,0:T(8,128)}, u32[]{:S(2)}) copy-start(f32[9,8,128]{2,1,0:T(8,128)} %get-tuple-element.18) | copy-start | bytes 110596
  3.3 20.2 %copy-start.1 = (f32[18,8,128]{2,1,0:T(8,128)S(1)}, f32[18,8,128]{2,1,0:T(8,128)}, u32[]{:S(2)}) copy-start(f32[18,8,128]{2,1,0:T(8,128)} %get-tuple-element.17.refs_6_) | copy-start | bytes 221188
  3.3 20.2 %copy-start.3 = (s32[8,128]{1,0:T(8,128)S(1)}, s32[8,128]{1,0:T(8,128)}, u32[]{:S(2)}) copy-start(s32[8,128]{1,0:T(8,128)} %get-tuple-element.12.refs_0_) | copy-start | bytes 12292
  3.3 20.2 %all-to-all-start = ((f32[32,8,256]{2,1,0:T(8,128)}), f32[32,8,256]{2,1,0:T(8,128)S(1)}, u32[]{:S(2)}, u32[]{:S(2)}) async-start(f32[32,8,256]{2,1,0:T(8,128)} %get-tuple-element.15), calls=%async_computation | async-start | bytes 524288 | tf_op jit(solution)/shard_map/all_to_all | solution.py:409
  10.4 13.1 %copy-start.2 = (f32[8,256]{1,0:T(8,128)S(1)}, f32[8,256]{1,0:T(8,128)}, u32[]{:S(2)}) copy-start(f32[8,256]{1,0:T(8,128)} %get-tuple-element.16.refs_5_) | copy-start | bytes 24580
  10.4 5.4 %collective-permute-start = (f32[464,128]{1,0:T(8,128)}, f32[464,128]{1,0:T(8,128)S(1)}, u32[]{:S(2)}, u32[]{:S(2)}) collective-permute-start(f32[464,128]{1,0:T(8,128)} %get-tuple-element.13), channel_id=1, source_target_pairs={{0,2},{2,0},{4,6},{6,4},{8,10},{10,8},{12,14},{14,12},{16,18},{18,... | collective-permute-start | bytes 712712 | tf_op jit(solution)/shard_map/ppermute | solution.py:414
  10.8 8.9 %collective-permute-start.1 = (f32[464,128]{1,0:T(8,128)S(1)}, f32[464,128]{1,0:T(8,128)S(1)}, u32[]{:S(2)}, u32[]{:S(2)}) collective-permute-start(f32[464,128]{1,0:T(8,128)S(1)} %copy-done.4), channel_id=1, source_target_pairs={{0,30},{2,4},{4,2},{6,8},{8,6},{10,12},{12,10},{14,16},{16,14},{18... | collective-permute-start | bytes 712712 | tf_op jit(solution)/shard_map/ppermute | solution.py:416
  12.3 3.5 %collective-permute-start.2 = (f32[9,8,128]{2,1,0:T(8,128)S(1)}, f32[9,8,128]{2,1,0:T(8,128)S(1)}, u32[]{:S(2)}, u32[]{:S(2)}) collective-permute-start(f32[9,8,128]{2,1,0:T(8,128)S(1)} %copy-done.5), channel_id=1, source_target_pairs={{0,1},{1,0},{2,3},{3,2},{4,5},{5,4},{6,7},{7,6},{8,9},{9,8},{10,11... | collective-permute-start | bytes 110600 | tf_op jit(solution)/shard_map/ppermute | solution.py:411

commit v3 on v2

v3 whole, which is shorter than its diff:
```python
import jax
import jax.numpy as jnp
from jax import lax
from jax.experimental import pallas as pl
from jax.experimental.pallas import tpu as pltpu
from jax.sharding import PartitionSpec as P

F32 = jnp.float32
VMEM_LIMIT = 12 << 20
CHUNKS = 2
OUT_CHUNKS = 4


def up(value, unit):
    return -(-value // unit) * unit


class Sizes:
    def __init__(self, mixing, halves, tiles):
        self.species, _, _, self.rows, self.width = mixing.shape
        self.tiles, self.halves = tiles, halves
        self.part = self.width // halves
        self.group = up(2 * self.species, 8)
        self.flux = 3 * self.group
        self.flux2 = self.flux + 8
        self.lanes = up(self.flux2 + 8, 128)
        self.vregs = self.lanes // 128
        self.dp_at = 2 * self.flux
        self.fy_at = self.dp_at + 8
        self.extra = self.fy_at + 8
        self.sent = self.extra + 8 * self.vregs
        self.per = 128 // self.part
        self.own = up(18, self.per) // self.per
        self.pieces = 21
        self.shared = up(self.pieces, self.per) // self.per


def slots(face_slot):
    return [sum(jnp.where(face_slot[s] == f, s, 0) for s in range(6)) for f in range(6)]


def roll(x, shift, axis):
    shift %= x.shape[axis]
    return pltpu.roll(x, shift, axis) if shift else x


def reverse8(x):
    row = lax.broadcasted_iota(jnp.int32, x.shape, 0)
    x = jnp.where((row & 1) == 0, roll(x, -1, 0), roll(x, 1, 0))
    x = jnp.where((row & 2) == 0, roll(x, -2, 0), roll(x, 2, 0))
    return roll(x, 4, 0)


def upwind(u, total):
    return 0.5 * jnp.abs(u) * (1.0 - jnp.abs(u / (0.5 * total)))


def wide(x, width):
    return jnp.concatenate([x] * (width // 128), axis=-1) if width > 128 else x


def side_by_side(tiles, per):
    tiles = tiles + [tiles[0]] * (per - len(tiles))
    return jnp.concatenate(tiles, axis=-1) if per > 1 else tiles[0]


def pack_kernel(
    z, slot_in, mixing_in, dp_in, fx_in, fy_in,
    to_a, to_b, out, edges, own, order, face_slot, mixing, fluxes, sems,
):
    cuts = [z.species * n // CHUNKS for n in range(CHUNKS + 1)]
    copies = [pltpu.make_async_copy(slot_in, face_slot, sems.at[0])]
    for c, ref in enumerate((dp_in, fx_in, fy_in)):
        copies.append(pltpu.make_async_copy(ref, fluxes.at[c], sems.at[1 + c]))
    for n in range(CHUNKS):
        some = pl.ds(cuts[n], cuts[n + 1] - cuts[n])
        copies.append(pltpu.make_async_copy(mixing_in.at[some], mixing.at[some], sems.at[4 + n]))
    for copy in copies:
        copy.start()
    place = lax.axis_index("tile")
    half = lax.axis_index("spec")
    copies[0].wait()
    slot = slots(face_slot)
    even = lax.rem(place, 2) == 0
    first, last = place == 0, place == z.tiles - 1
    width, part, species, n_half = z.width, z.part, z.species, z.halves
    lane = lax.broadcasted_iota(jnp.int32, (8, 128), 1)
    order[...] = sum(jnp.where(lane == f, slot[f], 0) for f in range(6))
    for copy in copies[1:4]:
        copy.wait()
    raw = [[fluxes[c, 0, slot[f]] for f in range(6)] for c in range(3)]
    flat = [raw[c][f] for c in range(3) for f in range(6)]
    for n in range(z.own):
        own[n] = side_by_side(flat[n * z.per : (n + 1) * z.per], z.per)

    def both(low, high, at):
        to_a[pl.ds(at, low.shape[0])] = jnp.where(even, high, low)
        to_b[pl.ds(at, low.shape[0])] = jnp.where(even, low, high)

    def padded(x):
        return jnp.concatenate([x, jnp.zeros((8, width - part), F32)], axis=-1) if width > part else x

    pad = jnp.zeros((2, part), F32)
    low_dp = jnp.concatenate([x[0:1] for x in raw[0]] + [pad], axis=0)
    high_dp = jnp.concatenate([x[7:8] for x in raw[0]] + [pad], axis=0)
    low_fy = padded(jnp.concatenate([x[0:1] for x in raw[2]] + [pad], axis=0))
    both(padded(low_dp), padded(high_dp), z.dp_at)
    both(low_fy, low_fy, z.fy_at)

    columns = [[jnp.zeros((8, 128), F32) for _ in range(z.vregs)] for _ in range(2)]
    for parity in range(2):
        for a in range(3):
            f = 2 * a + parity
            if z.group > 2 * species:
                zero = jnp.zeros((z.group - 2 * species, width), F32)
                both(zero, zero, parity * z.flux + a * z.group + 2 * species)
            for c in range(2):
                at = z.flux2 + 3 * c + a
                edge = side_by_side([raw[c][f]] * z.per, z.per)
                moved = roll(edge, at - (0 if parity == 0 else 127), 1)
                k = at // 128
                columns[parity][k] = jnp.where(lane == at % 128, moved, columns[parity][k])
    for n in range(CHUNKS):
        copies[4 + n].wait()
        for s in range(cuts[n], cuts[n + 1]):
            for f in range(6):
                a, parity = f // 2, f % 2
                tile = mixing[s, 0, slot[f]]
                at = a * z.group + 2 * s
                both(tile[0:2], tile[6:8], parity * z.flux + at)
                edge = tile[:, :128] if parity == 0 else tile[:, width - 128 :]
                moved = roll(edge, at - (0 if parity == 0 else 126), 1)
                k = at // 128
                columns[parity][k] = jnp.where((lane >> 1) == (at % 128) // 2, moved, columns[parity][k])
    turned = [[reverse8(x) for x in lanes] for lanes in columns]
    for k in range(z.vregs):
        for parity in range(2):
            edges[parity, :, k * 128 : (k + 1) * 128] = columns[parity][k]
        spare = wide(jnp.where(first, turned[0][k], turned[1][k]), width)
        to_a[pl.ds(z.extra + 8 * k, 8)] = spare
        to_b[pl.ds(z.extra + 8 * k, 8)] = spare

    ends = ((0, turned[1]), (z.tiles - 1, turned[0]))

    @pl.when(first | last)
    def _():
        rows, dps, fys = [], [], []
        for a in range(3):
            for_odd, for_even = (a + 1) % 3, (a + 2) % 3
            start = jnp.where(first, z.flux + for_odd * z.group, for_even * z.group)
            rows.append(to_b[pl.ds(pl.multiple_of(start, 8), z.group)])
            for c, values in ((0, dps), (2, fys)):
                values.append(jnp.where(first, raw[c][2 * for_odd + 1][0:1], raw[c][2 * for_even][7:8]))
        flux = jnp.concatenate(dps + fys + [pad], axis=0)
        flux = jnp.concatenate([jnp.where(half == n, flux, 0.0) for n in range(n_half)], axis=-1)
        rows += [flux, jnp.zeros((z.lanes - z.flux - 8, width), F32)]
        messages = jnp.concatenate(rows, axis=0).T
        for t in range(z.tiles):
            at = 8 * (z.tiles - 1 - t)
            for n in range(n_half):
                out[t * n_half + n] = messages[at : at + 8]
        for t, cols in ends:
            at = 8 * (z.tiles - 1 - t)
            k = z.flux2 // 128
            here = (lane >= z.flux2 % 128) & (lane < z.flux2 % 128 + 8)
            mixed = jnp.where(here, cols[k], messages[at : at + 8, k * 128 : (k + 1) * 128])
            for n in range(n_half):
                out[t * n_half + n, :, k * 128 : (k + 1) * 128] = mixed

    @pl.when(jnp.logical_not(first | last))
    def _():
        for t, cols in ends:
            for n in range(n_half):
                for k in range(z.vregs):
                    out[t * n_half + n, :, k * 128 : (k + 1) * 128] = cols[k]


def share_kernel(z, own, from_a, from_b, out):
    even = lax.rem(lax.axis_index("tile"), 2) == 0
    part = z.part
    dp_a, dp_b = from_a[z.dp_at : z.dp_at + 8, :part], from_b[z.dp_at : z.dp_at + 8, :part]
    fy_a, fy_b = from_a[z.fy_at : z.fy_at + 8, :part], from_b[z.fy_at : z.fy_at + 8, :part]
    halo = [jnp.where(even, dp_b, dp_a), jnp.where(even, dp_a, dp_b), jnp.where(even, fy_a, fy_b)]
    flat = [own[n // z.per][:, (n % z.per) * part : (n % z.per + 1) * part] for n in range(18)] + halo
    for n in range(z.shared):
        out[n] = side_by_side(flat[n * z.per : (n + 1) * z.per], z.per)


def interior_kernel(
    z, order_in, mixing, from_a, from_b, mine, others, partial, ends, aux,
    order, south, north, coef, order_sem,
):
    fetch = pltpu.make_async_copy(order_in, order, order_sem)
    fetch.start()
    place = lax.axis_index("tile")
    half = lax.axis_index("spec")
    even = lax.rem(place, 2) == 0
    first, last = place == 0, place == z.tiles - 1
    width, part, species = z.width, z.part, z.species
    lane = lax.broadcasted_iota(jnp.int32, (8, width), 1)
    row = lax.broadcasted_iota(jnp.int32, (8, width), 0)
    lane1 = lax.broadcasted_iota(jnp.int32, (8, 128), 1)

    a_rows, b_rows = from_a[0 : z.dp_at], from_b[0 : z.dp_at]
    south[...] = jnp.where(even, b_rows, a_rows)
    north[...] = jnp.where(even, a_rows, b_rows)

    full = []
    for n in range(z.pieces):
        cut = slice((n % z.per) * part, (n % z.per + 1) * part)
        if z.halves == 2:
            x, y = mine[n // z.per][:, cut], others[n // z.per][:, cut]
            parts = [jnp.where(half == 0, x, y), jnp.where(half == 0, y, x)]
        else:
            parts = [others[h, n // z.per][:, cut] for h in range(z.halves)]
        full.append(jnp.concatenate(parts, axis=-1))
    dp_south, dp_north, fy_north = full[18:]

    def left(x, ghost, n):
        return pltpu.roll(jnp.where(lane >= width - n, ghost, x), n, 1)

    def right(x, ghost, n):
        return pltpu.roll(jnp.where(lane < n, ghost, x), width - n, 1)

    def below(x, ghost, n):
        return pltpu.roll(jnp.where(row >= 8 - n, ghost, x), n, 0)

    def above(x, ghost, n):
        return pltpu.roll(jnp.where(row < n, ghost, x), 8 - n, 0)

    for f in range(6):
        parity = f % 2
        dp, fx, fy = full[f], full[6 + f], full[12 + f]
        if parity == 0:
            west, east, east_u = dp, full[f + 1], full[6 + f + 1]
            s_end, n_end, v_end = roll(dp_south, 7 - (f - 1) % 6, 0), dp, 0.0
            known = jnp.logical_not(last & (row == 7))
        else:
            west, east, east_u = full[f - 1], dp, 0.0
            s_end, n_end, v_end = dp, roll(dp_north, -((f + 1) % 6), 0), roll(fy_north, -((f + 1) % 6), 0)
            known = lane < width - 1
        dp_w, dp_e = left(dp, west, 1), right(dp, east, 1)
        u0, u1 = fx, right(fx, east_u, 1)
        dp_s = below(dp, jnp.where(first, s_end, roll(dp_south, 7 - f, 0)), 1)
        dp_n = above(dp, jnp.where(last, n_end, roll(dp_north, -f, 0)), 1)
        v0, v1 = fy, above(fy, jnp.where(last, v_end, roll(fy_north, -f, 0)), 1)
        new = dp - (u1 - u0) - (v1 - v0)
        inverse = jnp.where(known, 1.0 / jnp.where(known, new, 1.0), 1.0)
        for n, x in enumerate((fx, dp, inverse, new, v0, v1)):
            aux[f, n] = x
        center = dp
        for n, (w0, w1, d0, d1) in enumerate(((u0, u1, dp_w, dp_e), (v0, v1, dp_s, dp_n))):
            b0, b1 = upwind(w0, d0 + dp), upwind(w1, dp + d1)
            if n == 0 and parity == 0:
                b0 = jnp.where(lane == 0, 0.0, b0)
            if n == 1 and parity == 1:
                b0 = jnp.where(first & (row == 0), 0.0, b0)
            p0, p1 = w0 * (1.0 / 12.0), w1 * (1.0 / 12.0)
            coef[f, 4 * n] = -p0 * inverse
            coef[f, 4 * n + 1] = (7.0 * p0 + b0 + p1) * inverse
            coef[f, 4 * n + 2] = (-p0 - 7.0 * p1 + b1) * inverse
            coef[f, 4 * n + 3] = p1 * inverse
            center = center + (7.0 * p0 - b0) - (7.0 * p1 + b1)
        coef[f, 8] = center * inverse

    block = z.flux
    south_at, north_at = jnp.where(first, block, 0), jnp.where(last, 0, block)
    fetch.wait()
    slot = [order[0, f] for f in range(6)]

    def quad(it, count):
        for a in range(3):
            a_s, a_n = jnp.where(first, (a + 2) % 3, a), jnp.where(last, (a + 1) % 3, a)

            def ghosts(ref, at, ref_a):
                return ref[pl.ds(pl.multiple_of(at + ref_a * z.group + 8 * it, 8), 8)]

            south_rows = [ghosts(south, south_at, a_s), jnp.where(first, 0.0, ghosts(south, block, a))]
            north_rows = [jnp.where(last, 0.0, ghosts(north, 0, a)), ghosts(north, north_at, a_n)]
            fe, fo = 2 * a, 2 * a + 1
            ce = [coef[fe, n] for n in range(9)]
            co = [coef[fo, n] for n in range(9)]
            for u in range(count):
                s = 4 * it + u
                qe, qo = mixing[s, 0, slot[fe]], mixing[s, 0, slot[fo]]
                for q, west, east, c, parity, f in ((qe, 0.0, qo, ce, 0, fe), (qo, qe, 0.0, co, 1, fo)):
                    sv = roll(south_rows[parity], 6 - 2 * u, 0)
                    nv = roll(north_rows[parity], -2 * u, 0)
                    value = c[8] * q
                    value += c[0] * left(q, west, 2)
                    value += c[1] * left(q, west, 1)
                    value += c[2] * right(q, east, 1)
                    value += c[3] * right(q, east, 2)
                    value += c[4] * below(q, sv, 2)
                    value += c[5] * below(q, sv, 1)
                    value += c[6] * above(q, nv, 1)
                    value += c[7] * above(q, nv, 2)
                    partial[s, f] = value

    @pl.loop(0, species // 4)
    def _(it):
        quad(it, 4)

    if species % 4:
        quad(species // 4, species % 4)

    lanes = [[jnp.zeros((8, 128), F32) for _ in range(z.vregs)] for _ in range(2)]
    for s in range(species):
        for f in range(6):
            a, parity = f // 2, f % 2
            at = a * z.group + 2 * s
            cut = slice(0, 128) if parity == 0 else slice(width - 128, width)
            moved = roll(partial[s, f, :, cut], at - (0 if parity == 0 else 126), 1)
            k = at // 128
            lanes[parity][k] = jnp.where((lane1 >> 1) == (at % 128) // 2, moved, lanes[parity][k])
    for parity in range(2):
        for k in range(z.vregs):
            ends[parity, :, k * 128 : (k + 1) * 128] = lanes[parity][k]


def finish_kernel(
    z, order_in, mixing, from_b, partial, ends, aux, edges, arrived, out,
    order, turned, fixed, result, order_sem, out_sem,
):
    fetch = pltpu.make_async_copy(order_in, order, order_sem)
    fetch.start()
    place = lax.axis_index("tile")
    half = lax.axis_index("spec")
    first, last = place == 0, place == z.tiles - 1
    width, part, species, n_half = z.width, z.part, z.species, z.halves
    lane = lax.broadcasted_iota(jnp.int32, (8, width), 1)
    row = lax.broadcasted_iota(jnp.int32, (8, width), 0)
    lane1 = lax.broadcasted_iota(jnp.int32, (8, 128), 1)
    twelfth = 1.0 / 12.0
    holder = lax.div(width - 8 - 8 * place, part)

    def column(x, at):
        return x[:, at : at + 1]

    def spread(values, k):
        at = lane1 + k * 128
        return jnp.where(at < z.group, values[0], jnp.where(at < 2 * z.group, values[1], values[2]))

    last_column = []
    odd_end = (lane1 & 1) == 1
    for parity in range(2):
        end = z.tiles - 1 if parity == 0 else 0
        flux = reverse8(arrived[end * n_half + holder, :, (z.flux // 128) * 128 : (z.flux // 128 + 1) * 128])
        mul = []
        for a in range(3):
            f = 2 * a + parity
            fx, dp, inverse, new = (aux[f, n] for n in range(4))
            ghost_dp = column(flux, z.flux % 128 + a)
            if parity == 0:
                u0, p1 = column(fx, 0), column(fx, 1) * twelfth
                p0, b0 = u0 * twelfth, upwind(u0, ghost_dp + column(dp, 0))
                i0, i1 = column(inverse, 0), column(inverse, 1)
                mul.append((-p0 * i0, -p1 * i1, (7.0 * p0 + b0 + p1) * i0, -b0 * i0))
            else:
                u1 = column(flux, z.flux % 128 + 3 + a)
                p1, b1 = u1 * twelfth, upwind(u1, column(dp, width - 1) + ghost_dp)
                p0 = column(fx, width - 1) * twelfth
                i1 = 1.0 / (column(new, width - 1) - u1)
                last_column.append(i1)
                mul.append(
                    (p0 * column(inverse, width - 2), p1 * i1, (b1 - 7.0 * p1 - p0) * i1, -(7.0 * p1 + b1) * i1, p1 * i1, i1)
                )
        for k in range(z.vregs):
            cut = slice(k * 128, (k + 1) * 128)
            g = reverse8(arrived[end * n_half + half, :, cut])
            own, q = ends[parity, :, cut], edges[parity, :, cut]
            m = [spread([mul[a][n] for a in range(3)], k) for n in range(len(mul[0]))]
            if parity == 0:
                value = own + jnp.where(odd_end, m[1], m[0]) * g
                value += jnp.where(odd_end, 0.0, m[2] * roll(g, -1, 1) + m[3] * q)
            else:
                value = own * jnp.where(odd_end, m[5], 1.0) + jnp.where(odd_end, m[1], m[0]) * g
                value += jnp.where(odd_end, m[2] * roll(g, 1, 1) + m[3] * q + m[4] * roll(q, 1, 1), 0.0)
            fixed[parity, :, cut] = value

    cuts = [species * n // OUT_CHUNKS for n in range(OUT_CHUNKS + 1)]

    def store(n, special):
        for f in range(6):
            a, parity = f // 2, f % 2
            extra = special(a, parity) if special else None
            for s in range(cuts[n], cuts[n + 1]):
                at = a * z.group + 2 * s
                value = partial[s, f]
                end = fixed[parity, :, (at // 128) * 128 : (at // 128 + 1) * 128]
                end = wide(roll(end, -at if parity == 0 else 126 - at, 1), width)
                value = jnp.where(lane < 2 if parity == 0 else lane >= width - 2, end, value)
                if extra is not None:
                    value = extra(value, s, f)
                result[f, s] = value

    def send(n):
        some = pl.ds(cuts[n], cuts[n + 1] - cuts[n])
        for f in range(6):
            pltpu.make_async_copy(result.at[f, some], out.at[some, 0, order[0, f]], out_sem).start()

    def everything(special=None):
        for n in range(OUT_CHUNKS):
            store(n, special)
            send(n)

    def gather():
        holder = jnp.where(first, n_half - 1, 0)
        pieces = []
        for k in range(z.vregs):
            cut = slice(k * 128, (k + 1) * 128)
            spare = from_b[z.extra + 8 * k : z.extra + 8 * k + 8, 0:128]
            mine = reverse8(jnp.where(first, edges[1, :, cut], edges[0, :, cut]))
            parts = []
            for t in reversed(range(z.tiles)):
                if t == 0:
                    x = jnp.where(first, mine, spare)
                elif t == z.tiles - 1:
                    x = jnp.where(first, spare, mine)
                else:
                    x = arrived[t * n_half + half, :, cut]
                if (k + 1) * 128 > z.flux:
                    x = jnp.where(lane1 + k * 128 < z.flux, x, arrived[t * n_half + holder, :, cut])
                parts.append(x)
            pieces.append(jnp.concatenate(parts, axis=0).T)
        turned[...] = jnp.concatenate(pieces, axis=0) if len(pieces) > 1 else pieces[0]
        return turned[z.flux2 : z.flux2 + 8]

    fetch.wait()

    @pl.when(first)
    def _():
        flux = gather()

        def special(a, parity):
            if parity == 0:
                return None
            f, source = 2 * a + 1, (a + 2) % 3
            dp, inverse, v0, v1 = aux[f, 1], aux[f, 2], aux[f, 4], aux[f, 5]
            inverse = jnp.where(lane == width - 1, last_column[a], inverse)
            ghost_dp = flux[source : source + 1]
            p0, p1, b0 = v0 * twelfth, v1 * twelfth, upwind(v0, ghost_dp + dp)
            zero = jnp.zeros_like(dp)
            on0, on1 = row == 0, row < 2
            two = jnp.where(on1, -p0 * inverse, zero)
            one = jnp.where(on0, (7.0 * p0 + b0 + p1) * inverse, zero)
            none = jnp.where(on0, -b0 * inverse, zero)

            def extra(value, s, f):
                rows = turned[source * z.group + 8 * (s // 4) : source * z.group + 8 * (s // 4) + 8]
                u = s % 4
                q = mixing[s, 0, order[0, f]]
                return value + two * roll(rows, -2 * u, 0) + one * roll(rows, -2 * u - 1, 0) + none * q

            return extra

        everything(special)

    @pl.when(last)
    def _():
        flux = gather()

        def special(a, parity):
            if parity == 1:
                return None
            f, source = 2 * a, (a + 1) % 3
            dp, inverse, new, v0 = (aux[f, n] for n in (1, 2, 3, 4))
            ghost_dp, v1 = flux[source : source + 1], flux[3 + source : 4 + source]
            on7, on6 = row == 7, row >= 6
            inverse = jnp.where(on7, 1.0 / jnp.where(on7, new - v1, 1.0), inverse)
            zero = jnp.zeros_like(dp)
            p0, p1, b1 = v0 * twelfth, v1 * twelfth, upwind(v1, dp + ghost_dp)
            two = jnp.where(on7, p1 * inverse, jnp.where(on6, roll(p0, -1, 0) * inverse, zero))
            one = jnp.where(on7, (b1 - 7.0 * p1 - p0) * inverse, zero)
            none = jnp.where(on7, -(7.0 * p1 + b1) * inverse, zero)
            back = jnp.where(on7, p1 * inverse, zero)
            scale = jnp.where(on7, inverse, 1.0)

            def extra(value, s, f):
                rows = turned[source * z.group + 8 * (s // 4) : source * z.group + 8 * (s // 4) + 8]
                u = s % 4
                q = mixing[s, 0, order[0, f]]
                value = value * scale + two * roll(rows, 6 - 2 * u, 0) + one * roll(rows, 7 - 2 * u, 0)
                return value + none * q + back * roll(q, 1, 0)

            return extra

        everything(special)

    @pl.when(jnp.logical_not(first | last))
    def _():
        everything()

    for f in range(6):
        pltpu.make_async_copy(result.at[f], out.at[:, 0, order[0, f]], out_sem).wait()


def local(mixing, layer_mass, mass_east, mass_north, face_slot):
    tiles = lax.axis_size("tile")
    halves = lax.axis_size("spec")
    z = Sizes(mixing, halves, tiles)
    assert z.rows == 8 and mixing.shape[1] == 1 and tiles > 2 and tiles % 2 == 0
    assert z.width == 8 * tiles and z.width % 128 == 0 and 128 % z.part == 0
    vmem = pl.BlockSpec(memory_space=pltpu.VMEM)
    hbm = pl.BlockSpec(memory_space=pl.ANY)
    params = pltpu.CompilerParams(vmem_limit_bytes=VMEM_LIMIT)
    cells = (z.species, 6, 8, z.width)

    def f32(*shape):
        return jax.ShapeDtypeStruct(shape, F32)

    to_a, to_b, messages, edges, own, order = pl.pallas_call(
        lambda *refs: pack_kernel(z, *refs),
        out_shape=(
            f32(z.sent, z.width),
            f32(z.sent, z.width),
            f32(tiles * halves, 8, z.lanes),
            f32(2, 8, z.lanes),
            f32(z.own, 8, 128),
            jax.ShapeDtypeStruct((8, 128), jnp.int32),
        ),
        in_specs=[hbm] * 5,
        out_specs=[vmem] * 6,
        scratch_shapes=[
            pltpu.SMEM((6,), jnp.int32),
            pltpu.VMEM(mixing.shape, F32),
            pltpu.VMEM((3,) + layer_mass.shape, F32),
            pltpu.SemaphoreType.DMA((4 + CHUNKS,)),
        ],
        name="pack",
    )(face_slot, mixing, layer_mass, mass_east, mass_north)
    arrived = lax.all_to_all(messages, ("tile", "spec"), 0, 0, tiled=True)
    from_a = lax.ppermute(to_a, "tile", [(i, i ^ 1) for i in range(tiles)])
    pairs = [(i, (i + 1) % tiles) if i % 2 else (i, (i - 1) % tiles) for i in range(tiles)]
    from_b = lax.ppermute(to_b, "tile", pairs)
    mine = pl.pallas_call(
        lambda *refs: share_kernel(z, *refs),
        out_shape=f32(z.shared, 8, 128),
        in_specs=[vmem] * 3,
        out_specs=vmem,
        compiler_params=params,
        cost_estimate=pl.CostEstimate(flops=23 * 10**9, bytes_accessed=0, transcendentals=0),
        name="share",
    )(own, from_a, from_b)
    if halves == 2:
        others = lax.ppermute(mine, "spec", [(0, 1), (1, 0)])
    else:
        others = lax.all_gather(mine, "spec", axis=0, tiled=False)
    partial, ends, aux = pl.pallas_call(
        lambda *refs: interior_kernel(z, *refs),
        out_shape=(f32(*cells), f32(2, 8, z.lanes), f32(6, 6, 8, z.width)),
        in_specs=[vmem] * 6,
        out_specs=[vmem] * 3,
        scratch_shapes=[
            pltpu.SMEM((8, 128), jnp.int32),
            pltpu.VMEM((2 * z.flux, z.width), F32),
            pltpu.VMEM((2 * z.flux, z.width), F32),
            pltpu.VMEM((6, 9, 8, z.width), F32),
            pltpu.SemaphoreType.DMA,
        ],
        compiler_params=params,
        name="interior",
    )(order, mixing, from_a, from_b, mine, others)
    return pl.pallas_call(
        lambda *refs: finish_kernel(z, *refs),
        out_shape=f32(*mixing.shape),
        in_specs=[vmem] * 8,
        out_specs=hbm,
        scratch_shapes=[
            pltpu.SMEM((8, 128), jnp.int32),
            pltpu.VMEM((z.lanes, z.width), F32),
            pltpu.VMEM((2, 8, z.lanes), F32),
            pltpu.VMEM((6, z.species, 8, z.width), F32),
            pltpu.SemaphoreType.DMA,
            pltpu.SemaphoreType.DMA,
        ],
        compiler_params=params,
        name="finish",
    )(order, mixing, from_b, partial, ends, aux, edges, arrived)


def solution(mesh):
    flux = P(None, None, "tile", "spec")
    cells = P("spec", None, None, "tile", None)
    return jax.shard_map(
        local,
        mesh=mesh,
        in_specs=(cells, flux, flux, flux, P()),
        out_specs=cells,
        check_vma=False,
    )
```

time: 26.6 us -> 23.4 us (0.88)
  the two profiles are of different devices: /device:TPU:1 before, /device:TPU:0 now
where the time goes in v3:
time: 23.4 us; the launch traced here: 23.2 us
  starting transfers between devices  9.83 us (42%)
  Pallas kernels  6.83 us (29%)
  waiting for transfers between devices  6.44 us (28%)
    ppermute x1, starting transfers between devices, local(): from_b = lax.ppermute(to_b, 'tile', pairs)  5.48 us
    ppermute x1, waiting for transfers between devices, local(): others = lax.ppermute(mine, 'spec', [(0, 1), (1, 0)])  2.74 us
    all_to_all x1, starting transfers between devices, local(): arrived = lax.all_to_all(messages, ('tile', 'spec'), 0, 0, tiled=True)  2.72 us
    pallas_call x1, Pallas kernels, local(): pl.pallas_call(lambda *refs: pack_kernel(z, *refs), out_shape=(f32(z.sent...  2.52 us
    pallas_call x1, Pallas kernels, local(): pl.pallas_call(lambda *refs: interior_kernel(z, *refs), out_shape=(f32(*c...  2.51 us
    all_to_all x1, waiting for transfers between devices, local(): arrived = lax.all_to_all(messages, ('tile', 'spec'), 0, 0, tiled=True)  2.04 us
    pallas_call x1, Pallas kernels, local(): pl.pallas_call(lambda *refs: finish_kernel(z, *refs), out_shape=f32(*mixi...  1.71 us
    ppermute x1, waiting for transfers between devices, local(): from_b = lax.ppermute(to_b, 'tile', pairs)  1.65 us
  transfers between devices with their start and end apart: 4, of which 3 were waited for; matrix products, arithmetic and copies ran while one was open for 0% of the time, Pallas kernels for 11%

profile of v3, /device:TPU:0, one launch (start us, length us, event | category | flops | bytes accessed | tf_op | source)
XLA Modules:
  0.0 23.2 jit_solution(6329290293255156346)
XLA Ops:
  0.0 2.5 %pack.1 = (f32[464,128]{1,0:T(8,128)}, f32[464,128]{1,0:T(8,128)}, f32[32,8,256]{2,1,0:T(8,128)}, f32[2,8,256]{2,1,0:T(8,128)}, f32[9,8,128]{2,1,0:T(8,128)}, /*index=5*/s32[8,128]{1,0:T(8,128)}) custom-call(s32[6]{0:T(128)} %refs_0_.1, f32[36,1,6,8,128]{4,3,2,1,0:T(8,128)} %refs_1_.5, f32[1,6,8,64]{3,2,1,0:T(8,128)} %refs_2_.1, f32[1,6,8,64]{3,2,1,0:T(8,128)} %refs_3_.1, ...), custom_call_target="tpu_custom_call" | custom-call | tf_op jit(solution)/shard_map/pack/pallas_call | solution.py:512
  2.5 5.5 %collective-permute-start = (f32[464,128]{1,0:T(8,128)}, f32[464,128]{1,0:T(8,128)S(1)}, u32[]{:S(2)}, u32[]{:S(2)}) collective-permute-start(f32[464,128]{1,0:T(8,128)} %get-tuple-element.15), channel_id=1, source_target_pairs={{0,30},{2,4},{4,2},{6,8},{8,6},{10,12},{12,10},{14,16},{16,14},{18... | collective-permute-start | bytes 712712 | tf_op jit(solution)/shard_map/ppermute | solution.py:535
  8.0 0.0 collective-permute-start.1
  8.0 0.0 copy-start.3
  8.0 2.7 %all-to-all-start = ((f32[32,8,256]{2,1,0:T(8,128)}), f32[32,8,256]{2,1,0:T(8,128)S(1)}, u32[]{:S(2)}, u32[]{:S(2)}) async-start(f32[32,8,256]{2,1,0:T(8,128)} %get-tuple-element.22), calls=%async_computation | async-start | bytes 524288 | tf_op jit(solution)/shard_map/all_to_all | solution.py:532
  10.7 1.6 %collective-permute-done.refs_2_.refs_3_ = f32[464,128]{1,0:T(8,128)S(1)} collective-permute-done((f32[464,128]{1,0:T(8,128)}, f32[464,128]{1,0:T(8,128)S(1)}, u32[]{:S(2)}, u32[]{:S(2)}) %collective-permute-start) | collective-permute-done | bytes 237600 | tf_op jit(solution)/shard_map/ppermute | solution.py:535
  12.4 0.0 collective-permute-done.1.refs_1_.refs_2_
  12.4 0.0 copy-done.3
  12.4 0.0 copy-start
  12.4 0.0 copy-start.2
  12.4 0.1 share.1.refs_4_
  12.5 1.6 %collective-permute-start.2 = (f32[11,8,128]{2,1,0:T(8,128)S(1)}, f32[11,8,128]{2,1,0:T(8,128)S(1)}, u32[]{:S(2)}, u32[]{:S(2)}) collective-permute-start(f32[11,8,128]{2,1,0:T(8,128)S(1)} %share.1.refs_4_), channel_id=1, source_target_pairs={{0,1},{1,0},{2,3},{3,2},{4,5},{5,4},{6,7},{7,6},{8,9},{9,8},{10,11... | collective-permute-start | bytes 135176 | tf_op jit(solution)/shard_map/ppermute | solution.py:546
  14.1 2.7 %collective-permute-done.2.refs_5_ = f32[11,8,128]{2,1,0:T(8,128)S(1)} collective-permute-done((f32[11,8,128]{2,1,0:T(8,128)S(1)}, f32[11,8,128]{2,1,0:T(8,128)S(1)}, u32[]{:S(2)}, u32[]{:S(2)}) %collective-permute-start.2) | collective-permute-done | bytes 45088 | tf_op jit(solution)/shard_map/ppermute | solution.py:546
  16.9 0.0 copy-done
  16.9 0.0 copy-done.2
  16.9 0.0 copy-start.1
  16.9 2.5 %interior.1 = (f32[36,6,8,128]{3,2,1,0:T(8,128)S(1)}, f32[2,8,256]{2,1,0:T(8,128)S(1)}, f32[6,6,8,128]{3,2,1,0:T(8,128)S(1)}) custom-call(s32[8,128]{1,0:T(8,128)S(1)} %copy-done.2, f32[36,1,6,8,128]{4,3,2,1,0:T(8,128)S(1)} %copy-done, f32[464,128]{1,0:T(8,128)S(1)} %collective-permute-done.1.refs_1_.refs_2_, ...), custom_call_target="tpu_custom_call" | custom-call | tf_op jit(solution)/shard_map/interior/pallas_call | solution.py:549
  19.4 2.0 %all-to-all-done.refs_7_ = f32[32,8,256]{2,1,0:T(8,128)S(1)} async-done(((f32[32,8,256]{2,1,0:T(8,128)}), f32[32,8,256]{2,1,0:T(8,128)S(1)}, u32[]{:S(2)}, u32[]{:S(2)}) %all-to-all-start) | async-done | bytes 262176 | tf_op jit(solution)/shard_map/all_to_all | solution.py:532
  21.4 0.0 copy-done.1
  21.4 1.7 %finish.1 = f32[36,1,6,8,128]{4,3,2,1,0:T(8,128)} custom-call(s32[8,128]{1,0:T(8,128)S(1)} %copy-done.2, f32[36,1,6,8,128]{4,3,2,1,0:T(8,128)S(1)} %copy-done, f32[464,128]{1,0:T(8,128)S(1)} %collective-permute-done.refs_2_.refs_3_, f32[36,6,8,128]{3,2,1,0:T(8,128)S(1)} %get-tuple-element.18.refs_3_, f32[2,8,256]{2,1,0:T(8,128)S(1)} %get-tuple-element.19.refs_4_, ...), custom_call_target="tpu_custom_call" | custom-call | tf_op jit(solution)/shard_map/finish/pallas_call | solution.py:564
Async XLA Ops:
  2.5 9.9 %collective-permute-start = (f32[464,128]{1,0:T(8,128)}, f32[464,128]{1,0:T(8,128)S(1)}, u32[]{:S(2)}, u32[]{:S(2)}) collective-permute-start(f32[464,128]{1,0:T(8,128)} %get-tuple-element.15), channel_id=1, source_target_pairs={{0,30},{2,4},{4,2},{6,8},{8,6},{10,12},{12,10},{14,16},{16,14},{18... | collective-permute-start | bytes 712712 | tf_op jit(solution)/shard_map/ppermute | solution.py:535
  8.0 4.4 %collective-permute-start.1 = (f32[464,128]{1,0:T(8,128)}, f32[464,128]{1,0:T(8,128)S(1)}, u32[]{:S(2)}, u32[]{:S(2)}) collective-permute-start(f32[464,128]{1,0:T(8,128)} %get-tuple-element.16), channel_id=1, source_target_pairs={{0,2},{2,0},{4,6},{6,4},{8,10},{10,8},{12,14},{14,12},{16,18},{18,... | collective-permute-start | bytes 712712 | tf_op jit(solution)/shard_map/ppermute | solution.py:533
  8.0 4.4 %copy-start.3 = (f32[9,8,128]{2,1,0:T(8,128)S(1)}, f32[9,8,128]{2,1,0:T(8,128)}, u32[]{:S(2)}) copy-start(f32[9,8,128]{2,1,0:T(8,128)} %get-tuple-element.17.refs_0_) | copy-start | bytes 110596
  8.0 13.4 %all-to-all-start = ((f32[32,8,256]{2,1,0:T(8,128)}), f32[32,8,256]{2,1,0:T(8,128)S(1)}, u32[]{:S(2)}, u32[]{:S(2)}) async-start(f32[32,8,256]{2,1,0:T(8,128)} %get-tuple-element.22), calls=%async_computation | async-start | bytes 524288 | tf_op jit(solution)/shard_map/all_to_all | solution.py:532
  12.4 4.5 %copy-start = (f32[36,1,6,8,128]{4,3,2,1,0:T(8,128)S(1)}, f32[36,1,6,8,128]{4,3,2,1,0:T(8,128)}, u32[]{:S(2)}) copy-start(f32[36,1,6,8,128]{4,3,2,1,0:T(8,128)} %refs_1_.5) | copy-start | bytes 2654212
  12.4 4.5 %copy-start.2 = (s32[8,128]{1,0:T(8,128)S(1)}, s32[8,128]{1,0:T(8,128)}, u32[]{:S(2)}) copy-start(s32[8,128]{1,0:T(8,128)} %get-tuple-element.14.refs_0_) | copy-start | bytes 12292
  12.5 4.4 %collective-permute-start.2 = (f32[11,8,128]{2,1,0:T(8,128)S(1)}, f32[11,8,128]{2,1,0:T(8,128)S(1)}, u32[]{:S(2)}, u32[]{:S(2)}) collective-permute-start(f32[11,8,128]{2,1,0:T(8,128)S(1)} %share.1.refs_4_), channel_id=1, source_target_pairs={{0,1},{1,0},{2,3},{3,2},{4,5},{5,4},{6,7},{7,6},{8,9},{9,8},{10,11... | collective-permute-start | bytes 135176 | tf_op jit(solution)/shard_map/ppermute | solution.py:546
  16.9 4.6 %copy-start.1 = (f32[2,8,256]{2,1,0:T(8,128)S(1)}, f32[2,8,256]{2,1,0:T(8,128)}, u32[]{:S(2)}) copy-start(f32[2,8,256]{2,1,0:T(8,128)} %get-tuple-element.21.refs_6_) | copy-start | bytes 49156

commit v4 on v3

--- a/solution.py
+++ b/solution.py
@@ -66,7 +66,8 @@
 
 def pack_kernel(
     z, slot_in, mixing_in, dp_in, fx_in, fy_in,
-    to_a, to_b, out, edges, own, order, face_slot, mixing, fluxes, sems,
+    to_a_out, to_b_out, out_out, edges_out, own_out, order_out,
+    to_a, to_b, out, edges, own, order, face_slot, mixing, fluxes, sems, out_sems,
 ):
     cuts = [z.species * n // CHUNKS for n in range(CHUNKS + 1)]
     copies = [pltpu.make_async_copy(slot_in, face_slot, sems.at[0])]
@@ -86,12 +87,20 @@
     width, part, species, n_half = z.width, z.part, z.species, z.halves
     lane = lax.broadcasted_iota(jnp.int32, (8, 128), 1)
     order[...] = sum(jnp.where(lane == f, slot[f], 0) for f in range(6))
+    results = [
+        pltpu.make_async_copy(x, y, out_sems.at[n])
+        for n, (x, y) in enumerate(
+            ((to_a, to_a_out), (to_b, to_b_out), (edges, edges_out), (own, own_out), (order, order_out))
+        )
+    ]
+    results[4].start()
     for copy in copies[1:4]:
         copy.wait()
     raw = [[fluxes[c, 0, slot[f]] for f in range(6)] for c in range(3)]
     flat = [raw[c][f] for c in range(3) for f in range(6)]
     for n in range(z.own):
         own[n] = side_by_side(flat[n * z.per : (n + 1) * z.per], z.per)
+    results[3].start()
 
     def both(low, high, at):
         to_a[pl.ds(at, low.shape[0])] = jnp.where(even, high, low)
@@ -139,6 +148,8 @@
         spare = wide(jnp.where(first, turned[0][k], turned[1][k]), width)
         to_a[pl.ds(z.extra + 8 * k, 8)] = spare
         to_b[pl.ds(z.extra + 8 * k, 8)] = spare
+    for n in range(3):
+        results[n].start()
 
     ends = ((0, turned[1]), (z.tiles - 1, turned[0]))
 
@@ -166,6 +177,9 @@
             mixed = jnp.where(here, cols[k], messages[at : at + 8, k * 128 : (k + 1) * 128])
             for n in range(n_half):
                 out[t * n_half + n, :, k * 128 : (k + 1) * 128] = mixed
+        copy = pltpu.make_async_copy(out, out_out, out_sems.at[5])
+        copy.start()
+        copy.wait()
 
     @pl.when(jnp.logical_not(first | last))
     def _():
@@ -173,6 +187,17 @@
             for n in range(n_half):
                 for k in range(z.vregs):
                     out[t * n_half + n, :, k * 128 : (k + 1) * 128] = cols[k]
+        copies = []
+        for t, _ in ends:
+            some = pl.ds(t * n_half, n_half)
+            copies.append(pltpu.make_async_copy(out.at[some], out_out.at[some], out_sems.at[5 + (t > 0)]))
+        for copy in copies:
+            copy.start()
+        for copy in copies:
+            copy.wait()
+
+    for copy in results:
+        copy.wait()
 
 
 def share_kernel(z, own, from_a, from_b, out):
@@ -320,10 +345,8 @@
 
 def finish_kernel(
     z, order_in, mixing, from_b, partial, ends, aux, edges, arrived, out,
-    order, turned, fixed, result, order_sem, out_sem,
+    turned, fixed, result, out_sem,
 ):
-    fetch = pltpu.make_async_copy(order_in, order, order_sem)
-    fetch.start()
     place = lax.axis_index("tile")
     half = lax.axis_index("spec")
     first, last = place == 0, place == z.tiles - 1
@@ -333,6 +356,8 @@
     lane1 = lax.broadcasted_iota(jnp.int32, (8, 128), 1)
     twelfth = 1.0 / 12.0
     holder = lax.div(width - 8 - 8 * place, part)
+    places = order_in[0:1].astype(F32)
+    slot = [jnp.sum(jnp.where(lane1[0:1] == f, places, 0.0)).astype(jnp.int32) for f in range(6)]
 
     def column(x, at):
         return x[:, at : at + 1]
@@ -397,7 +422,7 @@
     def send(n):
         some = pl.ds(cuts[n], cuts[n + 1] - cuts[n])
         for f in range(6):
-            pltpu.make_async_copy(result.at[f, some], out.at[some, 0, order[0, f]], out_sem).start()
+            pltpu.make_async_copy(result.at[f, some], out.at[some, 0, slot[f]], out_sem).start()
 
     def everything(special=None):
         for n in range(OUT_CHUNKS):
@@ -426,8 +451,6 @@
         turned[...] = jnp.concatenate(pieces, axis=0) if len(pieces) > 1 else pieces[0]
         return turned[z.flux2 : z.flux2 + 8]
 
-    fetch.wait()
-
     @pl.when(first)
     def _():
         flux = gather()
@@ -449,7 +472,7 @@
             def extra(value, s, f):
                 rows = turned[source * z.group + 8 * (s // 4) : source * z.group + 8 * (s // 4) + 8]
                 u = s % 4
-                q = mixing[s, 0, order[0, f]]
+                q = mixing[s, 0, slot[f]]
                 return value + two * roll(rows, -2 * u, 0) + one * roll(rows, -2 * u - 1, 0) + none * q
 
             return extra
@@ -479,7 +502,7 @@
             def extra(value, s, f):
                 rows = turned[source * z.group + 8 * (s // 4) : source * z.group + 8 * (s // 4) + 8]
                 u = s % 4
-                q = mixing[s, 0, order[0, f]]
+                q = mixing[s, 0, slot[f]]
                 value = value * scale + two * roll(rows, 6 - 2 * u, 0) + one * roll(rows, 7 - 2 * u, 0)
                 return value + none * q + back * roll(q, 1, 0)
 
@@ -492,7 +515,7 @@
         everything()
 
     for f in range(6):
-        pltpu.make_async_copy(result.at[f], out.at[:, 0, order[0, f]], out_sem).wait()
+        pltpu.make_async_copy(result.at[f], out.at[:, 0, slot[f]], out_sem).wait()
 
 
 def local(mixing, layer_mass, mass_east, mass_north, face_slot):
@@ -509,23 +532,26 @@
     def f32(*shape):
         return jax.ShapeDtypeStruct(shape, F32)
 
+    packed = (
+        f32(z.sent, z.width),
+        f32(z.sent, z.width),
+        f32(tiles * halves, 8, z.lanes),
+        f32(2, 8, z.lanes),
+        f32(z.own, 8, 128),
+        jax.ShapeDtypeStruct((8, 128), jnp.int32),
+    )
     to_a, to_b, messages, edges, own, order = pl.pallas_call(
         lambda *refs: pack_kernel(z, *refs),
-        out_shape=(
-            f32(z.sent, z.width),
-            f32(z.sent, z.width),
-            f32(tiles * halves, 8, z.lanes),
-            f32(2, 8, z.lanes),
-            f32(z.own, 8, 128),
-            jax.ShapeDtypeStruct((8, 128), jnp.int32),
-        ),
+        out_shape=packed,
         in_specs=[hbm] * 5,
-        out_specs=[vmem] * 6,
-        scratch_shapes=[
+        out_specs=[hbm] * 6,
+        scratch_shapes=[pltpu.VMEM(x.shape, x.dtype) for x in packed]
+        + [
             pltpu.SMEM((6,), jnp.int32),
             pltpu.VMEM(mixing.shape, F32),
             pltpu.VMEM((3,) + layer_mass.shape, F32),
             pltpu.SemaphoreType.DMA((4 + CHUNKS,)),
+            pltpu.SemaphoreType.DMA((7,)),
         ],
         name="pack",
     )(face_slot, mixing, layer_mass, mass_east, mass_north)
@@ -567,11 +593,9 @@
         in_specs=[vmem] * 8,
         out_specs=hbm,
         scratch_shapes=[
-            pltpu.SMEM((8, 128), jnp.int32),
             pltpu.VMEM((z.lanes, z.width), F32),
             pltpu.VMEM((2, 8, z.lanes), F32),
             pltpu.VMEM((6, z.species, 8, z.width), F32),
-            pltpu.SemaphoreType.DMA,
             pltpu.SemaphoreType.DMA,
         ],
         compiler_params=params,

time: 23.4 us -> 23 us (0.983)
  Pallas kernels: 6.83 us -> 6.4 us
    pallas_call x1, Pallas kernels: 1.71 us -> 1.37 us  [local(): pl.pallas_call(lambda *refs: finish_kernel(z, *refs), out_shape=f32(*mixi...]
where the time goes in v4:
time: 23 us; the launch traced here: 22.7 us
  starting transfers between devices  9.83 us (43%)
  waiting for transfers between devices  6.44 us (28%)
  Pallas kernels  6.4 us (28%)
    ppermute x1, starting transfers between devices, local(): from_b = lax.ppermute(to_b, 'tile', pairs)  5.48 us
    ppermute x1, waiting for transfers between devices, local(): others = lax.ppermute(mine, 'spec', [(0, 1), (1, 0)])  2.74 us
    all_to_all x1, starting transfers between devices, local(): arrived = lax.all_to_all(messages, ('tile', 'spec'), 0, 0, tiled=True)  2.72 us
    pallas_call x1, Pallas kernels, local(): pl.pallas_call(lambda *refs: interior_kernel(z, *refs), out_shape=(f32(*c...  2.51 us
    pallas_call x1, Pallas kernels, local(): pl.pallas_call(lambda *refs: pack_kernel(z, *refs), out_shape=packed, in_...  2.44 us
    all_to_all x1, waiting for transfers between devices, local(): arrived = lax.all_to_all(messages, ('tile', 'spec'), 0, 0, tiled=True)  2.04 us
    ppermute x1, waiting for transfers between devices, local(): from_b = lax.ppermute(to_b, 'tile', pairs)  1.65 us
    ppermute x1, starting transfers between devices, local(): others = lax.ppermute(mine, 'spec', [(0, 1), (1, 0)])  1.63 us
  transfers between devices with their start and end apart: 4, of which 3 were waited for; matrix products, arithmetic and copies ran while one was open for 0% of the time, Pallas kernels for 11%

profile of v4, /device:TPU:0, one launch (start us, length us, event | category | flops | bytes accessed | tf_op | source)
XLA Modules:
  0.0 22.7 jit_solution(8074119710311467750)
XLA Ops:
  0.0 2.4 %pack.1 = (f32[464,128]{1,0:T(8,128)}, f32[464,128]{1,0:T(8,128)}, f32[32,8,256]{2,1,0:T(8,128)}, f32[2,8,256]{2,1,0:T(8,128)}, f32[9,8,128]{2,1,0:T(8,128)}, /*index=5*/s32[8,128]{1,0:T(8,128)}) custom-call(s32[6]{0:T(128)} %refs_0_.1, f32[36,1,6,8,128]{4,3,2,1,0:T(8,128)} %refs_1_.5, f32[1,6,8,64]{3,2,1,0:T(8,128)} %refs_2_.1, f32[1,6,8,64]{3,2,1,0:T(8,128)} %refs_3_.1, ...), custom_call_target="tpu_custom_call" | custom-call | tf_op jit(solution)/shard_map/pack/pallas_call | solution.py:543
  2.4 5.5 %collective-permute-start = (f32[464,128]{1,0:T(8,128)}, f32[464,128]{1,0:T(8,128)S(1)}, u32[]{:S(2)}, u32[]{:S(2)}) collective-permute-start(f32[464,128]{1,0:T(8,128)} %get-tuple-element.15), channel_id=1, source_target_pairs={{0,30},{2,4},{4,2},{6,8},{8,6},{10,12},{12,10},{14,16},{16,14},{18... | collective-permute-start | bytes 712712 | tf_op jit(solution)/shard_map/ppermute | solution.py:561
  7.9 0.0 collective-permute-start.1
  7.9 0.0 copy-start.3
  7.9 2.7 %all-to-all-start = ((f32[32,8,256]{2,1,0:T(8,128)}), f32[32,8,256]{2,1,0:T(8,128)S(1)}, u32[]{:S(2)}, u32[]{:S(2)}) async-start(f32[32,8,256]{2,1,0:T(8,128)} %get-tuple-element.22), calls=%async_computation | async-start | bytes 524288 | tf_op jit(solution)/shard_map/all_to_all | solution.py:558
  10.7 1.6 %collective-permute-done.refs_2_.refs_3_ = f32[464,128]{1,0:T(8,128)S(1)} collective-permute-done((f32[464,128]{1,0:T(8,128)}, f32[464,128]{1,0:T(8,128)S(1)}, u32[]{:S(2)}, u32[]{:S(2)}) %collective-permute-start) | collective-permute-done | bytes 237600 | tf_op jit(solution)/shard_map/ppermute | solution.py:561
  12.3 0.0 collective-permute-done.1.refs_1_.refs_2_
  12.3 0.0 copy-done.3
  12.3 0.0 copy-start
  12.3 0.0 copy-start.2
  12.3 0.1 share.1.refs_4_
  12.4 1.6 %collective-permute-start.2 = (f32[11,8,128]{2,1,0:T(8,128)S(1)}, f32[11,8,128]{2,1,0:T(8,128)S(1)}, u32[]{:S(2)}, u32[]{:S(2)}) collective-permute-start(f32[11,8,128]{2,1,0:T(8,128)S(1)} %share.1.refs_4_), channel_id=1, source_target_pairs={{0,1},{1,0},{2,3},{3,2},{4,5},{5,4},{6,7},{7,6},{8,9},{9,8},{10,11... | collective-permute-start | bytes 135176 | tf_op jit(solution)/shard_map/ppermute | solution.py:572
  14.0 2.7 %collective-permute-done.2.refs_5_ = f32[11,8,128]{2,1,0:T(8,128)S(1)} collective-permute-done((f32[11,8,128]{2,1,0:T(8,128)S(1)}, f32[11,8,128]{2,1,0:T(8,128)S(1)}, u32[]{:S(2)}, u32[]{:S(2)}) %collective-permute-start.2) | collective-permute-done | bytes 45088 | tf_op jit(solution)/shard_map/ppermute | solution.py:572
  16.8 0.0 copy-done
  16.8 0.0 copy-done.2
  16.8 0.0 copy-start.1
  16.8 2.5 %interior.1 = (f32[36,6,8,128]{3,2,1,0:T(8,128)S(1)}, f32[2,8,256]{2,1,0:T(8,128)S(1)}, f32[6,6,8,128]{3,2,1,0:T(8,128)S(1)}) custom-call(s32[8,128]{1,0:T(8,128)S(1)} %copy-done.2, f32[36,1,6,8,128]{4,3,2,1,0:T(8,128)S(1)} %copy-done, f32[464,128]{1,0:T(8,128)S(1)} %collective-permute-done.1.refs_1_.refs_2_, ...), custom_call_target="tpu_custom_call" | custom-call | tf_op jit(solution)/shard_map/interior/pallas_call | solution.py:575
  19.3 2.0 %all-to-all-done.refs_7_ = f32[32,8,256]{2,1,0:T(8,128)S(1)} async-done(((f32[32,8,256]{2,1,0:T(8,128)}), f32[32,8,256]{2,1,0:T(8,128)S(1)}, u32[]{:S(2)}, u32[]{:S(2)}) %all-to-all-start) | async-done | bytes 262176 | tf_op jit(solution)/shard_map/all_to_all | solution.py:558
  21.4 0.0 copy-done.1
  21.4 1.4 %finish.1 = f32[36,1,6,8,128]{4,3,2,1,0:T(8,128)} custom-call(s32[8,128]{1,0:T(8,128)S(1)} %copy-done.2, f32[36,1,6,8,128]{4,3,2,1,0:T(8,128)S(1)} %copy-done, f32[464,128]{1,0:T(8,128)S(1)} %collective-permute-done.refs_2_.refs_3_, f32[36,6,8,128]{3,2,1,0:T(8,128)S(1)} %get-tuple-element.18.refs_3_, f32[2,8,256]{2,1,0:T(8,128)S(1)} %get-tuple-element.19.refs_4_, ...), custom_call_target="tpu_custom_call" | custom-call | tf_op jit(solution)/shard_map/finish/pallas_call | solution.py:590
Async XLA Ops:
  2.4 9.9 %collective-permute-start = (f32[464,128]{1,0:T(8,128)}, f32[464,128]{1,0:T(8,128)S(1)}, u32[]{:S(2)}, u32[]{:S(2)}) collective-permute-start(f32[464,128]{1,0:T(8,128)} %get-tuple-element.15), channel_id=1, source_target_pairs={{0,30},{2,4},{4,2},{6,8},{8,6},{10,12},{12,10},{14,16},{16,14},{18... | collective-permute-start | bytes 712712 | tf_op jit(solution)/shard_map/ppermute | solution.py:561
  7.9 4.4 %collective-permute-start.1 = (f32[464,128]{1,0:T(8,128)}, f32[464,128]{1,0:T(8,128)S(1)}, u32[]{:S(2)}, u32[]{:S(2)}) collective-permute-start(f32[464,128]{1,0:T(8,128)} %get-tuple-element.16), channel_id=1, source_target_pairs={{0,2},{2,0},{4,6},{6,4},{8,10},{10,8},{12,14},{14,12},{16,18},{18,... | collective-permute-start | bytes 712712 | tf_op jit(solution)/shard_map/ppermute | solution.py:559
  7.9 4.4 %copy-start.3 = (f32[9,8,128]{2,1,0:T(8,128)S(1)}, f32[9,8,128]{2,1,0:T(8,128)}, u32[]{:S(2)}) copy-start(f32[9,8,128]{2,1,0:T(8,128)} %get-tuple-element.17.refs_0_) | copy-start | bytes 110596
  7.9 13.4 %all-to-all-start = ((f32[32,8,256]{2,1,0:T(8,128)}), f32[32,8,256]{2,1,0:T(8,128)S(1)}, u32[]{:S(2)}, u32[]{:S(2)}) async-start(f32[32,8,256]{2,1,0:T(8,128)} %get-tuple-element.22), calls=%async_computation | async-start | bytes 524288 | tf_op jit(solution)/shard_map/all_to_all | solution.py:558
  12.3 4.5 %copy-start = (f32[36,1,6,8,128]{4,3,2,1,0:T(8,128)S(1)}, f32[36,1,6,8,128]{4,3,2,1,0:T(8,128)}, u32[]{:S(2)}) copy-start(f32[36,1,6,8,128]{4,3,2,1,0:T(8,128)} %refs_1_.5) | copy-start | bytes 2654212
  12.3 4.5 %copy-start.2 = (s32[8,128]{1,0:T(8,128)S(1)}, s32[8,128]{1,0:T(8,128)}, u32[]{:S(2)}) copy-start(s32[8,128]{1,0:T(8,128)} %get-tuple-element.14.refs_0_) | copy-start | bytes 12292
  12.4 4.4 %collective-permute-start.2 = (f32[11,8,128]{2,1,0:T(8,128)S(1)}, f32[11,8,128]{2,1,0:T(8,128)S(1)}, u32[]{:S(2)}, u32[]{:S(2)}) collective-permute-start(f32[11,8,128]{2,1,0:T(8,128)S(1)} %share.1.refs_4_), channel_id=1, source_target_pairs={{0,1},{1,0},{2,3},{3,2},{4,5},{5,4},{6,7},{7,6},{8,9},{9,8},{10,11... | collective-permute-start | bytes 135176 | tf_op jit(solution)/shard_map/ppermute | solution.py:572
  16.8 4.6 %copy-start.1 = (f32[2,8,256]{2,1,0:T(8,128)S(1)}, f32[2,8,256]{2,1,0:T(8,128)}, u32[]{:S(2)}) copy-start(f32[2,8,256]{2,1,0:T(8,128)} %get-tuple-element.21.refs_6_) | copy-start | bytes 49156

commit v5 on v4

--- a/solution.py
+++ b/solution.py
@@ -169,14 +169,14 @@
         for t in range(z.tiles):
             at = 8 * (z.tiles - 1 - t)
             for n in range(n_half):
-                out[t * n_half + n] = messages[at : at + 8]
+                out[n, t] = messages[at : at + 8]
         for t, cols in ends:
             at = 8 * (z.tiles - 1 - t)
             k = z.flux2 // 128
             here = (lane >= z.flux2 % 128) & (lane < z.flux2 % 128 + 8)
             mixed = jnp.where(here, cols[k], messages[at : at + 8, k * 128 : (k + 1) * 128])
             for n in range(n_half):
-                out[t * n_half + n, :, k * 128 : (k + 1) * 128] = mixed
+                out[n, t, :, k * 128 : (k + 1) * 128] = mixed
         copy = pltpu.make_async_copy(out, out_out, out_sems.at[5])
         copy.start()
         copy.wait()
@@ -186,11 +186,10 @@
         for t, cols in ends:
             for n in range(n_half):
                 for k in range(z.vregs):
-                    out[t * n_half + n, :, k * 128 : (k + 1) * 128] = cols[k]
+                    out[n, t, :, k * 128 : (k + 1) * 128] = cols[k]
         copies = []
         for t, _ in ends:
-            some = pl.ds(t * n_half, n_half)
-            copies.append(pltpu.make_async_copy(out.at[some], out_out.at[some], out_sems.at[5 + (t > 0)]))
+            copies.append(pltpu.make_async_copy(out.at[:, t], out_out.at[:, t], out_sems.at[5 + (t > 0)]))
         for copy in copies:
             copy.start()
         for copy in copies:
@@ -370,7 +369,7 @@
     odd_end = (lane1 & 1) == 1
     for parity in range(2):
         end = z.tiles - 1 if parity == 0 else 0
-        flux = reverse8(arrived[end * n_half + holder, :, (z.flux // 128) * 128 : (z.flux // 128 + 1) * 128])
+        flux = reverse8(arrived[holder, end, :, (z.flux // 128) * 128 : (z.flux // 128 + 1) * 128])
         mul = []
         for a in range(3):
             f = 2 * a + parity
@@ -392,7 +391,7 @@
                 )
         for k in range(z.vregs):
             cut = slice(k * 128, (k + 1) * 128)
-            g = reverse8(arrived[end * n_half + half, :, cut])
+            g = reverse8(arrived[half, end, :, cut])
             own, q = ends[parity, :, cut], edges[parity, :, cut]
             m = [spread([mul[a][n] for a in range(3)], k) for n in range(len(mul[0]))]
             if parity == 0:
@@ -443,9 +442,9 @@
                 elif t == z.tiles - 1:
                     x = jnp.where(first, spare, mine)
                 else:
-                    x = arrived[t * n_half + half, :, cut]
+                    x = arrived[half, t, :, cut]
                 if (k + 1) * 128 > z.flux:
-                    x = jnp.where(lane1 + k * 128 < z.flux, x, arrived[t * n_half + holder, :, cut])
+                    x = jnp.where(lane1 + k * 128 < z.flux, x, arrived[holder, t, :, cut])
                 parts.append(x)
             pieces.append(jnp.concatenate(parts, axis=0).T)
         turned[...] = jnp.concatenate(pieces, axis=0) if len(pieces) > 1 else pieces[0]
@@ -535,7 +534,7 @@
     packed = (
         f32(z.sent, z.width),
         f32(z.sent, z.width),
-        f32(tiles * halves, 8, z.lanes),
+        f32(halves, tiles, 8, z.lanes),
         f32(2, 8, z.lanes),
         f32(z.own, 8, 128),
         jax.ShapeDtypeStruct((8, 128), jnp.int32),
@@ -555,7 +554,9 @@
         ],
         name="pack",
     )(face_slot, mixing, layer_mass, mass_east, mass_north)
-    arrived = lax.all_to_all(messages, ("tile", "spec"), 0, 0, tiled=True)
+    arrived = lax.all_to_all(
+        messages.reshape(halves * tiles, 8, z.lanes), ("spec", "tile"), 0, 0, tiled=True
+    ).reshape(messages.shape)
     from_a = lax.ppermute(to_a, "tile", [(i, i ^ 1) for i in range(tiles)])
     pairs = [(i, (i + 1) % tiles) if i % 2 else (i, (i - 1) % tiles) for i in range(tiles)]
     from_b = lax.ppermute(to_b, "tile", pairs)

time: 23 us -> 22.6 us (0.983)
  waiting for transfers between devices: 6.44 us -> 6.03 us
    all_to_all x1, waiting for transfers between devices: 2.04 us -> 1.58 us  [local(): lax.all_to_all(messages.reshape(halves * tiles, 8, z.lanes), ('spec', 'ti...]
  transfers between devices with their start and end apart: 4 -> 4, of which waited for: 3 -> 3; matrix products, arithmetic and copies ran while one was open for 0% -> 0% of each run, Pallas kernels for 11% -> 12%
where the time goes in v5:
time: 22.6 us; the launch traced here: 22.3 us
  starting transfers between devices  9.83 us (43%)
  Pallas kernels  6.41 us (28%)
  waiting for transfers between devices  6.03 us (27%)
    ppermute x1, starting transfers between devices, local(): from_b = lax.ppermute(to_b, 'tile', pairs)  5.48 us
    ppermute x1, waiting for transfers between devices, local(): others = lax.ppermute(mine, 'spec', [(0, 1), (1, 0)])  2.8 us
    all_to_all x1, starting transfers between devices, local(): lax.all_to_all(messages.reshape(halves * tiles, 8, z.lanes), ('spec', 'ti...  2.72 us
    pallas_call x1, Pallas kernels, local(): pl.pallas_call(lambda *refs: interior_kernel(z, *refs), out_shape=(f32(*c...  2.52 us
    pallas_call x1, Pallas kernels, local(): pl.pallas_call(lambda *refs: pack_kernel(z, *refs), out_shape=packed, in_...  2.43 us
    ppermute x1, waiting for transfers between devices, local(): from_b = lax.ppermute(to_b, 'tile', pairs)  1.65 us
    ppermute x1, starting transfers between devices, local(): others = lax.ppermute(mine, 'spec', [(0, 1), (1, 0)])  1.63 us
    all_to_all x1, waiting for transfers between devices, local(): lax.all_to_all(messages.reshape(halves * tiles, 8, z.lanes), ('spec', 'ti...  1.58 us
  transfers between devices with their start and end apart: 4, of which 3 were waited for; matrix products, arithmetic and copies ran while one was open for 0% of the time, Pallas kernels for 12%

profile of v5, /device:TPU:0, one launch (start us, length us, event | category | flops | bytes accessed | tf_op | source)
XLA Modules:
  0.0 22.3 jit_solution(1124103992621551397)
XLA Ops:
  0.0 2.4 %pack.1 = (f32[464,128]{1,0:T(8,128)}, f32[464,128]{1,0:T(8,128)}, f32[2,16,8,256]{3,2,1,0:T(8,128)}, f32[2,8,256]{2,1,0:T(8,128)}, f32[9,8,128]{2,1,0:T(8,128)}, /*index=5*/s32[8,128]{1,0:T(8,128)}) custom-call(s32[6]{0:T(128)} %refs_0_.1, f32[36,1,6,8,128]{4,3,2,1,0:T(8,128)} %refs_1_.5, f32[1,6,8,64]{3,2,1,0:T(8,128)} %refs_2_.1, ...), custom_call_target="tpu_custom_call" | custom-call | tf_op jit(solution)/shard_map/pack/pallas_call | solution.py:542
  2.4 5.5 %collective-permute-start = (f32[464,128]{1,0:T(8,128)}, f32[464,128]{1,0:T(8,128)S(1)}, u32[]{:S(2)}, u32[]{:S(2)}) collective-permute-start(f32[464,128]{1,0:T(8,128)} %get-tuple-element.15), channel_id=1, source_target_pairs={{0,30},{2,4},{4,2},{6,8},{8,6},{10,12},{12,10},{14,16},{16,14},{18... | collective-permute-start | bytes 712712 | tf_op jit(solution)/shard_map/ppermute | solution.py:562
  7.9 0.0 collective-permute-start.1
  7.9 0.0 copy-start.3
  7.9 2.7 %all-to-all-start = ((f32[32,8,256]{2,1,0:T(8,128)}), f32[32,8,256]{2,1,0:T(8,128)S(1)}, u32[]{:S(2)}, u32[]{:S(2)}) async-start(f32[32,8,256]{2,1,0:T(8,128)} %bitcast.3), calls=%async_computation | async-start | bytes 524288 | tf_op jit(solution)/shard_map/all_to_all | solution.py:557
  10.7 1.6 %collective-permute-done.refs_2_.refs_3_ = f32[464,128]{1,0:T(8,128)S(1)} collective-permute-done((f32[464,128]{1,0:T(8,128)}, f32[464,128]{1,0:T(8,128)S(1)}, u32[]{:S(2)}, u32[]{:S(2)}) %collective-permute-start) | collective-permute-done | bytes 237600 | tf_op jit(solution)/shard_map/ppermute | solution.py:562
  12.3 0.0 collective-permute-done.1.refs_1_.refs_2_
  12.3 0.0 copy-done.3
  12.3 0.0 copy-start
  12.3 0.0 copy-start.2
  12.3 0.1 share.1.refs_4_
  12.4 1.6 %collective-permute-start.2 = (f32[11,8,128]{2,1,0:T(8,128)S(1)}, f32[11,8,128]{2,1,0:T(8,128)S(1)}, u32[]{:S(2)}, u32[]{:S(2)}) collective-permute-start(f32[11,8,128]{2,1,0:T(8,128)S(1)} %share.1.refs_4_), channel_id=1, source_target_pairs={{0,1},{1,0},{2,3},{3,2},{4,5},{5,4},{6,7},{7,6},{8,9},{9,8},{10,11... | collective-permute-start | bytes 135176 | tf_op jit(solution)/shard_map/ppermute | solution.py:573
  14.0 2.8 %collective-permute-done.2.refs_5_ = f32[11,8,128]{2,1,0:T(8,128)S(1)} collective-permute-done((f32[11,8,128]{2,1,0:T(8,128)S(1)}, f32[11,8,128]{2,1,0:T(8,128)S(1)}, u32[]{:S(2)}, u32[]{:S(2)}) %collective-permute-start.2) | collective-permute-done | bytes 45088 | tf_op jit(solution)/shard_map/ppermute | solution.py:573
  16.8 0.0 copy-done
  16.8 0.0 copy-done.2
  16.8 0.0 copy-start.1
  16.8 2.5 %interior.1 = (f32[36,6,8,128]{3,2,1,0:T(8,128)S(1)}, f32[2,8,256]{2,1,0:T(8,128)S(1)}, f32[6,6,8,128]{3,2,1,0:T(8,128)S(1)}) custom-call(s32[8,128]{1,0:T(8,128)S(1)} %copy-done.2, f32[36,1,6,8,128]{4,3,2,1,0:T(8,128)S(1)} %copy-done, f32[464,128]{1,0:T(8,128)S(1)} %collective-permute-done.1.refs_1_.refs_2_, ...), custom_call_target="tpu_custom_call" | custom-call | tf_op jit(solution)/shard_map/interior/pallas_call | solution.py:576
  19.4 1.6 %all-to-all-done = f32[32,8,256]{2,1,0:T(8,128)S(1)} async-done(((f32[32,8,256]{2,1,0:T(8,128)}), f32[32,8,256]{2,1,0:T(8,128)S(1)}, u32[]{:S(2)}, u32[]{:S(2)}) %all-to-all-start) | async-done | bytes 262176 | tf_op jit(solution)/shard_map/all_to_all | solution.py:557
  21.0 0.0 copy-done.1
  21.0 1.4 %finish.1 = f32[36,1,6,8,128]{4,3,2,1,0:T(8,128)} custom-call(s32[8,128]{1,0:T(8,128)S(1)} %copy-done.2, f32[36,1,6,8,128]{4,3,2,1,0:T(8,128)S(1)} %copy-done, f32[464,128]{1,0:T(8,128)S(1)} %collective-permute-done.refs_2_.refs_3_, f32[36,6,8,128]{3,2,1,0:T(8,128)S(1)} %get-tuple-element.18.refs_3_, f32[2,8,256]{2,1,0:T(8,128)S(1)} %get-tuple-element.19.refs_4_, ...), custom_call_target="tpu_custom_call" | custom-call | tf_op jit(solution)/shard_map/finish/pallas_call | solution.py:591
Async XLA Ops:
  2.4 9.9 %collective-permute-start = (f32[464,128]{1,0:T(8,128)}, f32[464,128]{1,0:T(8,128)S(1)}, u32[]{:S(2)}, u32[]{:S(2)}) collective-permute-start(f32[464,128]{1,0:T(8,128)} %get-tuple-element.15), channel_id=1, source_target_pairs={{0,30},{2,4},{4,2},{6,8},{8,6},{10,12},{12,10},{14,16},{16,14},{18... | collective-permute-start | bytes 712712 | tf_op jit(solution)/shard_map/ppermute | solution.py:562
  7.9 4.4 %collective-permute-start.1 = (f32[464,128]{1,0:T(8,128)}, f32[464,128]{1,0:T(8,128)S(1)}, u32[]{:S(2)}, u32[]{:S(2)}) collective-permute-start(f32[464,128]{1,0:T(8,128)} %get-tuple-element.16), channel_id=1, source_target_pairs={{0,2},{2,0},{4,6},{6,4},{8,10},{10,8},{12,14},{14,12},{16,18},{18,... | collective-permute-start | bytes 712712 | tf_op jit(solution)/shard_map/ppermute | solution.py:560
  7.9 4.4 %copy-start.3 = (f32[9,8,128]{2,1,0:T(8,128)S(1)}, f32[9,8,128]{2,1,0:T(8,128)}, u32[]{:S(2)}) copy-start(f32[9,8,128]{2,1,0:T(8,128)} %get-tuple-element.17.refs_0_) | copy-start | bytes 110596
  7.9 13.0 %all-to-all-start = ((f32[32,8,256]{2,1,0:T(8,128)}), f32[32,8,256]{2,1,0:T(8,128)S(1)}, u32[]{:S(2)}, u32[]{:S(2)}) async-start(f32[32,8,256]{2,1,0:T(8,128)} %bitcast.3), calls=%async_computation | async-start | bytes 524288 | tf_op jit(solution)/shard_map/all_to_all | solution.py:557
  12.3 4.5 %copy-start = (f32[36,1,6,8,128]{4,3,2,1,0:T(8,128)S(1)}, f32[36,1,6,8,128]{4,3,2,1,0:T(8,128)}, u32[]{:S(2)}) copy-start(f32[36,1,6,8,128]{4,3,2,1,0:T(8,128)} %refs_1_.5) | copy-start | bytes 2654212
  12.3 4.5 %copy-start.2 = (s32[8,128]{1,0:T(8,128)S(1)}, s32[8,128]{1,0:T(8,128)}, u32[]{:S(2)}) copy-start(s32[8,128]{1,0:T(8,128)} %get-tuple-element.14.refs_0_) | copy-start | bytes 12292
  12.4 4.4 %collective-permute-start.2 = (f32[11,8,128]{2,1,0:T(8,128)S(1)}, f32[11,8,128]{2,1,0:T(8,128)S(1)}, u32[]{:S(2)}, u32[]{:S(2)}) collective-permute-start(f32[11,8,128]{2,1,0:T(8,128)S(1)} %share.1.refs_4_), channel_id=1, source_target_pairs={{0,1},{1,0},{2,3},{3,2},{4,5},{5,4},{6,7},{7,6},{8,9},{9,8},{10,11... | collective-permute-start | bytes 135176 | tf_op jit(solution)/shard_map/ppermute | solution.py:573
  16.8 4.1 %copy-start.1 = (f32[2,8,256]{2,1,0:T(8,128)S(1)}, f32[2,8,256]{2,1,0:T(8,128)}, u32[]{:S(2)}) copy-start(f32[2,8,256]{2,1,0:T(8,128)} %get-tuple-element.21.refs_6_) | copy-start | bytes 49156

commit v6 on v5

--- a/solution.py
+++ b/solution.py
@@ -9,6 +9,10 @@
 VMEM_LIMIT = 12 << 20
 CHUNKS = 2
 OUT_CHUNKS = 4
+ORDERS = {(16, 2): (
+    19, 30, 2, 3, 17, 10, 15, 6, 20, 22, 16, 9, 25, 1, 5, 7,
+    12, 31, 28, 0, 14, 27, 21, 8, 11, 26, 18, 13, 4, 29, 24, 23,
+)}
 
 
 def up(value, unit):
@@ -33,6 +37,10 @@
         self.own = up(18, self.per) // self.per
         self.pieces = 21
         self.shared = up(self.pieces, self.per) // self.per
+        natural = tuple(t * halves + n for n in range(halves) for t in range(tiles))
+        self.order = ORDERS.get((tiles, halves), natural)
+        ranks = {device: rank for rank, device in enumerate(self.order)}
+        self.rank = [[ranks[t * halves + n] for n in range(halves)] for t in range(tiles)]
 
 
 def slots(face_slot):
@@ -169,14 +177,14 @@
         for t in range(z.tiles):
             at = 8 * (z.tiles - 1 - t)
             for n in range(n_half):
-                out[n, t] = messages[at : at + 8]
+                out[z.rank[t][n]] = messages[at : at + 8]
         for t, cols in ends:
             at = 8 * (z.tiles - 1 - t)
             k = z.flux2 // 128
             here = (lane >= z.flux2 % 128) & (lane < z.flux2 % 128 + 8)
             mixed = jnp.where(here, cols[k], messages[at : at + 8, k * 128 : (k + 1) * 128])
             for n in range(n_half):
-                out[n, t, :, k * 128 : (k + 1) * 128] = mixed
+                out[z.rank[t][n], :, k * 128 : (k + 1) * 128] = mixed
         copy = pltpu.make_async_copy(out, out_out, out_sems.at[5])
         copy.start()
         copy.wait()
@@ -186,10 +194,12 @@
         for t, cols in ends:
             for n in range(n_half):
                 for k in range(z.vregs):
-                    out[n, t, :, k * 128 : (k + 1) * 128] = cols[k]
+                    out[z.rank[t][n], :, k * 128 : (k + 1) * 128] = cols[k]
         copies = []
-        for t, _ in ends:
-            copies.append(pltpu.make_async_copy(out.at[:, t], out_out.at[:, t], out_sems.at[5 + (t > 0)]))
+        for e, (t, _) in enumerate(ends):
+            for n in range(n_half):
+                at = z.rank[t][n]
+                copies.append(pltpu.make_async_copy(out.at[at], out_out.at[at], out_sems.at[5 + e * n_half + n]))
         for copy in copies:
             copy.start()
         for copy in copies:
@@ -355,6 +365,11 @@
     lane1 = lax.broadcasted_iota(jnp.int32, (8, 128), 1)
     twelfth = 1.0 / 12.0
     holder = lax.div(width - 8 - 8 * place, part)
+
+    def message(n, t, cut):
+        rank = sum(jnp.where(n == h, z.rank[t][h], 0) for h in range(n_half))
+        return arrived[rank, :, cut]
+
     places = order_in[0:1].astype(F32)
     slot = [jnp.sum(jnp.where(lane1[0:1] == f, places, 0.0)).astype(jnp.int32) for f in range(6)]
 
@@ -369,7 +384,7 @@
     odd_end = (lane1 & 1) == 1
     for parity in range(2):
         end = z.tiles - 1 if parity == 0 else 0
-        flux = reverse8(arrived[holder, end, :, (z.flux // 128) * 128 : (z.flux // 128 + 1) * 128])
+        flux = reverse8(message(holder, end, slice((z.flux // 128) * 128, (z.flux // 128 + 1) * 128)))
         mul = []
         for a in range(3):
             f = 2 * a + parity
@@ -391,7 +406,7 @@
                 )
         for k in range(z.vregs):
             cut = slice(k * 128, (k + 1) * 128)
-            g = reverse8(arrived[half, end, :, cut])
+            g = reverse8(message(half, end, cut))
             own, q = ends[parity, :, cut], edges[parity, :, cut]
             m = [spread([mul[a][n] for a in range(3)], k) for n in range(len(mul[0]))]
             if parity == 0:
@@ -442,9 +457,9 @@
                 elif t == z.tiles - 1:
                     x = jnp.where(first, spare, mine)
                 else:
-                    x = arrived[half, t, :, cut]
+                    x = message(half, t, cut)
                 if (k + 1) * 128 > z.flux:
-                    x = jnp.where(lane1 + k * 128 < z.flux, x, arrived[holder, t, :, cut])
+                    x = jnp.where(lane1 + k * 128 < z.flux, x, message(holder, t, cut))
                 parts.append(x)
             pieces.append(jnp.concatenate(parts, axis=0).T)
         turned[...] = jnp.concatenate(pieces, axis=0) if len(pieces) > 1 else pieces[0]
@@ -534,7 +549,7 @@
     packed = (
         f32(z.sent, z.width),
         f32(z.sent, z.width),
-        f32(halves, tiles, 8, z.lanes),
+        f32(halves * tiles, 8, z.lanes),
         f32(2, 8, z.lanes),
         f32(z.own, 8, 128),
         jax.ShapeDtypeStruct((8, 128), jnp.int32),
@@ -550,13 +565,13 @@
             pltpu.VMEM(mixing.shape, F32),
             pltpu.VMEM((3,) + layer_mass.shape, F32),
             pltpu.SemaphoreType.DMA((4 + CHUNKS,)),
-            pltpu.SemaphoreType.DMA((7,)),
+            pltpu.SemaphoreType.DMA((5 + 2 * halves,)),
         ],
         name="pack",
     )(face_slot, mixing, layer_mass, mass_east, mass_north)
     arrived = lax.all_to_all(
-        messages.reshape(halves * tiles, 8, z.lanes), ("spec", "tile"), 0, 0, tiled=True
-    ).reshape(messages.shape)
+        messages, ("tile", "spec"), 0, 0, axis_index_groups=[list(z.order)], tiled=True
+    )
     from_a = lax.ppermute(to_a, "tile", [(i, i ^ 1) for i in range(tiles)])
     pairs = [(i, (i + 1) % tiles) if i % 2 else (i, (i - 1) % tiles) for i in range(tiles)]
     from_b = lax.ppermute(to_b, "tile", pairs)

time: 22.6 us -> 21.6 us (0.956)
  waiting for transfers between devices: 6.03 us -> 5.02 us
    all_to_all x1, waiting for transfers between devices: 1.58 us -> 0.69 us  [local(): lax.all_to_all(messages, ('tile', 'spec'), 0, 0, axis_index_groups=[list(...]
where the time goes in v6:
time: 21.6 us; the launch traced here: 21.3 us
  starting transfers between devices  9.83 us (46%)
  Pallas kernels  6.42 us (30%)
  waiting for transfers between devices  5.02 us (23%)
    ppermute x1, starting transfers between devices, local(): from_b = lax.ppermute(to_b, 'tile', pairs)  5.48 us
    all_to_all x1, starting transfers between devices, local(): lax.all_to_all(messages, ('tile', 'spec'), 0, 0, axis_index_groups=[list(...  2.72 us
    ppermute x1, waiting for transfers between devices, local(): others = lax.ppermute(mine, 'spec', [(0, 1), (1, 0)])  2.68 us
    pallas_call x1, Pallas kernels, local(): pl.pallas_call(lambda *refs: interior_kernel(z, *refs), out_shape=(f32(*c...  2.51 us
    pallas_call x1, Pallas kernels, local(): pl.pallas_call(lambda *refs: pack_kernel(z, *refs), out_shape=packed, in_...  2.46 us
    ppermute x1, waiting for transfers between devices, local(): from_b = lax.ppermute(to_b, 'tile', pairs)  1.65 us
    ppermute x1, starting transfers between devices, local(): others = lax.ppermute(mine, 'spec', [(0, 1), (1, 0)])  1.63 us
    pallas_call x1, Pallas kernels, local(): pl.pallas_call(lambda *refs: finish_kernel(z, *refs), out_shape=f32(*mixi...  1.37 us
  transfers between devices with their start and end apart: 4, of which 3 were waited for; matrix products, arithmetic and copies ran while one was open for 0% of the time, Pallas kernels for 12%

profile of v6, /device:TPU:0, one launch (start us, length us, event | category | flops | bytes accessed | tf_op | source)
XLA Modules:
  0.0 21.3 jit_solution(16227601945357404358)
XLA Ops:
  0.0 2.5 %pack.1 = (f32[464,128]{1,0:T(8,128)}, f32[464,128]{1,0:T(8,128)}, f32[32,8,256]{2,1,0:T(8,128)}, f32[2,8,256]{2,1,0:T(8,128)}, f32[9,8,128]{2,1,0:T(8,128)}, /*index=5*/s32[8,128]{1,0:T(8,128)}) custom-call(s32[6]{0:T(128)} %refs_0_.1, f32[36,1,6,8,128]{4,3,2,1,0:T(8,128)} %refs_1_.5, f32[1,6,8,64]{3,2,1,0:T(8,128)} %refs_2_.1, f32[1,6,8,64]{3,2,1,0:T(8,128)} %refs_3_.1, ...), custom_call_target="tpu_custom_call" | custom-call | tf_op jit(solution)/shard_map/pack/pallas_call | solution.py:557
  2.5 5.5 %collective-permute-start = (f32[464,128]{1,0:T(8,128)}, f32[464,128]{1,0:T(8,128)S(1)}, u32[]{:S(2)}, u32[]{:S(2)}) collective-permute-start(f32[464,128]{1,0:T(8,128)} %get-tuple-element.15), channel_id=1, source_target_pairs={{0,30},{2,4},{4,2},{6,8},{8,6},{10,12},{12,10},{14,16},{16,14},{18... | collective-permute-start | bytes 712712 | tf_op jit(solution)/shard_map/ppermute | solution.py:577
  7.9 0.0 collective-permute-start.1
  7.9 0.0 copy-start.3
  8.0 2.7 %all-to-all-start = ((f32[32,8,256]{2,1,0:T(8,128)}), f32[32,8,256]{2,1,0:T(8,128)S(1)}, u32[]{:S(2)}, u32[]{:S(2)}) async-start(f32[32,8,256]{2,1,0:T(8,128)} %get-tuple-element.22), calls=%async_computation | async-start | bytes 524288 | tf_op jit(solution)/shard_map/all_to_all | solution.py:572
  10.7 1.6 %collective-permute-done.refs_2_.refs_3_ = f32[464,128]{1,0:T(8,128)S(1)} collective-permute-done((f32[464,128]{1,0:T(8,128)}, f32[464,128]{1,0:T(8,128)S(1)}, u32[]{:S(2)}, u32[]{:S(2)}) %collective-permute-start) | collective-permute-done | bytes 237600 | tf_op jit(solution)/shard_map/ppermute | solution.py:577
  12.3 0.0 collective-permute-done.1.refs_1_.refs_2_
  12.3 0.0 copy-done.3
  12.3 0.0 copy-start
  12.3 0.0 copy-start.2
  12.3 0.1 share.1.refs_4_
  12.4 1.6 %collective-permute-start.2 = (f32[11,8,128]{2,1,0:T(8,128)S(1)}, f32[11,8,128]{2,1,0:T(8,128)S(1)}, u32[]{:S(2)}, u32[]{:S(2)}) collective-permute-start(f32[11,8,128]{2,1,0:T(8,128)S(1)} %share.1.refs_4_), channel_id=1, source_target_pairs={{0,1},{1,0},{2,3},{3,2},{4,5},{5,4},{6,7},{7,6},{8,9},{9,8},{10,11... | collective-permute-start | bytes 135176 | tf_op jit(solution)/shard_map/ppermute | solution.py:588
  14.1 2.7 %collective-permute-done.2.refs_5_ = f32[11,8,128]{2,1,0:T(8,128)S(1)} collective-permute-done((f32[11,8,128]{2,1,0:T(8,128)S(1)}, f32[11,8,128]{2,1,0:T(8,128)S(1)}, u32[]{:S(2)}, u32[]{:S(2)}) %collective-permute-start.2) | collective-permute-done | bytes 45088 | tf_op jit(solution)/shard_map/ppermute | solution.py:588
  16.7 0.0 copy-done
  16.7 0.0 copy-done.2
  16.7 0.0 copy-start.1
  16.7 2.5 %interior.1 = (f32[36,6,8,128]{3,2,1,0:T(8,128)S(1)}, f32[2,8,256]{2,1,0:T(8,128)S(1)}, f32[6,6,8,128]{3,2,1,0:T(8,128)S(1)}) custom-call(s32[8,128]{1,0:T(8,128)S(1)} %copy-done.2, f32[36,1,6,8,128]{4,3,2,1,0:T(8,128)S(1)} %copy-done, f32[464,128]{1,0:T(8,128)S(1)} %collective-permute-done.1.refs_1_.refs_2_, ...), custom_call_target="tpu_custom_call" | custom-call | tf_op jit(solution)/shard_map/interior/pallas_call | solution.py:591
  19.3 0.7 %all-to-all-done.refs_7_ = f32[32,8,256]{2,1,0:T(8,128)S(1)} async-done(((f32[32,8,256]{2,1,0:T(8,128)}), f32[32,8,256]{2,1,0:T(8,128)S(1)}, u32[]{:S(2)}, u32[]{:S(2)}) %all-to-all-start) | async-done | bytes 262176 | tf_op jit(solution)/shard_map/all_to_all | solution.py:572
  19.9 0.0 copy-done.1
  19.9 1.4 %finish.1 = f32[36,1,6,8,128]{4,3,2,1,0:T(8,128)} custom-call(s32[8,128]{1,0:T(8,128)S(1)} %copy-done.2, f32[36,1,6,8,128]{4,3,2,1,0:T(8,128)S(1)} %copy-done, f32[464,128]{1,0:T(8,128)S(1)} %collective-permute-done.refs_2_.refs_3_, f32[36,6,8,128]{3,2,1,0:T(8,128)S(1)} %get-tuple-element.18.refs_3_, f32[2,8,256]{2,1,0:T(8,128)S(1)} %get-tuple-element.19.refs_4_, ...), custom_call_target="tpu_custom_call" | custom-call | tf_op jit(solution)/shard_map/finish/pallas_call | solution.py:606
Async XLA Ops:
  2.5 9.9 %collective-permute-start = (f32[464,128]{1,0:T(8,128)}, f32[464,128]{1,0:T(8,128)S(1)}, u32[]{:S(2)}, u32[]{:S(2)}) collective-permute-start(f32[464,128]{1,0:T(8,128)} %get-tuple-element.15), channel_id=1, source_target_pairs={{0,30},{2,4},{4,2},{6,8},{8,6},{10,12},{12,10},{14,16},{16,14},{18... | collective-permute-start | bytes 712712 | tf_op jit(solution)/shard_map/ppermute | solution.py:577
  7.9 4.4 %collective-permute-start.1 = (f32[464,128]{1,0:T(8,128)}, f32[464,128]{1,0:T(8,128)S(1)}, u32[]{:S(2)}, u32[]{:S(2)}) collective-permute-start(f32[464,128]{1,0:T(8,128)} %get-tuple-element.16), channel_id=1, source_target_pairs={{0,2},{2,0},{4,6},{6,4},{8,10},{10,8},{12,14},{14,12},{16,18},{18,... | collective-permute-start | bytes 712712 | tf_op jit(solution)/shard_map/ppermute | solution.py:575
  7.9 4.4 %copy-start.3 = (f32[9,8,128]{2,1,0:T(8,128)S(1)}, f32[9,8,128]{2,1,0:T(8,128)}, u32[]{:S(2)}) copy-start(f32[9,8,128]{2,1,0:T(8,128)} %get-tuple-element.17.refs_0_) | copy-start | bytes 110596
  8.0 12.0 %all-to-all-start = ((f32[32,8,256]{2,1,0:T(8,128)}), f32[32,8,256]{2,1,0:T(8,128)S(1)}, u32[]{:S(2)}, u32[]{:S(2)}) async-start(f32[32,8,256]{2,1,0:T(8,128)} %get-tuple-element.22), calls=%async_computation | async-start | bytes 524288 | tf_op jit(solution)/shard_map/all_to_all | solution.py:572
  12.3 4.4 %copy-start = (f32[36,1,6,8,128]{4,3,2,1,0:T(8,128)S(1)}, f32[36,1,6,8,128]{4,3,2,1,0:T(8,128)}, u32[]{:S(2)}) copy-start(f32[36,1,6,8,128]{4,3,2,1,0:T(8,128)} %refs_1_.5) | copy-start | bytes 2654212
  12.3 4.4 %copy-start.2 = (s32[8,128]{1,0:T(8,128)S(1)}, s32[8,128]{1,0:T(8,128)}, u32[]{:S(2)}) copy-start(s32[8,128]{1,0:T(8,128)} %get-tuple-element.14.refs_0_) | copy-start | bytes 12292
  12.4 4.3 %collective-permute-start.2 = (f32[11,8,128]{2,1,0:T(8,128)S(1)}, f32[11,8,128]{2,1,0:T(8,128)S(1)}, u32[]{:S(2)}, u32[]{:S(2)}) collective-permute-start(f32[11,8,128]{2,1,0:T(8,128)S(1)} %share.1.refs_4_), channel_id=1, source_target_pairs={{0,1},{1,0},{2,3},{3,2},{4,5},{5,4},{6,7},{7,6},{8,9},{9,8},{10,11... | collective-permute-start | bytes 135176 | tf_op jit(solution)/shard_map/ppermute | solution.py:588
  16.7 3.2 %copy-start.1 = (f32[2,8,256]{2,1,0:T(8,128)S(1)}, f32[2,8,256]{2,1,0:T(8,128)}, u32[]{:S(2)}) copy-start(f32[2,8,256]{2,1,0:T(8,128)} %get-tuple-element.21.refs_6_) | copy-start | bytes 49156

commit v7 on v6

--- a/solution.py
+++ b/solution.py
@@ -61,6 +61,15 @@
 
 def upwind(u, total):
     return 0.5 * jnp.abs(u) * (1.0 - jnp.abs(u / (0.5 * total)))
+
+
+def column(x, at):
+    return x[:, at : at + 1]
+
+
+def spread(z, values, k):
+    at = lax.broadcasted_iota(jnp.int32, (8, 128), 1) + k * 128
+    return jnp.where(at < z.group, values[0], jnp.where(at < 2 * z.group, values[1], values[2]))
 
 
 def wide(x, width):
@@ -221,7 +230,7 @@
 
 
 def interior_kernel(
-    z, order_in, mixing, from_a, from_b, mine, others, partial, ends, aux,
+    z, order_in, mixing, from_a, from_b, mine, others, partial, ends, aux, early,
     order, south, north, coef, order_sem,
 ):
     fetch = pltpu.make_async_copy(order_in, order, order_sem)
@@ -338,6 +347,26 @@
     if species % 4:
         quad(species // 4, species % 4)
 
+    for parity in range(2):
+        values = []
+        for a in range(3):
+            f = 2 * a + parity
+            fx, dp, inverse, new = (aux[f, n] for n in range(4))
+            if parity == 0:
+                u0, p0, p1 = column(fx, 0), column(fx, 0) * (1.0 / 12.0), column(fx, 1) * (1.0 / 12.0)
+                i0, i1 = column(inverse, 0), column(inverse, 1)
+                values.append((u0, column(dp, 0), i0, -p0 * i0, (7.0 * p0 + p1) * i0, -p1 * i1))
+            else:
+                p0 = column(fx, width - 1) * (1.0 / 12.0)
+                i0 = column(inverse, width - 2)
+                values.append((column(dp, width - 1), column(new, width - 1), p0, p0 * i0, i0))
+        for k in range(z.vregs):
+            x = [spread(z, [v[n] for v in values], k) for n in range(len(values[0]))]
+            if parity == 0:
+                x[3] = jnp.where((lane1 & 1) == 1, x[5], x[3])
+            for n in range(5):
+                early[parity, n, :, k * 128 : (k + 1) * 128] = x[n]
+
     lanes = [[jnp.zeros((8, 128), F32) for _ in range(z.vregs)] for _ in range(2)]
     for s in range(species):
         for f in range(6):
@@ -353,7 +382,7 @@
 
 
 def finish_kernel(
-    z, order_in, mixing, from_b, partial, ends, aux, edges, arrived, out,
+    z, order_in, mixing, from_b, partial, ends, aux, early, edges, arrived, out,
     turned, fixed, result, out_sem,
 ):
     place = lax.axis_index("tile")
@@ -373,48 +402,28 @@
     places = order_in[0:1].astype(F32)
     slot = [jnp.sum(jnp.where(lane1[0:1] == f, places, 0.0)).astype(jnp.int32) for f in range(6)]
 
-    def column(x, at):
-        return x[:, at : at + 1]
-
-    def spread(values, k):
-        at = lane1 + k * 128
-        return jnp.where(at < z.group, values[0], jnp.where(at < 2 * z.group, values[1], values[2]))
-
-    last_column = []
+    east_flow = []
     odd_end = (lane1 & 1) == 1
     for parity in range(2):
         end = z.tiles - 1 if parity == 0 else 0
         flux = reverse8(message(holder, end, slice((z.flux // 128) * 128, (z.flux // 128 + 1) * 128)))
-        mul = []
-        for a in range(3):
-            f = 2 * a + parity
-            fx, dp, inverse, new = (aux[f, n] for n in range(4))
-            ghost_dp = column(flux, z.flux % 128 + a)
-            if parity == 0:
-                u0, p1 = column(fx, 0), column(fx, 1) * twelfth
-                p0, b0 = u0 * twelfth, upwind(u0, ghost_dp + column(dp, 0))
-                i0, i1 = column(inverse, 0), column(inverse, 1)
-                mul.append((-p0 * i0, -p1 * i1, (7.0 * p0 + b0 + p1) * i0, -b0 * i0))
-            else:
-                u1 = column(flux, z.flux % 128 + 3 + a)
-                p1, b1 = u1 * twelfth, upwind(u1, column(dp, width - 1) + ghost_dp)
-                p0 = column(fx, width - 1) * twelfth
-                i1 = 1.0 / (column(new, width - 1) - u1)
-                last_column.append(i1)
-                mul.append(
-                    (p0 * column(inverse, width - 2), p1 * i1, (b1 - 7.0 * p1 - p0) * i1, -(7.0 * p1 + b1) * i1, p1 * i1, i1)
-                )
+        ghost_dp = [column(flux, z.flux % 128 + a) for a in range(3)]
+        if parity == 1:
+            east_flow = [column(flux, z.flux % 128 + 3 + a) for a in range(3)]
         for k in range(z.vregs):
             cut = slice(k * 128, (k + 1) * 128)
             g = reverse8(message(half, end, cut))
             own, q = ends[parity, :, cut], edges[parity, :, cut]
-            m = [spread([mul[a][n] for a in range(3)], k) for n in range(len(mul[0]))]
+            m = [early[parity, n, :, cut] for n in range(5)]
+            ghost = spread(z, ghost_dp, k)
             if parity == 0:
-                value = own + jnp.where(odd_end, m[1], m[0]) * g
-                value += jnp.where(odd_end, 0.0, m[2] * roll(g, -1, 1) + m[3] * q)
+                b = upwind(m[0], ghost + m[1]) * m[2]
+                value = own + m[3] * g + jnp.where(odd_end, 0.0, (m[4] + b) * roll(g, -1, 1) - b * q)
             else:
-                value = own * jnp.where(odd_end, m[5], 1.0) + jnp.where(odd_end, m[1], m[0]) * g
-                value += jnp.where(odd_end, m[2] * roll(g, 1, 1) + m[3] * q + m[4] * roll(q, 1, 1), 0.0)
+                u = spread(z, east_flow, k)
+                p, b = u * twelfth, upwind(u, m[0] + ghost)
+                last_cell = own + p * (g + roll(q, 1, 1)) + (b - 7.0 * p - m[2]) * roll(g, 1, 1) - (7.0 * p + b) * q
+                value = jnp.where(odd_end, last_cell / (m[1] - u), own + m[3] * g)
             fixed[parity, :, cut] = value
 
     cuts = [species * n // OUT_CHUNKS for n in range(OUT_CHUNKS + 1)]
@@ -473,8 +482,9 @@
             if parity == 0:
                 return None
             f, source = 2 * a + 1, (a + 2) % 3
-            dp, inverse, v0, v1 = aux[f, 1], aux[f, 2], aux[f, 4], aux[f, 5]
-            inverse = jnp.where(lane == width - 1, last_column[a], inverse)
+            dp, inverse, new, v0, v1 = (aux[f, n] for n in range(1, 6))
+            east = lane == width - 1
+            inverse = jnp.where(east, 1.0 / jnp.where(east, new - east_flow[a], 1.0), inverse)
             ghost_dp = flux[source : source + 1]
             p0, p1, b0 = v0 * twelfth, v1 * twelfth, upwind(v0, ghost_dp + dp)
             zero = jnp.zeros_like(dp)
@@ -588,11 +598,11 @@
         others = lax.ppermute(mine, "spec", [(0, 1), (1, 0)])
     else:
         others = lax.all_gather(mine, "spec", axis=0, tiled=False)
-    partial, ends, aux = pl.pallas_call(
+    partial, ends, aux, early = pl.pallas_call(
         lambda *refs: interior_kernel(z, *refs),
-        out_shape=(f32(*cells), f32(2, 8, z.lanes), f32(6, 6, 8, z.width)),
+        out_shape=(f32(*cells), f32(2, 8, z.lanes), f32(6, 6, 8, z.width), f32(2, 5, 8, z.lanes)),
         in_specs=[vmem] * 6,
-        out_specs=[vmem] * 3,
+        out_specs=[vmem] * 4,
         scratch_shapes=[
             pltpu.SMEM((8, 128), jnp.int32),
             pltpu.VMEM((2 * z.flux, z.width), F32),
@@ -606,7 +616,7 @@
     return pl.pallas_call(
         lambda *refs: finish_kernel(z, *refs),
         out_shape=f32(*mixing.shape),
-        in_specs=[vmem] * 8,
+        in_specs=[vmem] * 9,
         out_specs=hbm,
         scratch_shapes=[
             pltpu.VMEM((z.lanes, z.width), F32),
@@ -616,7 +626,7 @@
         ],
         compiler_params=params,
         name="finish",
-    )(order, mixing, from_b, partial, ends, aux, edges, arrived)
+    )(order, mixing, from_b, partial, ends, aux, early, edges, arrived)
 
 
 def solution(mesh):

time: 21.6 us -> 21.5 us (level)
  transfers between devices with their start and end apart: 4 -> 4, of which waited for: 3 -> 3; matrix products, arithmetic and copies ran while one was open for 0% -> 0% of each run, Pallas kernels for 12% -> 13%
where the time goes in v7:
time: 21.5 us; the launch traced here: 21.2 us
  starting transfers between devices  9.83 us (46%)
  Pallas kernels  6.37 us (30%)
  waiting for transfers between devices  4.94 us (23%)
    ppermute x1, starting transfers between devices, local(): from_b = lax.ppermute(to_b, 'tile', pairs)  5.48 us
    all_to_all x1, starting transfers between devices, local(): lax.all_to_all(messages, ('tile', 'spec'), 0, 0, axis_index_groups=[list(...  2.72 us
    ppermute x1, waiting for transfers between devices, local(): others = lax.ppermute(mine, 'spec', [(0, 1), (1, 0)])  2.68 us
    pallas_call x1, Pallas kernels, local(): pl.pallas_call(lambda *refs: interior_kernel(z, *refs), out_shape=(f32(*c...  2.59 us
    pallas_call x1, Pallas kernels, local(): pl.pallas_call(lambda *refs: pack_kernel(z, *refs), out_shape=packed, in_...  2.46 us
    ppermute x1, waiting for transfers between devices, local(): from_b = lax.ppermute(to_b, 'tile', pairs)  1.65 us
    ppermute x1, starting transfers between devices, local(): others = lax.ppermute(mine, 'spec', [(0, 1), (1, 0)])  1.63 us
    pallas_call x1, Pallas kernels, local(): pl.pallas_call(lambda *refs: finish_kernel(z, *refs), out_shape=f32(*mixi...  1.24 us
  transfers between devices with their start and end apart: 4, of which 3 were waited for; matrix products, arithmetic and copies ran while one was open for 0% of the time, Pallas kernels for 13%

profile of v7, /device:TPU:0, one launch (start us, length us, event | category | flops | bytes accessed | tf_op | source)
XLA Modules:
  0.0 21.2 jit_solution(1447740362922875280)
XLA Ops:
  0.0 2.5 %pack.1 = (f32[464,128]{1,0:T(8,128)}, f32[464,128]{1,0:T(8,128)}, f32[32,8,256]{2,1,0:T(8,128)}, f32[2,8,256]{2,1,0:T(8,128)}, f32[9,8,128]{2,1,0:T(8,128)}, /*index=5*/s32[8,128]{1,0:T(8,128)}) custom-call(s32[6]{0:T(128)} %refs_0_.1, f32[36,1,6,8,128]{4,3,2,1,0:T(8,128)} %refs_1_.5, f32[1,6,8,64]{3,2,1,0:T(8,128)} %refs_2_.1, f32[1,6,8,64]{3,2,1,0:T(8,128)} %refs_3_.1, ...), custom_call_target="tpu_custom_call" | custom-call | tf_op jit(solution)/shard_map/pack/pallas_call | solution.py:567
  2.5 5.5 %collective-permute-start = (f32[464,128]{1,0:T(8,128)}, f32[464,128]{1,0:T(8,128)S(1)}, u32[]{:S(2)}, u32[]{:S(2)}) collective-permute-start(f32[464,128]{1,0:T(8,128)} %get-tuple-element.16), channel_id=1, source_target_pairs={{0,30},{2,4},{4,2},{6,8},{8,6},{10,12},{12,10},{14,16},{16,14},{18... | collective-permute-start | bytes 712712 | tf_op jit(solution)/shard_map/ppermute | solution.py:587
  7.9 0.0 collective-permute-start.1
  7.9 0.0 copy-start.3
  8.0 2.7 %all-to-all-start = ((f32[32,8,256]{2,1,0:T(8,128)}), f32[32,8,256]{2,1,0:T(8,128)S(1)}, u32[]{:S(2)}, u32[]{:S(2)}) async-start(f32[32,8,256]{2,1,0:T(8,128)} %get-tuple-element.24), calls=%async_computation | async-start | bytes 524288 | tf_op jit(solution)/shard_map/all_to_all | solution.py:582
  10.7 1.6 %collective-permute-done.refs_2_.refs_3_ = f32[464,128]{1,0:T(8,128)S(1)} collective-permute-done((f32[464,128]{1,0:T(8,128)}, f32[464,128]{1,0:T(8,128)S(1)}, u32[]{:S(2)}, u32[]{:S(2)}) %collective-permute-start) | collective-permute-done | bytes 237600 | tf_op jit(solution)/shard_map/ppermute | solution.py:587
  12.3 0.0 collective-permute-done.1.refs_1_.refs_2_
  12.3 0.0 copy-done.3
  12.3 0.0 copy-start
  12.3 0.0 copy-start.2
  12.3 0.1 share.1.refs_4_
  12.4 1.6 %collective-permute-start.2 = (f32[11,8,128]{2,1,0:T(8,128)S(1)}, f32[11,8,128]{2,1,0:T(8,128)S(1)}, u32[]{:S(2)}, u32[]{:S(2)}) collective-permute-start(f32[11,8,128]{2,1,0:T(8,128)S(1)} %share.1.refs_4_), channel_id=1, source_target_pairs={{0,1},{1,0},{2,3},{3,2},{4,5},{5,4},{6,7},{7,6},{8,9},{9,8},{10,11... | collective-permute-start | bytes 135176 | tf_op jit(solution)/shard_map/ppermute | solution.py:598
  14.1 2.7 %collective-permute-done.2.refs_5_ = f32[11,8,128]{2,1,0:T(8,128)S(1)} collective-permute-done((f32[11,8,128]{2,1,0:T(8,128)S(1)}, f32[11,8,128]{2,1,0:T(8,128)S(1)}, u32[]{:S(2)}, u32[]{:S(2)}) %collective-permute-start.2) | collective-permute-done | bytes 45088 | tf_op jit(solution)/shard_map/ppermute | solution.py:598
  16.7 0.0 copy-done
  16.7 0.0 copy-done.2
  16.7 0.0 copy-start.1
  16.7 2.6 %interior.1 = (f32[36,6,8,128]{3,2,1,0:T(8,128)S(1)}, f32[2,8,256]{2,1,0:T(8,128)S(1)}, f32[6,6,8,128]{3,2,1,0:T(8,128)S(1)}, f32[2,5,8,256]{3,2,1,0:T(8,128)S(1)}) custom-call(s32[8,128]{1,0:T(8,128)S(1)} %copy-done.2, f32[36,1,6,8,128]{4,3,2,1,0:T(8,128)S(1)} %copy-done, f32[464,128]{1,0:T(8,128)S(1)} %collective-permute-done.1.refs_1_.refs_2_, ...), custom_call_target="tpu_custom_call" | custom-call | tf_op jit(solution)/shard_map/interior/pallas_call | solution.py:601
  19.3 0.6 %all-to-all-done.refs_8_ = f32[32,8,256]{2,1,0:T(8,128)S(1)} async-done(((f32[32,8,256]{2,1,0:T(8,128)}), f32[32,8,256]{2,1,0:T(8,128)S(1)}, u32[]{:S(2)}, u32[]{:S(2)}) %all-to-all-start) | async-done | bytes 262176 | tf_op jit(solution)/shard_map/all_to_all | solution.py:582
  19.9 0.0 copy-done.1
  19.9 1.2 %finish.1 = f32[36,1,6,8,128]{4,3,2,1,0:T(8,128)} custom-call(s32[8,128]{1,0:T(8,128)S(1)} %copy-done.2, f32[36,1,6,8,128]{4,3,2,1,0:T(8,128)S(1)} %copy-done, f32[464,128]{1,0:T(8,128)S(1)} %collective-permute-done.refs_2_.refs_3_, f32[36,6,8,128]{3,2,1,0:T(8,128)S(1)} %get-tuple-element.19.refs_3_, f32[2,8,256]{2,1,0:T(8,128)S(1)} %get-tuple-element.20.refs_4_, ...), custom_call_target="tpu_custom_call" | custom-call | tf_op jit(solution)/shard_map/finish/pallas_call | solution.py:616
Async XLA Ops:
  2.5 9.9 %collective-permute-start = (f32[464,128]{1,0:T(8,128)}, f32[464,128]{1,0:T(8,128)S(1)}, u32[]{:S(2)}, u32[]{:S(2)}) collective-permute-start(f32[464,128]{1,0:T(8,128)} %get-tuple-element.16), channel_id=1, source_target_pairs={{0,30},{2,4},{4,2},{6,8},{8,6},{10,12},{12,10},{14,16},{16,14},{18... | collective-permute-start | bytes 712712 | tf_op jit(solution)/shard_map/ppermute | solution.py:587
  7.9 4.4 %collective-permute-start.1 = (f32[464,128]{1,0:T(8,128)}, f32[464,128]{1,0:T(8,128)S(1)}, u32[]{:S(2)}, u32[]{:S(2)}) collective-permute-start(f32[464,128]{1,0:T(8,128)} %get-tuple-element.17), channel_id=1, source_target_pairs={{0,2},{2,0},{4,6},{6,4},{8,10},{10,8},{12,14},{14,12},{16,18},{18,... | collective-permute-start | bytes 712712 | tf_op jit(solution)/shard_map/ppermute | solution.py:585
  7.9 4.4 %copy-start.3 = (f32[9,8,128]{2,1,0:T(8,128)S(1)}, f32[9,8,128]{2,1,0:T(8,128)}, u32[]{:S(2)}) copy-start(f32[9,8,128]{2,1,0:T(8,128)} %get-tuple-element.18.refs_0_) | copy-start | bytes 110596
  8.0 12.0 %all-to-all-start = ((f32[32,8,256]{2,1,0:T(8,128)}), f32[32,8,256]{2,1,0:T(8,128)S(1)}, u32[]{:S(2)}, u32[]{:S(2)}) async-start(f32[32,8,256]{2,1,0:T(8,128)} %get-tuple-element.24), calls=%async_computation | async-start | bytes 524288 | tf_op jit(solution)/shard_map/all_to_all | solution.py:582
  12.3 4.4 %copy-start = (f32[36,1,6,8,128]{4,3,2,1,0:T(8,128)S(1)}, f32[36,1,6,8,128]{4,3,2,1,0:T(8,128)}, u32[]{:S(2)}) copy-start(f32[36,1,6,8,128]{4,3,2,1,0:T(8,128)} %refs_1_.5) | copy-start | bytes 2654212
  12.3 4.4 %copy-start.2 = (s32[8,128]{1,0:T(8,128)S(1)}, s32[8,128]{1,0:T(8,128)}, u32[]{:S(2)}) copy-start(s32[8,128]{1,0:T(8,128)} %get-tuple-element.15.refs_0_) | copy-start | bytes 12292
  12.4 4.3 %collective-permute-start.2 = (f32[11,8,128]{2,1,0:T(8,128)S(1)}, f32[11,8,128]{2,1,0:T(8,128)S(1)}, u32[]{:S(2)}, u32[]{:S(2)}) collective-permute-start(f32[11,8,128]{2,1,0:T(8,128)S(1)} %share.1.refs_4_), channel_id=1, source_target_pairs={{0,1},{1,0},{2,3},{3,2},{4,5},{5,4},{6,7},{7,6},{8,9},{9,8},{10,11... | collective-permute-start | bytes 135176 | tf_op jit(solution)/shard_map/ppermute | solution.py:598
  16.7 3.2 %copy-start.1 = (f32[2,8,256]{2,1,0:T(8,128)S(1)}, f32[2,8,256]{2,1,0:T(8,128)}, u32[]{:S(2)}) copy-start(f32[2,8,256]{2,1,0:T(8,128)} %get-tuple-element.23.refs_7_) | copy-start | bytes 49156

commit v8 on v7

--- a/solution.py
+++ b/solution.py
@@ -8,10 +8,10 @@
 F32 = jnp.float32
 VMEM_LIMIT = 12 << 20
 CHUNKS = 2
-OUT_CHUNKS = 4
+OUT_CHUNKS = 6
 ORDERS = {(16, 2): (
-    19, 30, 2, 3, 17, 10, 15, 6, 20, 22, 16, 9, 25, 1, 5, 7,
-    12, 31, 28, 0, 14, 27, 21, 8, 11, 26, 18, 13, 4, 29, 24, 23,
+    19, 30, 2, 7, 17, 10, 26, 18, 20, 22, 16, 9, 25, 1, 5, 3,
+    12, 31, 28, 0, 14, 27, 21, 8, 11, 15, 6, 13, 4, 29, 24, 23,
 )}
 
 

time: 21.5 us -> 21.5 us (level)
  no operation moved by 1% of the time
where the time goes in v8:
time: 21.5 us; the launch traced here: 21.2 us
  starting transfers between devices  9.83 us (46%)
  Pallas kernels  6.34 us (29%)
  waiting for transfers between devices  4.94 us (23%)
    ppermute x1, starting transfers between devices, local(): from_b = lax.ppermute(to_b, 'tile', pairs)  5.48 us
    all_to_all x1, starting transfers between devices, local(): lax.all_to_all(messages, ('tile', 'spec'), 0, 0, axis_index_groups=[list(...  2.72 us
    ppermute x1, waiting for transfers between devices, local(): others = lax.ppermute(mine, 'spec', [(0, 1), (1, 0)])  2.65 us
    pallas_call x1, Pallas kernels, local(): pl.pallas_call(lambda *refs: interior_kernel(z, *refs), out_shape=(f32(*c...  2.59 us
    pallas_call x1, Pallas kernels, local(): pl.pallas_call(lambda *refs: pack_kernel(z, *refs), out_shape=packed, in_...  2.45 us
    ppermute x1, waiting for transfers between devices, local(): from_b = lax.ppermute(to_b, 'tile', pairs)  1.65 us
    ppermute x1, starting transfers between devices, local(): others = lax.ppermute(mine, 'spec', [(0, 1), (1, 0)])  1.63 us
    pallas_call x1, Pallas kernels, local(): pl.pallas_call(lambda *refs: finish_kernel(z, *refs), out_shape=f32(*mixi...  1.21 us
  transfers between devices with their start and end apart: 4, of which 3 were waited for; matrix products, arithmetic and copies ran while one was open for 0% of the time, Pallas kernels for 13%

profile of v8, /device:TPU:0, one launch (start us, length us, event | category | flops | bytes accessed | tf_op | source)
XLA Modules:
  0.0 21.2 jit_solution(1338855505047016152)
XLA Ops:
  0.0 2.5 %pack.1 = (f32[464,128]{1,0:T(8,128)}, f32[464,128]{1,0:T(8,128)}, f32[32,8,256]{2,1,0:T(8,128)}, f32[2,8,256]{2,1,0:T(8,128)}, f32[9,8,128]{2,1,0:T(8,128)}, /*index=5*/s32[8,128]{1,0:T(8,128)}) custom-call(s32[6]{0:T(128)} %refs_0_.1, f32[36,1,6,8,128]{4,3,2,1,0:T(8,128)} %refs_1_.5, f32[1,6,8,64]{3,2,1,0:T(8,128)} %refs_2_.1, f32[1,6,8,64]{3,2,1,0:T(8,128)} %refs_3_.1, ...), custom_call_target="tpu_custom_call" | custom-call | tf_op jit(solution)/shard_map/pack/pallas_call | solution.py:567
  2.5 5.5 %collective-permute-start = (f32[464,128]{1,0:T(8,128)}, f32[464,128]{1,0:T(8,128)S(1)}, u32[]{:S(2)}, u32[]{:S(2)}) collective-permute-start(f32[464,128]{1,0:T(8,128)} %get-tuple-element.16), channel_id=1, source_target_pairs={{0,30},{2,4},{4,2},{6,8},{8,6},{10,12},{12,10},{14,16},{16,14},{18... | collective-permute-start | bytes 712712 | tf_op jit(solution)/shard_map/ppermute | solution.py:587
  7.9 0.0 collective-permute-start.1
  7.9 0.0 copy-start.3
  7.9 2.7 %all-to-all-start = ((f32[32,8,256]{2,1,0:T(8,128)}), f32[32,8,256]{2,1,0:T(8,128)S(1)}, u32[]{:S(2)}, u32[]{:S(2)}) async-start(f32[32,8,256]{2,1,0:T(8,128)} %get-tuple-element.24), calls=%async_computation | async-start | bytes 524288 | tf_op jit(solution)/shard_map/all_to_all | solution.py:582
  10.7 1.6 %collective-permute-done.refs_2_.refs_3_ = f32[464,128]{1,0:T(8,128)S(1)} collective-permute-done((f32[464,128]{1,0:T(8,128)}, f32[464,128]{1,0:T(8,128)S(1)}, u32[]{:S(2)}, u32[]{:S(2)}) %collective-permute-start) | collective-permute-done | bytes 237600 | tf_op jit(solution)/shard_map/ppermute | solution.py:587
  12.3 0.0 collective-permute-done.1.refs_1_.refs_2_
  12.3 0.0 copy-done.3
  12.3 0.0 copy-start
  12.3 0.0 copy-start.2
  12.3 0.1 share.1.refs_4_
  12.4 1.6 %collective-permute-start.2 = (f32[11,8,128]{2,1,0:T(8,128)S(1)}, f32[11,8,128]{2,1,0:T(8,128)S(1)}, u32[]{:S(2)}, u32[]{:S(2)}) collective-permute-start(f32[11,8,128]{2,1,0:T(8,128)S(1)} %share.1.refs_4_), channel_id=1, source_target_pairs={{0,1},{1,0},{2,3},{3,2},{4,5},{5,4},{6,7},{7,6},{8,9},{9,8},{10,11... | collective-permute-start | bytes 135176 | tf_op jit(solution)/shard_map/ppermute | solution.py:598
  14.1 2.7 %collective-permute-done.2.refs_5_ = f32[11,8,128]{2,1,0:T(8,128)S(1)} collective-permute-done((f32[11,8,128]{2,1,0:T(8,128)S(1)}, f32[11,8,128]{2,1,0:T(8,128)S(1)}, u32[]{:S(2)}, u32[]{:S(2)}) %collective-permute-start.2) | collective-permute-done | bytes 45088 | tf_op jit(solution)/shard_map/ppermute | solution.py:598
  16.7 0.0 copy-done
  16.7 0.0 copy-done.2
  16.7 0.0 copy-start.1
  16.7 2.6 %interior.1 = (f32[36,6,8,128]{3,2,1,0:T(8,128)S(1)}, f32[2,8,256]{2,1,0:T(8,128)S(1)}, f32[6,6,8,128]{3,2,1,0:T(8,128)S(1)}, f32[2,5,8,256]{3,2,1,0:T(8,128)S(1)}) custom-call(s32[8,128]{1,0:T(8,128)S(1)} %copy-done.2, f32[36,1,6,8,128]{4,3,2,1,0:T(8,128)S(1)} %copy-done, f32[464,128]{1,0:T(8,128)S(1)} %collective-permute-done.1.refs_1_.refs_2_, ...), custom_call_target="tpu_custom_call" | custom-call | tf_op jit(solution)/shard_map/interior/pallas_call | solution.py:601
  19.3 0.6 %all-to-all-done.refs_8_ = f32[32,8,256]{2,1,0:T(8,128)S(1)} async-done(((f32[32,8,256]{2,1,0:T(8,128)}), f32[32,8,256]{2,1,0:T(8,128)S(1)}, u32[]{:S(2)}, u32[]{:S(2)}) %all-to-all-start) | async-done | bytes 262176 | tf_op jit(solution)/shard_map/all_to_all | solution.py:582
  19.9 0.0 copy-done.1
  19.9 1.2 %finish.1 = f32[36,1,6,8,128]{4,3,2,1,0:T(8,128)} custom-call(s32[8,128]{1,0:T(8,128)S(1)} %copy-done.2, f32[36,1,6,8,128]{4,3,2,1,0:T(8,128)S(1)} %copy-done, f32[464,128]{1,0:T(8,128)S(1)} %collective-permute-done.refs_2_.refs_3_, f32[36,6,8,128]{3,2,1,0:T(8,128)S(1)} %get-tuple-element.19.refs_3_, f32[2,8,256]{2,1,0:T(8,128)S(1)} %get-tuple-element.20.refs_4_, ...), custom_call_target="tpu_custom_call" | custom-call | tf_op jit(solution)/shard_map/finish/pallas_call | solution.py:616
Async XLA Ops:
  2.5 9.9 %collective-permute-start = (f32[464,128]{1,0:T(8,128)}, f32[464,128]{1,0:T(8,128)S(1)}, u32[]{:S(2)}, u32[]{:S(2)}) collective-permute-start(f32[464,128]{1,0:T(8,128)} %get-tuple-element.16), channel_id=1, source_target_pairs={{0,30},{2,4},{4,2},{6,8},{8,6},{10,12},{12,10},{14,16},{16,14},{18... | collective-permute-start | bytes 712712 | tf_op jit(solution)/shard_map/ppermute | solution.py:587
  7.9 4.4 %collective-permute-start.1 = (f32[464,128]{1,0:T(8,128)}, f32[464,128]{1,0:T(8,128)S(1)}, u32[]{:S(2)}, u32[]{:S(2)}) collective-permute-start(f32[464,128]{1,0:T(8,128)} %get-tuple-element.17), channel_id=1, source_target_pairs={{0,2},{2,0},{4,6},{6,4},{8,10},{10,8},{12,14},{14,12},{16,18},{18,... | collective-permute-start | bytes 712712 | tf_op jit(solution)/shard_map/ppermute | solution.py:585
  7.9 4.4 %copy-start.3 = (f32[9,8,128]{2,1,0:T(8,128)S(1)}, f32[9,8,128]{2,1,0:T(8,128)}, u32[]{:S(2)}) copy-start(f32[9,8,128]{2,1,0:T(8,128)} %get-tuple-element.18.refs_0_) | copy-start | bytes 110596
  7.9 12.0 %all-to-all-start = ((f32[32,8,256]{2,1,0:T(8,128)}), f32[32,8,256]{2,1,0:T(8,128)S(1)}, u32[]{:S(2)}, u32[]{:S(2)}) async-start(f32[32,8,256]{2,1,0:T(8,128)} %get-tuple-element.24), calls=%async_computation | async-start | bytes 524288 | tf_op jit(solution)/shard_map/all_to_all | solution.py:582
  12.3 4.4 %copy-start = (f32[36,1,6,8,128]{4,3,2,1,0:T(8,128)S(1)}, f32[36,1,6,8,128]{4,3,2,1,0:T(8,128)}, u32[]{:S(2)}) copy-start(f32[36,1,6,8,128]{4,3,2,1,0:T(8,128)} %refs_1_.5) | copy-start | bytes 2654212
  12.3 4.4 %copy-start.2 = (s32[8,128]{1,0:T(8,128)S(1)}, s32[8,128]{1,0:T(8,128)}, u32[]{:S(2)}) copy-start(s32[8,128]{1,0:T(8,128)} %get-tuple-element.15.refs_0_) | copy-start | bytes 12292
  12.4 4.3 %collective-permute-start.2 = (f32[11,8,128]{2,1,0:T(8,128)S(1)}, f32[11,8,128]{2,1,0:T(8,128)S(1)}, u32[]{:S(2)}, u32[]{:S(2)}) collective-permute-start(f32[11,8,128]{2,1,0:T(8,128)S(1)} %share.1.refs_4_), channel_id=1, source_target_pairs={{0,1},{1,0},{2,3},{3,2},{4,5},{5,4},{6,7},{7,6},{8,9},{9,8},{10,11... | collective-permute-start | bytes 135176 | tf_op jit(solution)/shard_map/ppermute | solution.py:598
  16.7 3.2 %copy-start.1 = (f32[2,8,256]{2,1,0:T(8,128)S(1)}, f32[2,8,256]{2,1,0:T(8,128)}, u32[]{:S(2)}) copy-start(f32[2,8,256]{2,1,0:T(8,128)} %get-tuple-element.23.refs_7_) | copy-start | bytes 49156

commit v9 on v8

--- a/solution.py
+++ b/solution.py
@@ -86,7 +86,7 @@
     to_a_out, to_b_out, out_out, edges_out, own_out, order_out,
     to_a, to_b, out, edges, own, order, face_slot, mixing, fluxes, sems, out_sems,
 ):
-    cuts = [z.species * n // CHUNKS for n in range(CHUNKS + 1)]
+    cuts = [0, z.species * 5 // 12, z.species]
     copies = [pltpu.make_async_copy(slot_in, face_slot, sems.at[0])]
     for c, ref in enumerate((dp_in, fx_in, fy_in)):
         copies.append(pltpu.make_async_copy(ref, fluxes.at[c], sems.at[1 + c]))

time: 21.5 us -> 21.4 us (level)
  no operation moved by 1% of the time
where the time goes in v9:
time: 21.4 us; the launch traced here: 21.1 us
  starting transfers between devices  9.83 us (46%)
  Pallas kernels  6.32 us (30%)
  waiting for transfers between devices  4.93 us (23%)
    ppermute x1, starting transfers between devices, local(): from_b = lax.ppermute(to_b, 'tile', pairs)  5.48 us
    all_to_all x1, starting transfers between devices, local(): lax.all_to_all(messages, ('tile', 'spec'), 0, 0, axis_index_groups=[list(...  2.72 us
    ppermute x1, waiting for transfers between devices, local(): others = lax.ppermute(mine, 'spec', [(0, 1), (1, 0)])  2.65 us
    pallas_call x1, Pallas kernels, local(): pl.pallas_call(lambda *refs: interior_kernel(z, *refs), out_shape=(f32(*c...  2.6 us
    pallas_call x1, Pallas kernels, local(): pl.pallas_call(lambda *refs: pack_kernel(z, *refs), out_shape=packed, in_...  2.43 us
    ppermute x1, waiting for transfers between devices, local(): from_b = lax.ppermute(to_b, 'tile', pairs)  1.65 us
    ppermute x1, starting transfers between devices, local(): others = lax.ppermute(mine, 'spec', [(0, 1), (1, 0)])  1.63 us
    pallas_call x1, Pallas kernels, local(): pl.pallas_call(lambda *refs: finish_kernel(z, *refs), out_shape=f32(*mixi...  1.21 us
  transfers between devices with their start and end apart: 4, of which 3 were waited for; matrix products, arithmetic and copies ran while one was open for 0% of the time, Pallas kernels for 13%

profile of v9, /device:TPU:0, one launch (start us, length us, event | category | flops | bytes accessed | tf_op | source)
XLA Modules:
  0.0 21.1 jit_solution(1050199196352888918)
XLA Ops:
  0.0 2.4 %pack.1 = (f32[464,128]{1,0:T(8,128)}, f32[464,128]{1,0:T(8,128)}, f32[32,8,256]{2,1,0:T(8,128)}, f32[2,8,256]{2,1,0:T(8,128)}, f32[9,8,128]{2,1,0:T(8,128)}, /*index=5*/s32[8,128]{1,0:T(8,128)}) custom-call(s32[6]{0:T(128)} %refs_0_.1, f32[36,1,6,8,128]{4,3,2,1,0:T(8,128)} %refs_1_.5, f32[1,6,8,64]{3,2,1,0:T(8,128)} %refs_2_.1, f32[1,6,8,64]{3,2,1,0:T(8,128)} %refs_3_.1, ...), custom_call_target="tpu_custom_call" | custom-call | tf_op jit(solution)/shard_map/pack/pallas_call | solution.py:567
  2.4 5.5 %collective-permute-start = (f32[464,128]{1,0:T(8,128)}, f32[464,128]{1,0:T(8,128)S(1)}, u32[]{:S(2)}, u32[]{:S(2)}) collective-permute-start(f32[464,128]{1,0:T(8,128)} %get-tuple-element.16), channel_id=1, source_target_pairs={{0,30},{2,4},{4,2},{6,8},{8,6},{10,12},{12,10},{14,16},{16,14},{18... | collective-permute-start | bytes 712712 | tf_op jit(solution)/shard_map/ppermute | solution.py:587
  7.9 0.0 collective-permute-start.1
  7.9 0.0 copy-start.3
  7.9 2.7 %all-to-all-start = ((f32[32,8,256]{2,1,0:T(8,128)}), f32[32,8,256]{2,1,0:T(8,128)S(1)}, u32[]{:S(2)}, u32[]{:S(2)}) async-start(f32[32,8,256]{2,1,0:T(8,128)} %get-tuple-element.24), calls=%async_computation | async-start | bytes 524288 | tf_op jit(solution)/shard_map/all_to_all | solution.py:582
  10.7 1.6 %collective-permute-done.refs_2_.refs_3_ = f32[464,128]{1,0:T(8,128)S(1)} collective-permute-done((f32[464,128]{1,0:T(8,128)}, f32[464,128]{1,0:T(8,128)S(1)}, u32[]{:S(2)}, u32[]{:S(2)}) %collective-permute-start) | collective-permute-done | bytes 237600 | tf_op jit(solution)/shard_map/ppermute | solution.py:587
  12.3 0.0 collective-permute-done.1.refs_1_.refs_2_
  12.3 0.0 copy-done.3
  12.3 0.0 copy-start
  12.3 0.0 copy-start.2
  12.3 0.1 share.1.refs_4_
  12.4 1.6 %collective-permute-start.2 = (f32[11,8,128]{2,1,0:T(8,128)S(1)}, f32[11,8,128]{2,1,0:T(8,128)S(1)}, u32[]{:S(2)}, u32[]{:S(2)}) collective-permute-start(f32[11,8,128]{2,1,0:T(8,128)S(1)} %share.1.refs_4_), channel_id=1, source_target_pairs={{0,1},{1,0},{2,3},{3,2},{4,5},{5,4},{6,7},{7,6},{8,9},{9,8},{10,11... | collective-permute-start | bytes 135176 | tf_op jit(solution)/shard_map/ppermute | solution.py:598
  14.0 2.7 %collective-permute-done.2.refs_5_ = f32[11,8,128]{2,1,0:T(8,128)S(1)} collective-permute-done((f32[11,8,128]{2,1,0:T(8,128)S(1)}, f32[11,8,128]{2,1,0:T(8,128)S(1)}, u32[]{:S(2)}, u32[]{:S(2)}) %collective-permute-start.2) | collective-permute-done | bytes 45088 | tf_op jit(solution)/shard_map/ppermute | solution.py:598
  16.7 0.0 copy-done
  16.7 0.0 copy-done.2
  16.7 0.0 copy-start.1
  16.7 2.6 %interior.1 = (f32[36,6,8,128]{3,2,1,0:T(8,128)S(1)}, f32[2,8,256]{2,1,0:T(8,128)S(1)}, f32[6,6,8,128]{3,2,1,0:T(8,128)S(1)}, f32[2,5,8,256]{3,2,1,0:T(8,128)S(1)}) custom-call(s32[8,128]{1,0:T(8,128)S(1)} %copy-done.2, f32[36,1,6,8,128]{4,3,2,1,0:T(8,128)S(1)} %copy-done, f32[464,128]{1,0:T(8,128)S(1)} %collective-permute-done.1.refs_1_.refs_2_, ...), custom_call_target="tpu_custom_call" | custom-call | tf_op jit(solution)/shard_map/interior/pallas_call | solution.py:601
  19.3 0.6 %all-to-all-done.refs_8_ = f32[32,8,256]{2,1,0:T(8,128)S(1)} async-done(((f32[32,8,256]{2,1,0:T(8,128)}), f32[32,8,256]{2,1,0:T(8,128)S(1)}, u32[]{:S(2)}, u32[]{:S(2)}) %all-to-all-start) | async-done | bytes 262176 | tf_op jit(solution)/shard_map/all_to_all | solution.py:582
  19.9 0.0 copy-done.1
  19.9 1.2 %finish.1 = f32[36,1,6,8,128]{4,3,2,1,0:T(8,128)} custom-call(s32[8,128]{1,0:T(8,128)S(1)} %copy-done.2, f32[36,1,6,8,128]{4,3,2,1,0:T(8,128)S(1)} %copy-done, f32[464,128]{1,0:T(8,128)S(1)} %collective-permute-done.refs_2_.refs_3_, f32[36,6,8,128]{3,2,1,0:T(8,128)S(1)} %get-tuple-element.19.refs_3_, f32[2,8,256]{2,1,0:T(8,128)S(1)} %get-tuple-element.20.refs_4_, ...), custom_call_target="tpu_custom_call" | custom-call | tf_op jit(solution)/shard_map/finish/pallas_call | solution.py:616
Async XLA Ops:
  2.4 9.9 %collective-permute-start = (f32[464,128]{1,0:T(8,128)}, f32[464,128]{1,0:T(8,128)S(1)}, u32[]{:S(2)}, u32[]{:S(2)}) collective-permute-start(f32[464,128]{1,0:T(8,128)} %get-tuple-element.16), channel_id=1, source_target_pairs={{0,30},{2,4},{4,2},{6,8},{8,6},{10,12},{12,10},{14,16},{16,14},{18... | collective-permute-start | bytes 712712 | tf_op jit(solution)/shard_map/ppermute | solution.py:587
  7.9 4.4 %collective-permute-start.1 = (f32[464,128]{1,0:T(8,128)}, f32[464,128]{1,0:T(8,128)S(1)}, u32[]{:S(2)}, u32[]{:S(2)}) collective-permute-start(f32[464,128]{1,0:T(8,128)} %get-tuple-element.17), channel_id=1, source_target_pairs={{0,2},{2,0},{4,6},{6,4},{8,10},{10,8},{12,14},{14,12},{16,18},{18,... | collective-permute-start | bytes 712712 | tf_op jit(solution)/shard_map/ppermute | solution.py:585
  7.9 4.4 %copy-start.3 = (f32[9,8,128]{2,1,0:T(8,128)S(1)}, f32[9,8,128]{2,1,0:T(8,128)}, u32[]{:S(2)}) copy-start(f32[9,8,128]{2,1,0:T(8,128)} %get-tuple-element.18.refs_0_) | copy-start | bytes 110596
  7.9 12.0 %all-to-all-start = ((f32[32,8,256]{2,1,0:T(8,128)}), f32[32,8,256]{2,1,0:T(8,128)S(1)}, u32[]{:S(2)}, u32[]{:S(2)}) async-start(f32[32,8,256]{2,1,0:T(8,128)} %get-tuple-element.24), calls=%async_computation | async-start | bytes 524288 | tf_op jit(solution)/shard_map/all_to_all | solution.py:582
  12.3 4.4 %copy-start = (f32[36,1,6,8,128]{4,3,2,1,0:T(8,128)S(1)}, f32[36,1,6,8,128]{4,3,2,1,0:T(8,128)}, u32[]{:S(2)}) copy-start(f32[36,1,6,8,128]{4,3,2,1,0:T(8,128)} %refs_1_.5) | copy-start | bytes 2654212
  12.3 4.4 %copy-start.2 = (s32[8,128]{1,0:T(8,128)S(1)}, s32[8,128]{1,0:T(8,128)}, u32[]{:S(2)}) copy-start(s32[8,128]{1,0:T(8,128)} %get-tuple-element.15.refs_0_) | copy-start | bytes 12292
  12.4 4.3 %collective-permute-start.2 = (f32[11,8,128]{2,1,0:T(8,128)S(1)}, f32[11,8,128]{2,1,0:T(8,128)S(1)}, u32[]{:S(2)}, u32[]{:S(2)}) collective-permute-start(f32[11,8,128]{2,1,0:T(8,128)S(1)} %share.1.refs_4_), channel_id=1, source_target_pairs={{0,1},{1,0},{2,3},{3,2},{4,5},{5,4},{6,7},{7,6},{8,9},{9,8},{10,11... | collective-permute-start | bytes 135176 | tf_op jit(solution)/shard_map/ppermute | solution.py:598
  16.7 3.2 %copy-start.1 = (f32[2,8,256]{2,1,0:T(8,128)S(1)}, f32[2,8,256]{2,1,0:T(8,128)}, u32[]{:S(2)}) copy-start(f32[2,8,256]{2,1,0:T(8,128)} %get-tuple-element.23.refs_7_) | copy-start | bytes 49156
